TPU v7x, 32 devices: a whole 2x2x4 slice. The times are simulated.
32 devices in a mesh: face: 1, tile: 32 (over z, y, x, core).
Axes of the slice: x: 2, y: 2, z: 4, core: 2. Of those that a mesh axis runs over, the one named last changes fastest.
Arguments:
- atmos_state: bfloat16 [32, 12, 256, 256], P(None, 'face', 'tile'), may hold values from -6 to 6
- land_sea: int32 [12, 256, 256], P('face', 'tile'), may hold values 0 or 1
- owners: int32 [3072, 1], P(('face', 'tile')), may hold values from 0 to 31; in each aligned block of 96 rows (0 to 95, 96 to 191, ...) at most 6 rows name the same one
- seam_table: int32 [48, 2], replicated, may hold values from 0 to 47, as said below
- ocean_state: float32 [1, 32, 192, 2, 256], P('face', 'tile'), may hold values from -6 to 6
- conv_input: bfloat16 [3, 64, 96], replicated, may hold values from -0.375 to 0.375
- conv_encode: bfloat16 [3, 64, 192], replicated, may hold values from -0.25 to 0.25
- conv_coarse: bfloat16 [3, 64, 192], replicated, may hold values from -0.25 to 0.25
- conv_decode: bfloat16 [3, 64, 384], replicated, may hold values from -0.1875 to 0.1875
- output_head: bfloat16 [12, 64], replicated, may hold values from -0.75 to 0.75
- ocean_in: float32 [64, 6], replicated, may hold values from -2.5 to 2.5
- ocean_out: float32 [64], replicated, may hold values from -0.75 to 0.75
Outputs:
- atmos_next: bfloat16 [8, 12, 256, 256], P(None, 'face', 'tile')
- ocean_next: float32 [1, 32, 192, 2, 256], P('face', 'tile')
Inputs may be any that keep to these rules, and one draw needn't show every extreme that they name: `owners`: among the 96 tiles of one face group and stripe (an aligned block of rows) no owner appears more than 6 times, and that bound is reached in some block. `seam_table`: row 4 g + s describes side s of face g. Column 0 names the partner side 4 h + u; the pairing is an involution with no fixed points, and paired sides carry the same reversal flag in column 1 (0 or 1).
All inputs are finite; a program needn't handle non-finite values. No bound on the sum of `land_sea` on one device may be relied on, other than what follows from the above.
Results may differ from a plain program's by a relative error of at most 0.0028.
Values may be sent and summed in bfloat16 or wider, within the bound.
No kernel may reach another device: no remote copies, remote signals or barrier semaphores. Data moves between devices by JAX's collectives and lax.ppermute only.
A program may use at most 128 MiB of HBM per device.

v0:
```python
import functools

import jax
import jax.numpy as jnp
import numpy as np
from jax import lax
from jax.experimental import pallas as pl
from jax.experimental.pallas import tpu as pltpu
from jax.sharding import PartitionSpec as P

OUT_VARS = 8
FLUX_CH = 4
OCEAN_CH = 2


def extended(shard, sides, width):
    for axis, dim in sides:
        size, length = (lax.axis_size(axis), shard.shape[dim])
        up = [(i, (i + 1) % size) for i in range(size)]
        down = [(j, i) for i, j in up]
        last = lax.slice_in_dim(shard, length - width, length, axis=dim)
        initial = lax.slice_in_dim(shard, 0, width, axis=dim)
        before = lax.ppermute(last, axis, up)
        after = lax.ppermute(initial, axis, down)
        shard = jnp.concatenate([before, shard, after], axis=dim)
    return shard


def pad_field(values, seam_table):
    channels, faces_dev, stripe_rows, face_side = values.shape
    tile_count = lax.axis_size("tile")
    stripe = lax.axis_index("tile")
    face_group = lax.axis_index("face")
    rimmed = extended(values, (("tile", 2),), 1)
    edge_rows = jnp.stack([values[:, :, 0, :], rimmed[:, :, 0, :]], axis=2)
    edge_pieces = edge_rows.reshape(channels, faces_dev, 2, tile_count, stripe_rows)
    received = lax.all_to_all(edge_pieces, "tile", split_axis=3, concat_axis=3, tiled=True)
    row_part = received[:, :, :, 0, :]
    row_start = stripe * stripe_rows
    col_part = jnp.stack([values[:, :, :, 0], values[:, :, :, face_side - 1]], axis=2)
    seam_piece = jnp.concatenate([row_part, col_part], axis=2)
    seam_piece = jnp.transpose(seam_piece, (1, 2, 0, 3)).reshape(
        1, faces_dev, 4, channels * stripe_rows
    )
    own_sides = lax.dynamic_slice_in_dim(seam_table, face_group * (faces_dev * 4), faces_dev * 4, 0)
    gathered = lax.all_gather(seam_piece, ("face", "tile"), axis=0, tiled=True)
    group_count = gathered.shape[0] // tile_count
    strip_table = gathered.reshape(group_count, tile_count, faces_dev, 4, channels, stripe_rows)
    strip_table = jnp.transpose(strip_table, (0, 2, 3, 4, 1, 5)).reshape(
        group_count * faces_dev * 4, channels, face_side
    )
    strips = jnp.take(strip_table, own_sides[:, 0], axis=0)
    strips = jnp.where(own_sides[:, 1][:, None, None] == 1, strips[:, :, ::-1], strips)
    strips = jnp.transpose(strips.reshape(faces_dev, 4, channels, face_side), (2, 0, 1, 3))
    upper_row = jnp.where(stripe == 0, strips[:, :, 0, :], rimmed[:, :, 0, :])
    bottom = jnp.where(
        stripe == tile_count - 1, strips[:, :, 1, :], rimmed[:, :, stripe_rows + 1, :]
    )
    middle = jnp.concatenate([upper_row[:, :, None, :], values, bottom[:, :, None, :]], axis=2)
    zero_cells = jnp.zeros((channels, faces_dev, 2, 1), values.dtype)
    columns = jnp.concatenate([zero_cells, strips[:, :, 2:, :], zero_cells], axis=3)
    columns = lax.dynamic_slice_in_dim(columns, row_start, stripe_rows + 2, 3)
    return jnp.concatenate([columns[:, :, 0, :, None], middle, columns[:, :, 1, :, None]], axis=3)


def convolve(padded, weight):
    channels, faces_dev, rows_two, side_two = padded.shape
    stripe_rows = rows_two - 2
    face_side = side_two - 2
    planes = []
    for face_index in range(faces_dev):
        summed = jnp.zeros((weight.shape[1], stripe_rows * face_side), jnp.float32)
        for row_shift in range(3):
            tap_rows = jnp.concatenate(
                [
                    padded[
                        :,
                        face_index,
                        row_shift : row_shift + stripe_rows,
                        col_shift : col_shift + face_side,
                    ]
                    for col_shift in range(3)
                ],
                axis=0,
            )
            summed = summed + jnp.dot(
                weight[row_shift],
                tap_rows.reshape(3 * channels, stripe_rows * face_side),
                preferred_element_type=jnp.float32,
            )
        planes.append(jax.nn.gelu(summed).astype(jnp.bfloat16).reshape(-1, stripe_rows, face_side))
    return jnp.stack(planes, axis=1)


def upsample(values):
    return jnp.repeat(jnp.repeat(values, 2, axis=2), 2, axis=3)


def ocean_update(held_state, arrived_flux, ocean_in, ocean_out):
    stacked = jnp.concatenate([held_state, arrived_flux.astype(jnp.float32)], axis=1)
    hidden = jax.nn.gelu(
        jnp.einsum("hc,ncs->nhs", ocean_in, stacked, precision=lax.Precision.HIGHEST)
    )
    sea_now = held_state[:, 0] + jnp.einsum(
        "h,nhs->ns", ocean_out, hidden, precision=lax.Precision.HIGHEST
    )
    return jnp.stack([sea_now, held_state[:, 0]], axis=1)


def ocean_blocks(held_state, arrived_flux, ocean_in, ocean_out, block_count):
    slot_count, state_ch, face_side = held_state.shape
    capacity = slot_count // block_count
    held_split = held_state.reshape(block_count, capacity, state_ch, face_side)
    flux_split = arrived_flux.reshape(block_count, capacity, arrived_flux.shape[1], face_side)
    stepped = lax.map(
        lambda pair: ocean_update(pair[0], pair[1], ocean_in, ocean_out), (held_split, flux_split)
    )
    return stepped.reshape(slot_count, state_ch, face_side)


def on_device(
    atmos_state,
    land_sea,
    owners,
    seam_table,
    ocean_state,
    conv_input,
    conv_encode,
    conv_coarse,
    conv_decode,
    output_head,
    ocean_in,
    ocean_out,
):
    encoded = convolve(pad_field(atmos_state, seam_table), conv_input)
    skip_level = convolve(pad_field(encoded, seam_table), conv_encode)
    channels, faces_dev, stripe_rows, face_side = skip_level.shape
    pooled = (
        skip_level.astype(jnp.float32)
        .reshape(channels, faces_dev, stripe_rows // 2, 2, face_side // 2, 2)
        .mean(axis=(3, 5))
        .astype(jnp.bfloat16)
    )
    coarse_out = convolve(pad_field(pooled, seam_table), conv_coarse)
    coarse_pad = upsample(pad_field(coarse_out, seam_table))[
        :, :, 1 : stripe_rows + 3, 1 : face_side + 3
    ]
    padded = jnp.concatenate([pad_field(skip_level, seam_table), coarse_pad], axis=0)
    decoded = convolve(padded, conv_decode)
    head_out = jnp.dot(
        output_head, decoded.reshape(channels, -1), preferred_element_type=jnp.float32
    )
    head_out = head_out.reshape(-1, faces_dev, stripe_rows, face_side)
    predicted = atmos_state[:OUT_VARS].astype(jnp.float32) + head_out[:OUT_VARS]
    is_ocean = land_sea == 1
    fluxes = jnp.where(is_ocean[None], head_out[OUT_VARS:], 0.0).astype(jnp.bfloat16)
    flux_tiles = jnp.transpose(fluxes, (1, 2, 0, 3)).reshape(
        faces_dev * stripe_rows, FLUX_CH * face_side
    )
    tile_count = lax.axis_size("tile")
    owner_ids = owners[:, 0]
    owner_hits = (owner_ids[:, None] == jnp.arange(tile_count)[None, :]).astype(jnp.int32)
    slot_rank = jnp.sum((jnp.cumsum(owner_hits, axis=0) - 1) * owner_hits, axis=1)
    slot_count = ocean_state.shape[2]
    capacity = slot_count // tile_count
    slot_index = owner_ids * capacity + slot_rank
    selector = (jnp.arange(slot_count)[:, None] == slot_index[None, :]).astype(jnp.bfloat16)
    outgoing = jnp.dot(selector, flux_tiles, preferred_element_type=jnp.float32).astype(
        jnp.bfloat16
    )
    outgoing = outgoing.reshape(tile_count, capacity, FLUX_CH, face_side)
    held_state = ocean_state[0, 0]
    arrived = lax.all_to_all(outgoing, "tile", split_axis=0, concat_axis=0, tiled=True)
    renewed = ocean_blocks(
        held_state, arrived.reshape(slot_count, FLUX_CH, face_side), ocean_in, ocean_out, tile_count
    )
    sea_back = renewed[:, 0].astype(jnp.bfloat16).reshape(tile_count, capacity, face_side)
    sea_slots = lax.all_to_all(sea_back, "tile", split_axis=0, concat_axis=0, tiled=True)
    sea_tiles = jnp.dot(
        selector.T, sea_slots.reshape(slot_count, face_side), preferred_element_type=jnp.float32
    )
    sea_temp = sea_tiles.reshape(faces_dev, stripe_rows, face_side)
    surface = jnp.where(is_ocean, sea_temp, predicted[0])
    atmos_next = jnp.concatenate([surface[None], predicted[1:]], axis=0).astype(jnp.bfloat16)
    return (atmos_next, renewed.reshape(1, 1, slot_count, OCEAN_CH, face_side))


GROUP = 16
LANES = 128
VMEM = pltpu.VMEM
BF = jnp.bfloat16
F32 = jnp.float32
NT = (((1,), (1,)), ((), ()))


def mm(a, b):
    return jnp.dot(a, b, preferred_element_type=F32)


def mm_nt(a, b):
    return lax.dot_general(a, b, NT, preferred_element_type=F32)


def iota(shape, dim):
    return lax.broadcasted_iota(jnp.int32, shape, dim)


def smooth(x):
    inner = x * (0.7978845608028654 + 0.03567740813636141 * (x * x))
    half = 0.5 * x
    return half * jnp.tanh(inner) + half


class Field:
    def __init__(self, faces, rows, chans, side, tiles):
        self.faces, self.rows, self.chans, self.side, self.tiles = faces, rows, chans, side, tiles
        self.per = LANES // chans
        self.groups = faces // self.per
        self.span = rows + 2
        used = self.groups * self.span
        self.chunk = used + (-used) % 16

    def main(self):
        return jax.ShapeDtypeStruct((self.faces, self.rows, self.chans, self.side), BF)

    def outs(self):
        edge = jax.ShapeDtypeStruct((self.faces, self.chans, self.side), BF)
        return [
            edge,
            edge,
            jax.ShapeDtypeStruct((2 * self.faces * 8, self.chans), BF),
            jax.ShapeDtypeStruct((self.tiles, self.chunk, LANES), BF),
        ]

    def send_scratch(self):
        return [
            pltpu.VMEM((2, self.faces, 8, self.chans), F32),
            pltpu.VMEM((self.tiles, self.chunk, LANES), F32),
            pltpu.VMEM((self.side + 8, LANES), F32),
        ]

    def halo_scratch(self):
        return [
            pltpu.VMEM((6, self.faces, GROUP, self.chans), F32),
            pltpu.VMEM((2, GROUP * GROUP, self.chans), F32),
            pltpu.VMEM((self.faces, self.chans, self.side), BF),
            pltpu.VMEM((self.faces, self.chans, self.side), BF),
            pltpu.VMEM((2, self.faces, self.chans, self.side), BF),
            pltpu.VMEM((self.tiles, self.chunk, LANES), F32),
        ]


def flip_matrix(size, flag):
    row, col = iota((size, size), 0), iota((size, size), 1)
    return (row == jnp.where(flag == 1, size - 1 - col, col)).astype(F32).astype(BF)


def edge_columns(fld, face_rows):
    row, col = iota((16, fld.side), 0), iota((16, fld.side), 1)
    total = jnp.zeros((16, fld.chans), F32)
    for r, cells in enumerate(face_rows):
        pick = ((row == r) & (col == 0)) | ((row == 8 + r) & (col == fld.side - 1))
        total = total + mm_nt(pick.astype(F32).astype(BF), cells)
    return total


def pack_sends(fld, stripe, tab, top, bot, ec_out, send_out, cols, stage, strip):
    last = fld.tiles - 1
    ec_out[...] = cols[...].reshape(2 * fld.faces * 8, fld.chans).astype(BF)
    stage[...] = jnp.zeros_like(stage)
    for q in range(2):
        for g in range(fld.faces):
            p = tab[4 * g + q, 0]
            kind, h = p % 4, p // 4
            piece = cols[jnp.maximum(kind - 2, 0), h]
            i, j = g // fld.per, g % fld.per
            stage[
                q * last,
                i * fld.span + 1 : i * fld.span + 1 + fld.rows,
                j * fld.chans : (j + 1) * fld.chans,
            ] = piece[: fld.rows]

    @pl.when((stripe == 0) | (stripe == last))
    def _():
        q = jnp.where(stripe == 0, 0, 1)
        for i in range(fld.groups):
            strip[...] = jnp.zeros_like(strip)
            for j in range(fld.per):
                h = i * fld.per + j
                cells = jnp.where(q == 0, top[h].astype(F32), bot[h].astype(F32)).astype(BF)
                turned = mm_nt(flip_matrix(fld.side, tab[4 * h + q, 1]), cells)
                strip[1 : fld.side + 1, j * fld.chans : (j + 1) * fld.chans] = turned
            for d in range(1, last):
                stage[d, i * fld.span : (i + 1) * fld.span, :] = strip[
                    d * fld.rows : d * fld.rows + fld.span, :
                ]

    send_out[...] = stage[...].astype(BF)


def gather_halos(fld, stripe, tab, x, up, dn, ec, ecm, ecf, ecl, recv, cand, cols, above, below, pair, got):
    faces, rows, chans, side, tiles = fld.faces, fld.rows, fld.chans, fld.side, fld.tiles
    last = tiles - 1
    got[...] = recv[...].astype(F32)
    own = ec[...].astype(F32).reshape(2, faces, 8, chans)
    row, col = iota((faces * 8, faces * 8), 0), iota((faces * 8, faces * 8), 1)
    turn = ((row // 8 == col // 8) & (row % 8 + col % 8 == rows - 1)).astype(F32).astype(BF)
    first = ecf[...].astype(F32).reshape(2, faces, 8, chans)
    final = ecl[...].astype(F32).reshape(2, faces, 8, chans)
    prow, pcol = iota((16, side), 0), iota((16, side), 1)
    ends = ((prow == 0) & (pcol == 0)) | ((prow == 1) & (pcol == side - 1))
    ends = ends.astype(F32).astype(BF)
    for h in range(faces):
        over, under = mm_nt(ends, up[h]), mm_nt(ends, dn[h])
        for s in range(2):
            cand[2 + s, h, 0:1] = over[s : s + 1]
            cand[2 + s, h, rows + 1 : rows + 2] = under[s : s + 1]
            cand[2 + s, h, 1 : rows + 1] = own[s, h, :rows]
    for s in range(2):
        turned = mm(turn, ecm[s * faces * 8 : (s + 1) * faces * 8, :]).reshape(faces, 8, chans)
        for h in range(faces):
            cand[4 + s, h, 0:1] = first[s, h, 0:1]
            cand[4 + s, h, rows + 1 : rows + 2] = final[s, h, rows - 1 : rows]
            cand[4 + s, h, 1 : rows + 1] = turned[h, :rows]
    above[...] = up[...]
    below[...] = dn[...]
    at_edge = (stripe == 0) | (stripe == last)

    @pl.when(jnp.logical_not(at_edge))
    def _():
        for q in range(2):
            for h in range(faces):
                i, j = h // fld.per, h % fld.per
                cand[q, h, 0 : fld.span] = got[
                    q * last,
                    i * fld.span : (i + 1) * fld.span,
                    j * chans : (j + 1) * chans,
                ]

    @pl.when(at_edge)
    def _():
        q = jnp.where(stripe == 0, 0, 1)
        for h in range(faces):
            pair[0, h] = jnp.where(q == 0, x[h, 0].astype(F32), dn[h].astype(F32)).astype(BF)
            pair[1, h] = jnp.where(q == 0, up[h].astype(F32), x[h, rows - 1].astype(F32)).astype(BF)
        place = stripe * rows - 1 + prow
        inside = (place >= 0) & (place < side)
        for s in range(2):
            for h in range(faces):
                want = jnp.where(tab[4 * h + s, 1] == 1, side - 1 - place, place)
                window = ((pcol == want) & inside).astype(F32).astype(BF)
                cand[s, h] = mm_nt(window, pair[s, h])
        for i in range(fld.groups):
            lined = jnp.concatenate(
                [got[d, i * fld.span + 1 : i * fld.span + 1 + rows, :] for d in range(tiles)], axis=0
            )
            lined = jnp.transpose(lined)
            for j in range(fld.per):
                g = i * fld.per + j
                p = tab[4 * g + q, 0]
                kind, h = p % 4, p // 4
                near = pair[jnp.minimum(kind, 1), h].astype(F32)
                far = lined[j * chans : (j + 1) * chans]
                cells = jnp.where(kind < 2, near, far).astype(BF)
                placed = mm(cells, flip_matrix(side, tab[4 * g + q, 1])).astype(BF)

                @pl.when(q == 0)
                def _():
                    above[g] = placed

                @pl.when(q == 1)
                def _():
                    below[g] = placed

    cols[...] = jnp.zeros_like(cols)
    slot = iota((GROUP, chans), 0)
    live = (slot < fld.span) & jnp.logical_not(
        ((slot == 0) & (stripe == 0)) | ((slot == rows + 1) & (stripe == last))
    )
    for s in range(2):
        for g in range(faces):
            p = tab[4 * g + 2 + s, 0]
            kind, h = p % 4, p // 4
            which = jnp.where((kind >= 2) & (tab[4 * g + 2 + s, 1] == 1), kind + 2, kind)
            cols[s, g * GROUP : (g + 1) * GROUP] = jnp.where(live, cand[which, h], 0.0)


def column_terms(side_weight, cols, out_ch):
    terms = []
    for s in range(2):
        part = mm_nt(side_weight[s], cols[s])
        size = part.shape[1]
        terms.append(
            part[out_ch : 2 * out_ch]
            + pltpu.roll(part[:out_ch], 1, 1)
            + pltpu.roll(part[2 * out_ch :], size - 1, 1)
        )
    return terms


def face_terms(terms, face_index):
    size = terms[0].shape[1]
    shift = lax.rem(2 * size - GROUP * face_index - 1, size)
    return [pltpu.roll(term, shift, 1)[:, :LANES] for term in terms]


def conv_row(weight, stacked, terms, r, out_ch):
    z = mm(weight, stacked)
    side = z.shape[1]
    left, right = pltpu.roll(z[:out_ch], 1, 1), pltpu.roll(z[2 * out_ch :], side - 1, 1)
    lane = iota((out_ch, LANES), 1)
    first = terms[0] if r == 0 else pltpu.roll(terms[0], LANES - r, 1)
    final = pltpu.roll(terms[1], LANES - 1 - r, 1)
    head = jnp.where(lane == 0, first, left[:, :LANES])
    tail = jnp.where(lane == LANES - 1, final, right[:, side - LANES :])
    if side > LANES:
        left = jnp.concatenate([head, left[:, LANES:]], axis=1)
        right = jnp.concatenate([right[:, : side - LANES], tail], axis=1)
    else:
        left, right = head, tail
    return smooth(z[out_ch : 2 * out_ch] + left + right).astype(BF)


def row_stack(x, above, below, f, rows):
    lines = [above[f]] + [x[f, r] for r in range(rows)] + [below[f]]
    return lambda r: lines[r : r + 3]


def prep_kernel(fld, stripe_ref, tab, atmos, perm, x_out, top, bot, ec_out, send_out, cols, stage, strip):
    stripe = stripe_ref[0]

    def one_face(f, carry):
        block = atmos[:, f].astype(F32).reshape(fld.chans * fld.rows, fld.side).astype(BF)
        moved = mm(perm[...], block).astype(BF)
        lines = [moved[r * fld.chans : (r + 1) * fld.chans] for r in range(fld.rows)]
        for r in range(fld.rows):
            x_out[f, r] = lines[r]
        top[f] = lines[0]
        bot[f] = lines[-1]
        edges = edge_columns(fld, lines)
        cols[0, f] = edges[:8]
        cols[1, f] = edges[8:]
        return carry

    lax.fori_loop(0, fld.faces, one_face, 0)
    pack_sends(fld, stripe, tab, top, bot, ec_out, send_out, cols, stage, strip)


def level_kernel(fld, out_fld, stripe_ref, tab, x, up, dn, ec, ecm, ecf, ecl, recv, weight, side_weight, *refs):
    outs, sends, halos = refs[:5], refs[5:8], refs[8:]
    x_out, top, bot, ec_out, send_out = outs
    stripe = stripe_ref[0]
    gather_halos(fld, stripe, tab, x, up, dn, ec, ecm, ecf, ecl, recv, *halos)
    _, cols, above, below = halos[:4]
    terms = column_terms(side_weight, [cols[0].astype(BF), cols[1].astype(BF)], out_fld.chans)

    def one_face(f, carry):
        lines = row_stack(x, above, below, f, fld.rows)
        ends = face_terms(terms, f)
        made = []
        for r in range(fld.rows):
            cells = conv_row(
                weight[...], jnp.concatenate(lines(r), axis=0), ends, r, out_fld.chans
            )
            x_out[f, r] = cells
            made.append(cells)
        top[f] = made[0]
        bot[f] = made[-1]
        edges = edge_columns(out_fld, made)
        sends[0][0, f] = edges[:8]
        sends[0][1, f] = edges[8:]
        return carry

    lax.fori_loop(0, fld.faces, one_face, 0)
    pack_sends(out_fld, stripe, tab, top, bot, ec_out, send_out, *sends)


def encode_kernel(fld, out_fld, low, stripe_ref, tab, x, up, dn, ec, ecm, ecf, ecl, recv, weight, side_weight, pool, *refs):
    outs, low_outs, sends, low_sends, halos = refs[:5], refs[5:10], refs[10:13], refs[13:16], refs[16:]
    x_out, top, bot, ec_out, send_out = outs
    y_out, low_top, low_bot, low_ec, low_send = low_outs
    stripe = stripe_ref[0]
    gather_halos(fld, stripe, tab, x, up, dn, ec, ecm, ecf, ecl, recv, *halos)
    _, cols, above, below = halos[:4]
    terms = column_terms(side_weight, [cols[0].astype(BF), cols[1].astype(BF)], out_fld.chans)

    def one_face(f, carry):
        lines = row_stack(x, above, below, f, fld.rows)
        ends = face_terms(terms, f)
        made, pooled = [], []
        for r in range(fld.rows):
            cells = conv_row(
                weight[...], jnp.concatenate(lines(r), axis=0), ends, r, out_fld.chans
            )
            x_out[f, r] = cells
            made.append(cells)
            if r % 2 == 1:
                mean = (mm(made[r - 1], pool[...]) + mm(cells, pool[...])).astype(BF)
                y_out[f, r // 2] = mean
                pooled.append(mean)
        top[f] = made[0]
        bot[f] = made[-1]
        edges = edge_columns(out_fld, made)
        sends[0][0, f] = edges[:8]
        sends[0][1, f] = edges[8:]
        low_top[f] = pooled[0]
        low_bot[f] = pooled[-1]
        edges = edge_columns(low, pooled)
        low_sends[0][0, f] = edges[:8]
        low_sends[0][1, f] = edges[8:]
        return carry

    lax.fori_loop(0, fld.faces, one_face, 0)
    pack_sends(low, stripe, tab, low_top, low_bot, low_ec, low_send, *low_sends)
    pack_sends(out_fld, stripe, tab, top, bot, ec_out, send_out, *sends)


def decode_kernel(fld, low, out_ch, vars_out, stripe_ref, tab, x, up, dn, ec, ecm, ecf, ecl, recv, y, yup, ydn, yec, yecm, yecf, yecl, yrecv, weight, side_weight, spread, head, atmos, land, row_key, col_key, pred_out, flux_out, *refs):
    halos, low_halos, flux = refs[:6], refs[6:12], refs[12]
    stripe = stripe_ref[0]
    gather_halos(low, stripe, tab, y, yup, ydn, yec, yecm, yecf, yecl, yrecv, *low_halos)
    gather_halos(fld, stripe, tab, x, up, dn, ec, ecm, ecf, ecl, recv, *halos)
    _, cols, above, below = halos[:4]
    _, low_cols, low_above, low_below = low_halos[:4]
    size = GROUP * GROUP
    row, col = iota((size, size), 0), iota((size, size), 1)
    widen = (col == (row // GROUP) * GROUP + (row % GROUP + 1) // 2).astype(F32).astype(BF)
    joined = []
    for s in range(2):
        wide = mm(widen, low_cols[s].astype(BF))
        joined.append(jnp.concatenate([cols[s], wide], axis=1).astype(BF))
    terms = column_terms(side_weight, joined, out_ch)

    def one_face(f, carry):
        lines = row_stack(x, above, below, f, fld.rows)
        ends = face_terms(terms, f)
        low_lines = [low_above[f]] + [y[f, r] for r in range(low.rows)] + [low_below[f]]
        wide = [mm(cells, spread[...]).astype(BF) for cells in low_lines]
        made = []
        for r in range(fld.rows):
            picked = [wide[(r + a + 1) // 2] for a in range(3)]
            made.append(
                conv_row(weight[...], jnp.concatenate(lines(r) + picked, axis=0), ends, r, out_ch)
            )
        result = mm(head[...], jnp.concatenate(made, axis=0)).reshape(-1, fld.rows, fld.side)
        pred_out[:, f] = (atmos[:, f].astype(F32) + result[:vars_out]).astype(BF)
        sea = land[f] == 1
        flux[:, f] = jnp.where(sea[None], result[vars_out:], 0.0)
        return carry

    lax.fori_loop(0, fld.faces, one_face, 0)
    chosen = (row_key[...] == col_key[...]).astype(F32).astype(BF)
    tiles = flux[...].reshape(-1, fld.side).astype(BF)
    flux_out[...] = mm(chosen, tiles).astype(BF).reshape(flux_out.shape)


def ocean_kernel(cap, recv, state, into, out_weight, sea_out, back_out):
    tiles, _, side = recv.shape

    def one_source(t, carry):
        flux = recv[t].astype(F32)
        pad = (-flux.shape[0]) % 16
        flux = jnp.concatenate([flux, jnp.zeros((pad, side), F32)], axis=0).astype(BF)
        held = state[t]
        high = held.astype(BF)
        low = (held - high.astype(F32)).astype(BF)
        hidden = smooth(mm(into[...], jnp.concatenate([flux, flux, high, high, low], axis=0)))
        width = out_weight[...]
        wide = jnp.concatenate([width] * (side // LANES), axis=1)
        drift = (hidden * wide).reshape(cap, -1, side).sum(axis=1)
        drift = jnp.concatenate([drift, jnp.zeros((8 - cap, side), F32)], axis=0)
        sea = held[:8] + drift
        sea_out[t] = sea
        back_out[t] = sea.astype(BF)
        return carry

    lax.fori_loop(0, tiles, one_source, 0)


def surface_kernel(back, key, land, pred, out):
    faces, rows, side = land.shape
    slots = back[...].astype(F32).reshape(-1, side).astype(BF)
    chosen = (key[...] == iota((faces * rows, slots.shape[0]), 1)).astype(F32).astype(BF)
    sea = mm(chosen, slots).reshape(faces, rows, side)
    out[0] = jnp.where(land[...] == 1, sea, pred[0].astype(F32)).astype(BF)


def call(kernel, outs, ins, scratch, flops, smem=0, specs=None, aliases=None, out_specs=None, name=None):
    whole = pl.BlockSpec(memory_space=pltpu.VMEM)
    in_specs = [pl.BlockSpec(memory_space=pltpu.SMEM)] * smem + [whole] * (len(ins) - smem)
    for position, spec in (specs or {}).items():
        in_specs[position] = spec
    grid = {"grid": (1,)} if specs else {}
    moved = sum(int(np.prod(a.shape)) * a.dtype.itemsize for a in list(ins) + list(outs))
    return pl.pallas_call(
        kernel,
        out_shape=outs,
        **grid,
        in_specs=in_specs,
        out_specs=out_specs or [whole] * len(outs),
        scratch_shapes=scratch,
        input_output_aliases=aliases or {},
        compiler_params=pltpu.CompilerParams(vmem_limit_bytes=56 * 1024 * 1024),
        cost_estimate=pl.CostEstimate(flops=int(flops), bytes_accessed=int(moved), transcendentals=0),
        name=name,
    )(*ins)


def exchange(fld, top, bot, ec, send):
    tiles = fld.tiles

    def move(values, to):
        return lax.ppermute(values, "tile", [(i, to(i) % tiles) for i in range(tiles)])

    return (
        move(bot, lambda i: i + 1),
        move(top, lambda i: i - 1),
        ec,
        move(ec, lambda i: tiles - 1 - i),
        move(ec, lambda i: tiles - i),
        move(ec, lambda i: tiles - 2 - i),
        lax.all_to_all(send, "tile", split_axis=0, concat_axis=0, tiled=True),
    )


def packed_weight(weight, chans):
    taps, out_ch, _ = weight.shape
    split = weight.reshape(taps, out_ch, taps, chans)
    body = jnp.transpose(split, (2, 1, 0, 3)).reshape(taps * out_ch, taps * chans)
    sides = jnp.stack([split[:, :, 0], split[:, :, 2]]).reshape(2, taps * out_ch, chans)
    return body, sides


def on_one_group(
    atmos_state,
    land_sea,
    owners,
    seam_table,
    ocean_state,
    conv_input,
    conv_encode,
    conv_coarse,
    conv_decode,
    output_head,
    ocean_in,
    ocean_out,
):
    in_ch, faces, rows, side = atmos_state.shape
    tiles = lax.axis_size("tile")
    width = conv_input.shape[1]
    stripe = lax.axis_index("tile").astype(jnp.int32).reshape(1)
    entry = Field(faces, rows, in_ch, side, tiles)
    full = Field(faces, rows, width, side, tiles)
    low = Field(faces, rows // 2, width, side // 2, tiles)
    cells = faces * rows * side

    order = np.arange(in_ch * rows)
    perm = np.zeros((in_ch * rows, in_ch * rows), np.float32)
    perm[order, (order % in_ch) * rows + order // in_ch] = 1.0
    spread = np.zeros((side // 2, side), np.float32)
    spread[np.arange(side) // 2, np.arange(side)] = 1.0
    perm, pool = jnp.asarray(perm, BF), jnp.asarray(0.25 * spread.T, BF)
    spread = jnp.asarray(spread, BF)

    x0, *edges = call(
        functools.partial(prep_kernel, entry),
        [entry.main()] + entry.outs(),
        (stripe, seam_table, atmos_state, perm),
        entry.send_scratch(),
        2 * cells * in_ch * in_ch * rows,
        smem=2,
        name="prep",
    )
    moved = exchange(entry, *edges)
    body, sides = packed_weight(conv_input, in_ch)
    x1, *edges = call(
        functools.partial(level_kernel, entry, full),
        [full.main()] + full.outs(),
        (stripe, seam_table, x0) + moved + (body, sides),
        full.send_scratch() + entry.halo_scratch(),
        2 * cells * 9 * in_ch * width,
        smem=2,
        name="conv_in",
    )
    moved = exchange(full, *edges)
    body, sides = packed_weight(conv_encode, width)
    made = call(
        functools.partial(encode_kernel, full, full, low),
        [full.main()] + full.outs() + [low.main()] + low.outs(),
        (stripe, seam_table, x1) + moved + (body, sides, pool),
        full.send_scratch() + low.send_scratch() + full.halo_scratch(),
        2 * cells * 9 * width * width,
        smem=2,
        name="encode",
    )
    x2, *edges = made[:5]
    y0, *low_edges = made[5:]
    low_moved = exchange(low, *low_edges)
    moved = exchange(full, *edges)
    body, sides = packed_weight(conv_coarse, width)
    y1, *low_edges = call(
        functools.partial(level_kernel, low, low),
        [low.main()] + low.outs(),
        (stripe, seam_table, y0) + low_moved + (body, sides),
        low.send_scratch() + low.halo_scratch(),
        2 * cells * 9 * width * width // 4,
        smem=2,
        name="coarse",
    )
    low_moved = exchange(low, *low_edges)

    taps = conv_decode.shape[0]
    split = conv_decode.reshape(taps, width, taps, 2, width)
    body = jnp.transpose(split, (2, 1, 3, 0, 4)).reshape(taps * width, 2 * taps * width)
    sides = jnp.stack([split[:, :, 0], split[:, :, 2]]).reshape(2, taps * width, 2 * width)
    heads = output_head.shape[0]
    flux_ch = heads - OUT_VARS
    eye = jnp.eye(rows, dtype=output_head.dtype)
    head = (output_head[:, None, None, :] * eye[None, :, :, None]).reshape(heads * rows, rows * width)

    slot_count = ocean_state.shape[2]
    cap = slot_count // tiles
    owner_ids = owners[:, 0]
    count = owner_ids.shape[0]
    earlier = np.tril(np.ones((count, count), bool), -1)
    rank = jnp.sum((owner_ids[:, None] == owner_ids[None, :]) & earlier, axis=1).astype(jnp.int32)
    slot_index = owner_ids * cap + rank
    col_key = (np.arange(flux_ch, dtype=np.int32)[:, None] * slot_count + slot_index[None, :]).reshape(1, -1)
    row_key = (
        np.arange(flux_ch, dtype=np.int32)[None, :, None] * slot_count
        + np.arange(slot_count, dtype=np.int32).reshape(tiles, 1, cap)
    ).reshape(-1, 1)
    row_key = jnp.asarray(row_key)
    pred, outgoing = call(
        functools.partial(decode_kernel, full, low, width, OUT_VARS),
        [
            jax.ShapeDtypeStruct((OUT_VARS, faces, rows, side), BF),
            jax.ShapeDtypeStruct((tiles, flux_ch * cap, side), BF),
        ],
        (stripe, seam_table, x2)
        + moved
        + (y1,)
        + low_moved
        + (body, sides, spread, head, atmos_state, land_sea, row_key, col_key),
        full.halo_scratch() + low.halo_scratch() + [pltpu.VMEM((flux_ch, faces, rows, side), F32)],
        2 * cells * 18 * width * width,
        smem=2,
        specs={22: pl.BlockSpec((OUT_VARS, faces, rows, side), lambda i: (0, 0, 0, 0))},
        name="decode",
    )
    arrived = lax.all_to_all(outgoing, "tile", split_axis=0, concat_axis=0, tiled=True)

    held = jnp.transpose(ocean_state[0, 0].reshape(tiles, cap, OCEAN_CH, side), (0, 2, 1, 3))
    state = jnp.pad(held, ((0, 0), (0, 0), (0, 8 - cap), (0, 0))).reshape(tiles, OCEAN_CH * 8, side)
    hidden = ocean_in.shape[0]
    high = ocean_in.astype(BF)
    rest = (ocean_in - high.astype(F32)).astype(BF)
    flux_pad = (-flux_ch * cap) % 16
    each = jnp.eye(cap, dtype=BF)
    slot8 = jnp.eye(cap, 8, dtype=BF)

    def flux_part(weights):
        part = each[:, None, None, :] * weights[None, :, OCEAN_CH:, None]
        return jnp.pad(part.reshape(cap * hidden, flux_ch * cap), ((0, 0), (0, flux_pad)))

    def state_part(weights):
        part = slot8[:, None, None, :] * weights[None, :, :OCEAN_CH, None]
        return part.reshape(cap * hidden, OCEAN_CH * 8)

    into = jnp.concatenate(
        [flux_part(high), flux_part(rest), state_part(high), state_part(rest), state_part(high)], axis=1
    )
    out_weight = jnp.broadcast_to(ocean_out[None, :, None], (cap, hidden, LANES)).reshape(-1, LANES)
    sea, back = call(
        functools.partial(ocean_kernel, cap),
        [jax.ShapeDtypeStruct((tiles, 8, side), F32), jax.ShapeDtypeStruct((tiles, 8, side), BF)],
        (arrived, state, into, out_weight),
        [],
        2 * slot_count * side * hidden * 8,
        name="ocean",
    )
    returned = lax.all_to_all(back, "tile", split_axis=0, concat_axis=0, tiled=True)
    key = (owner_ids * 8 + rank)[:, None]
    first = pl.BlockSpec((1, faces, rows, side), lambda i: (0, 0, 0, 0))
    (atmos_next,) = call(
        surface_kernel,
        [jax.ShapeDtypeStruct(pred.shape, BF)],
        (returned, key, land_sea, pred),
        [],
        2 * count * tiles * 8 * side,
        specs={3: first},
        out_specs=[first],
        aliases={3: 0},
        name="surface",
    )
    renewed = jnp.stack([sea[:, :cap], held[:, 0]], axis=2)
    return atmos_next, renewed.reshape(1, 1, slot_count, OCEAN_CH, side)


def fits(mesh):
    return mesh.shape["face"] == 1


def solution(mesh):
    in_specs = (
        P(None, "face", "tile", None),
        P("face", "tile", None),
        P(("face", "tile"), None),
        P(),
        P("face", "tile", None, None, None),
        P(),
        P(),
        P(),
        P(),
        P(),
        P(),
        P(),
    )
    out_specs = (P(None, "face", "tile", None), P("face", "tile", None, None, None))
    return jax.shard_map(
        on_one_group if fits(mesh) else on_device,
        mesh=mesh,
        in_specs=in_specs,
        out_specs=out_specs,
        check_vma=False,
    )
```

profile of v0, /device:TPU:0, one launch (start us, length us, event | category | flops | bytes accessed | tf_op | source)
XLA Modules:
  0.0 268.9 jit_solution(18378376703236078124)
XLA Ops:
  0.6 1.4 copy.197.tab
  2.0 7.9 %prep.1 = (bf16[12,8,32,256]{3,2,1,0:T(8,128)(2,1)}, bf16[12,32,256]{2,1,0:T(8,128)(2,1)}, bf16[12,32,256]{2,1,0:T(8,128)(2,1)}, bf16[192,32]{1,0:T(8,128)(2,1)}, bf16[32,32,128]{2,1,0:T(8,128)(2,1)}) custom-call(s32[1]{0:T(128)} %bitcast.stripe_ref, s32[48,2]{1,0:T(8,128)} %copy.197.tab, bf16[32,12,8,256]{3,2,1,0:T(8,128)(2,1)} %atmos.3, ...), custom_call_target="tpu_custom_call" | custom-call | flops 402653184 | bytes 3944836 | tf_op jit(solution)/shard_map/prep/pallas_call | solution.py:595
  9.9 6.7 %all-to-all-start = ((bf16[32,32,128]{2,1,0:T(8,128)(2,1)}), bf16[32,32,128]{2,1,0:T(8,128)(2,1)S(1)}, u32[]{:S(2)}, u32[]{:S(2)}) async-start(bf16[32,32,128]{2,1,0:T(8,128)(2,1)} %get-tuple-element.35), calls=%async_computation | async-start | bytes 524288 | tf_op jit(solution)/shard_map/all_to_all | solution.py:622
  16.6 5.3 %collective-permute-start.2 = (bf16[192,32]{1,0:T(8,128)(2,1)}, bf16[192,32]{1,0:T(8,128)(2,1)S(1)}, u32[]{:S(2)}, u32[]{:S(2)}) collective-permute-start(bf16[192,32]{1,0:T(8,128)(2,1)} %get-tuple-element.34.ec), channel_id=1, source_target_pairs={{0,31},{1,30},{2,29},{3,28},{4,27},{5,26},{6,25},{7,24},{8,23},{9,... | collective-permute-start | bytes 36872 | tf_op jit(solution)/shard_map/ppermute | solution.py:613
  21.9 1.4 collective-permute-start.3
  23.3 7.1 %collective-permute-start.4 = (bf16[192,32]{1,0:T(8,128)(2,1)}, bf16[192,32]{1,0:T(8,128)(2,1)S(1)}, u32[]{:S(2)}, u32[]{:S(2)}) collective-permute-start(bf16[192,32]{1,0:T(8,128)(2,1)} %get-tuple-element.34.ec), channel_id=1, source_target_pairs={{0,30},{1,29},{2,28},{3,27},{4,26},{5,25},{6,24},{7,23},{8,22},{9,... | collective-permute-start | bytes 36872 | tf_op jit(solution)/shard_map/ppermute | solution.py:613
  30.5 5.3 %collective-permute-start.1 = (bf16[12,32,256]{2,1,0:T(8,128)(2,1)}, bf16[12,32,256]{2,1,0:T(8,128)(2,1)S(1)}, u32[]{:S(2)}, u32[]{:S(2)}) collective-permute-start(bf16[12,32,256]{2,1,0:T(8,128)(2,1)} %get-tuple-element.33), channel_id=1, source_target_pairs={{0,31},{1,0},{2,1},{3,2},{4,3},{5,4},{6,5},{7,6},{8,7},{9,8},{10,9... | collective-permute-start | bytes 589832 | tf_op jit(solution)/shard_map/ppermute | solution.py:613
  35.8 0.9 copy.177
  37.0 0.7 copy.183.side_weight
  37.9 0.7 copy.182.weight
  38.7 0.7 collective-permute-done.up
  39.4 0.6 copy-done.28
  40.2 16.4 %conv_in.1 = (bf16[12,8,64,256]{3,2,1,0:T(8,128)(2,1)}, bf16[12,64,256]{2,1,0:T(8,128)(2,1)}, bf16[12,64,256]{2,1,0:T(8,128)(2,1)}, bf16[192,64]{1,0:T(8,128)(2,1)}, bf16[32,64,128]{2,1,0:T(8,128)(2,1)}) custom-call(s32[1]{0:T(128)} %bitcast.stripe_ref, s32[48,2]{1,0:T(8,128)} %copy.197.tab, bf16[12,8,32,256]{3,2,1,0:T(8,128)(2,1)} %get-tuple-element.31.x, ...), custom_call_target="tpu_custom_call" | custom-call | flops 905969664 | bytes 6820228 | tf_op jit(solution)/shard_map/conv_in/pallas_call | solution.py:595
  56.6 5.6 %all-to-all-start.1 = ((bf16[32,64,128]{2,1,0:T(8,128)(2,1)}), bf16[32,64,128]{2,1,0:T(8,128)(2,1)S(1)}, u32[]{:S(2)}, u32[]{:S(2)}) async-start(bf16[32,64,128]{2,1,0:T(8,128)(2,1)} %get-tuple-element.40), calls=%async_computation.1 | async-start | bytes 1048576 | tf_op jit(solution)/shard_map/all_to_all | solution.py:622
  62.6 5.1 %collective-permute-start.6 = (bf16[12,64,256]{2,1,0:T(8,128)(2,1)}, bf16[12,64,256]{2,1,0:T(8,128)(2,1)S(1)}, u32[]{:S(2)}, u32[]{:S(2)}) collective-permute-start(bf16[12,64,256]{2,1,0:T(8,128)(2,1)} %get-tuple-element.38), channel_id=1, source_target_pairs={{0,31},{1,0},{2,1},{3,2},{4,3},{5,4},{6,5},{7,6},{8,7},{9,8},{10,9... | collective-permute-start | bytes 1179656 | tf_op jit(solution)/shard_map/ppermute | solution.py:613
  68.5 1.4 collective-permute-start.8
  70.0 8.0 %collective-permute-start.9 = (bf16[192,64]{1,0:T(8,128)(2,1)}, bf16[192,64]{1,0:T(8,128)(2,1)S(1)}, u32[]{:S(2)}, u32[]{:S(2)}) collective-permute-start(bf16[192,64]{1,0:T(8,128)(2,1)} %get-tuple-element.39.ec), channel_id=1, source_target_pairs={{0,30},{1,29},{2,28},{3,27},{4,26},{5,25},{6,24},{7,23},{8,22},{9,... | collective-permute-start | bytes 73736 | tf_op jit(solution)/shard_map/ppermute | solution.py:613
  78.0 0.6 pad_maximum_fusion.1.side_weight
  78.8 0.8 reshape.149.weight
  79.6 4.5 %collective-permute-done.7.ecm = bf16[192,64]{1,0:T(8,128)(2,1)S(1)} collective-permute-done((bf16[192,64]{1,0:T(8,128)(2,1)}, bf16[192,64]{1,0:T(8,128)(2,1)S(1)}, u32[]{:S(2)}, u32[]{:S(2)}) %collective-permute-start.7) | collective-permute-done | bytes 24608 | tf_op jit(solution)/shard_map/ppermute | solution.py:613
  84.2 0.6 all-to-all-done.1.recv
  85.1 0.6 copy-done.4
  85.7 26.2 %encode.1 = (bf16[12,8,64,256]{3,2,1,0:T(8,128)(2,1)}, bf16[12,64,256]{2,1,0:T(8,128)(2,1)}, bf16[12,64,256]{2,1,0:T(8,128)(2,1)}, bf16[192,64]{1,0:T(8,128)(2,1...) custom-call(s32[1]{0:T(128)} %bitcast.stripe_ref, ...), custom_call_target="tpu_custom_call" | custom-call | flops 1811939328 | bytes 10822020 | tf_op jit(solution)/shard_map/encode/pallas_call | solution.py:595
  111.9 2.7 %all-to-all-start.3 = ((bf16[32,48,128]{2,1,0:T(8,128)(2,1)}), bf16[32,48,128]{2,1,0:T(8,128)(2,1)S(1)}, u32[]{:S(2)}, u32[]{:S(2)}) async-start(bf16[32,48,128]{2,1,0:T(8,128)(2,1)} %get-tuple-element.50), calls=%async_computation.3 | async-start | bytes 786432 | tf_op jit(solution)/shard_map/all_to_all | solution.py:622
  115.1 12.8 %all-to-all-done.3.recv = bf16[32,48,128]{2,1,0:T(8,128)(2,1)S(1)} async-done(((bf16[32,48,128]{2,1,0:T(8,128)(2,1)}), bf16[32,48,128]{2,1,0:T(8,128)(2,1)S(1)}, u32[]{:S(2)}, u32[]{:S(2)}) %all-to-all-start.3) | async-done | bytes 393248 | tf_op jit(solution)/shard_map/all_to_all | solution.py:622
  127.9 2.6 all-to-all-start.2
  131.0 5.2 %collective-permute-start.16 = (bf16[12,64,128]{2,1,0:T(8,128)(2,1)S(1)}, bf16[12,64,128]{2,1,0:T(8,128)(2,1)S(1)}, u32[]{:S(2)}, u32[]{:S(2)}) collective-permute-start(bf16[12,64,128]{2,1,0:T(8,128)(2,1)S(1)} %copy-done.27), channel_id=1, source_target_pairs={{0,31},{1,0},{2,1},{3,2},{4,3},{5,4},{6,5},{7,6},{8,7},{9,8},{10,9... | collective-permute-start | bytes 589832 | tf_op jit(solution)/shard_map/ppermute | solution.py:613
  136.8 0.7 collective-permute-start.18
  137.5 9.0 %collective-permute-start.19 = (bf16[192,64]{1,0:T(8,128)(2,1)S(1)}, bf16[192,64]{1,0:T(8,128)(2,1)S(1)}, u32[]{:S(2)}, u32[]{:S(2)}) collective-permute-start(bf16[192,64]{1,0:T(8,128)(2,1)S(1)} %copy-done.13), channel_id=1, source_target_pairs={{0,30},{1,29},{2,28},{3,27},{4,26},{5,25},{6,24},{7,23},{8,22},{9,... | collective-permute-start | bytes 73736 | tf_op jit(solution)/shard_map/ppermute | solution.py:613
  146.5 0.7 pad_maximum_fusion.2.side_weight
  147.3 0.8 reshape.151.weight
  148.1 1.6 collective-permute-done.17.ecm
  149.8 0.5 copy-done.14
  150.5 12.2 %coarse.1 = (bf16[12,4,64,128]{3,2,1,0:T(8,128)(2,1)}, bf16[12,64,128]{2,1,0:T(8,128)(2,1)}, bf16[12,64,128]{2,1,0:T(8,128)(2,1)}, bf16[192,64]{1,0:T(8,128)(2,1)}, bf16[32,48,128]{2,1,0:T(8,128)(2,1)}) custom-call(s32[1]{0:T(128)} %bitcast.stripe_ref, s32[48,2]{1,0:T(8,128)} %copy.197.tab, bf16[12,4,64,128]{3,2,1,0:T(8,128)(2,1)} %get-tuple-element.46.x, ...), custom_call_target="tpu_custom_call" | custom-call | flops 452984832 | bytes 3391876 | tf_op jit(solution)/shard_map/coarse/pallas_call | solution.py:595
  162.8 3.9 %all-to-all-start.4 = ((bf16[32,48,128]{2,1,0:T(8,128)(2,1)}), bf16[32,48,128]{2,1,0:T(8,128)(2,1)S(1)}, u32[]{:S(2)}, u32[]{:S(2)}) async-start(bf16[32,48,128]{2,1,0:T(8,128)(2,1)} %get-tuple-element.55), calls=%async_computation.4 | async-start | bytes 786432 | tf_op jit(solution)/shard_map/all_to_all | solution.py:622
  167.2 5.1 %collective-permute-start.11 = (bf16[12,64,256]{2,1,0:T(8,128)(2,1)S(1)}, bf16[12,64,256]{2,1,0:T(8,128)(2,1)}, u32[]{:S(2)}, u32[]{:S(2)}) collective-permute-start(bf16[12,64,256]{2,1,0:T(8,128)(2,1)S(1)} %copy-done.22), channel_id=1, source_target_pairs={{0,31},{1,0},{2,1},{3,2},{4,3},{5,4},{6,5},{7,6},{8,7},{9,8},{10,9... | collective-permute-start | bytes 1179656 | tf_op jit(solution)/shard_map/ppermute | solution.py:613
  172.7 1.4 collective-permute-start.13
  174.1 8.1 %collective-permute-start.14 = (bf16[192,64]{1,0:T(8,128)(2,1)}, bf16[192,64]{1,0:T(8,128)(2,1)S(1)}, u32[]{:S(2)}, u32[]{:S(2)}) collective-permute-start(bf16[192,64]{1,0:T(8,128)(2,1)} %get-tuple-element.44.ec), channel_id=1, source_target_pairs={{0,30},{1,29},{2,28},{3,27},{4,26},{5,25},{6,24},{7,23},{8,22},{9,... | collective-permute-start | bytes 73736 | tf_op jit(solution)/shard_map/ppermute | solution.py:613
  182.2 3.7 %collective-permute-done.12.ecm = bf16[192,64]{1,0:T(8,128)(2,1)S(1)} collective-permute-done((bf16[192,64]{1,0:T(8,128)(2,1)}, bf16[192,64]{1,0:T(8,128)(2,1)S(1)}, u32[]{:S(2)}, u32[]{:S(2)}) %collective-permute-start.12) | collective-permute-done | bytes 24608 | tf_op jit(solution)/shard_map/ppermute | solution.py:613
  185.9 0.6 copy-done.30
  186.5 5.3 %collective-permute-start.21 = (bf16[12,64,128]{2,1,0:T(8,128)(2,1)}, bf16[12,64,128]{2,1,0:T(8,128)(2,1)S(1)}, u32[]{:S(2)}, u32[]{:S(2)}) collective-permute-start(bf16[12,64,128]{2,1,0:T(8,128)(2,1)} %get-tuple-element.53), channel_id=1, source_target_pairs={{0,31},{1,0},{2,1},{3,2},{4,3},{5,4},{6,5},{7,6},{8,7},{9,8},{10,9... | collective-permute-start | bytes 589832 | tf_op jit(solution)/shard_map/ppermute | solution.py:613
  192.2 0.6 collective-permute-start.22
  192.8 2.1 collective-permute-start.23
  194.9 4.4 %collective-permute-start.24 = (bf16[192,64]{1,0:T(8,128)(2,1)}, bf16[192,64]{1,0:T(8,128)(2,1)S(1)}, u32[]{:S(2)}, u32[]{:S(2)}) collective-permute-start(bf16[192,64]{1,0:T(8,128)(2,1)} %get-tuple-element.54.yec), channel_id=1, source_target_pairs={{0,30},{1,29},{2,28},{3,27},{4,26},{5,25},{6,24},{7,23},{8,22},{9,... | collective-permute-start | bytes 73736 | tf_op jit(solution)/shard_map/ppermute | solution.py:613
  199.2 0.7 pad_maximum_fusion.3.side_weight
  200.6 1.0 reshape.153.weight
  201.6 0.7 add.47.col_key
  202.2 0.8 mul.112.head
  203.0 1.6 collective-permute-done.24.yecl
  204.7 0.6 copy-done.36
  205.5 22.4 %decode.1 = (bf16[8,12,8,256]{3,2,1,0:T(8,128)(2,1)}, bf16[32,24,256]{2,1,0:T(8,128)(2,1)}) custom-call(s32[1]{0:T(128)} %bitcast.stripe_ref, s32[48,2]{1,0:T(8,128)} %copy.197.tab, bf16[12,8,64,256]{3,2,1,0:T(8,128)(2,1)} %get-tuple-element.41.x, bf16[12,64,256]{2,1,0:T(8,128)(2,1)} %collective-permute-done.10.up, ...), custom_call_target="tpu_custom_call" | custom-call | flops 3623878656 | bytes 9098116 | tf_op jit(solution)/shard_map/decode/pallas_call | solution.py:595
  227.9 2.6 all-to-all-start.5
  231.9 0.8 concatenate.8.into
  232.7 0.8 pad_bitcast_fusion.state
  233.5 10.2 %all-to-all-done.5.recv = bf16[32,24,256]{2,1,0:T(8,128)(2,1)S(1)} async-done(((bf16[32,24,256]{2,1,0:T(8,128)(2,1)}), bf16[32,24,256]{2,1,0:T(8,128)(2,1)S(1)}, u32[]{:S(2)}, u32[]{:S(2)}) %all-to-all-start.5) | async-done | bytes 393248 | tf_op jit(solution)/shard_map/all_to_all | solution.py:751
  243.7 0.8 broadcast_in_dim.8.out_weight
  244.5 11.1 %ocean.1 = (f32[32,8,256]{2,1,0:T(8,128)}, bf16[32,8,256]{2,1,0:T(8,128)(2,1)}) custom-call(bf16[32,24,256]{2,1,0:T(8,128)(2,1)} %copy-done.1, f32[32,16,256]{2,1,0:T(8,128)} %pad_bitcast_fusion.state, bf16[384,112]{1,0:T(8,128)(2,1)} %concatenate.8.into, f32[384,128]{1,0:T(8,128)} %broadcast_in_dim.8.out_weight), custom_call_target="tpu_custom_call" | custom-call | flops 50331648 | bytes 1593344 | tf_op jit(solution)/shard_map/ocean/pallas_call | solution.py:595
  255.7 2.6 all-to-all-start.6
  258.2 0.7 copy.204.key
  259.0 1.0 stack.48
  260.0 1.1 copy.206
  261.0 5.4 %all-to-all-done.6.back = bf16[32,8,256]{2,1,0:T(8,128)(2,1)S(1)} async-done(((bf16[32,8,256]{2,1,0:T(8,128)(2,1)}), bf16[32,8,256]{2,1,0:T(8,128)(2,1)S(1)}, u32[]{:S(2)}, u32[]{:S(2)}) %all-to-all-start.6) | async-done | bytes 131104 | tf_op jit(solution)/shard_map/all_to_all | solution.py:782
  266.5 0.6 copy-done.5
  267.1 1.8 surface.1
  (160 shorter events, 7.5 us)
Async XLA Ops:
  9.9 57.8 %copy-start.11 = (bf16[3,64,192]{2,1,0:T(8,128)(2,1)S(1)}, bf16[3,64,192]{2,1,0:T(8,128)(2,1)}, u32[]{:S(2)}) copy-start(bf16[3,64,192]{2,1,0:T(8,128)(2,1)} %param.24) | copy-start | bytes 221188
  9.9 29.5 %all-to-all-start = ((bf16[32,32,128]{2,1,0:T(8,128)(2,1)}), bf16[32,32,128]{2,1,0:T(8,128)(2,1)S(1)}, u32[]{:S(2)}, u32[]{:S(2)}) async-start(bf16[32,32,128]{2,1,0:T(8,128)(2,1)} %get-tuple-element.35), calls=%async_computation | async-start | bytes 524288 | tf_op jit(solution)/shard_map/all_to_all | solution.py:622
  16.6 22.0 %collective-permute-start.2 = (bf16[192,32]{1,0:T(8,128)(2,1)}, bf16[192,32]{1,0:T(8,128)(2,1)S(1)}, u32[]{:S(2)}, u32[]{:S(2)}) collective-permute-start(bf16[192,32]{1,0:T(8,128)(2,1)} %get-tuple-element.34.ec), channel_id=1, source_target_pairs={{0,31},{1,30},{2,29},{3,28},{4,27},{5,26},{6,25},{7,24},{8,23},{9,... | collective-permute-start | bytes 36872 | tf_op jit(solution)/shard_map/ppermute | solution.py:613
  21.9 16.7 %collective-permute-start.3 = (bf16[192,32]{1,0:T(8,128)(2,1)}, bf16[192,32]{1,0:T(8,128)(2,1)S(1)}, u32[]{:S(2)}, u32[]{:S(2)}) collective-permute-start(bf16[192,32]{1,0:T(8,128)(2,1)} %get-tuple-element.34.ec), channel_id=1, source_target_pairs={{0,0},{1,31},{2,30},{3,29},{4,28},{5,27},{6,26},{7,25},{8,24},{9,2... | collective-permute-start | bytes 36872 | tf_op jit(solution)/shard_map/ppermute | solution.py:613
  23.3 15.3 %collective-permute-start.4 = (bf16[192,32]{1,0:T(8,128)(2,1)}, bf16[192,32]{1,0:T(8,128)(2,1)S(1)}, u32[]{:S(2)}, u32[]{:S(2)}) collective-permute-start(bf16[192,32]{1,0:T(8,128)(2,1)} %get-tuple-element.34.ec), channel_id=1, source_target_pairs={{0,30},{1,29},{2,28},{3,27},{4,26},{5,25},{6,24},{7,23},{8,22},{9,... | collective-permute-start | bytes 36872 | tf_op jit(solution)/shard_map/ppermute | solution.py:613
  30.4 9.0 %collective-permute-start = (bf16[12,32,256]{2,1,0:T(8,128)(2,1)}, bf16[12,32,256]{2,1,0:T(8,128)(2,1)S(1)}, u32[]{:S(2)}, u32[]{:S(2)}) collective-permute-start(bf16[12,32,256]{2,1,0:T(8,128)(2,1)} %get-tuple-element.32), channel_id=1, source_target_pairs={{0,1},{1,2},{2,3},{3,4},{4,5},{5,6},{6,7},{7,8},{8,9},{9,10},{10,1... | collective-permute-start | bytes 589832 | tf_op jit(solution)/shard_map/ppermute | solution.py:613
  30.5 8.9 %collective-permute-start.1 = (bf16[12,32,256]{2,1,0:T(8,128)(2,1)}, bf16[12,32,256]{2,1,0:T(8,128)(2,1)S(1)}, u32[]{:S(2)}, u32[]{:S(2)}) collective-permute-start(bf16[12,32,256]{2,1,0:T(8,128)(2,1)} %get-tuple-element.33), channel_id=1, source_target_pairs={{0,31},{1,0},{2,1},{3,2},{4,3},{5,4},{6,5},{7,6},{8,7},{9,8},{10,9... | collective-permute-start | bytes 589832 | tf_op jit(solution)/shard_map/ppermute | solution.py:613
  38.6 0.8 copy-start.33
  38.6 0.8 copy-start.34
  38.6 0.8 copy-start.35
  39.4 0.7 copy-start.29
  39.4 0.8 copy-start.7
  56.6 28.2 %all-to-all-start.1 = ((bf16[32,64,128]{2,1,0:T(8,128)(2,1)}), bf16[32,64,128]{2,1,0:T(8,128)(2,1)S(1)}, u32[]{:S(2)}, u32[]{:S(2)}) async-start(bf16[32,64,128]{2,1,0:T(8,128)(2,1)} %get-tuple-element.40), calls=%async_computation.1 | async-start | bytes 1048576 | tf_op jit(solution)/shard_map/all_to_all | solution.py:622
  62.3 21.9 %collective-permute-start.5 = (bf16[12,64,256]{2,1,0:T(8,128)(2,1)}, bf16[12,64,256]{2,1,0:T(8,128)(2,1)S(1)}, u32[]{:S(2)}, u32[]{:S(2)}) collective-permute-start(bf16[12,64,256]{2,1,0:T(8,128)(2,1)} %get-tuple-element.37), channel_id=1, source_target_pairs={{0,1},{1,2},{2,3},{3,4},{4,5},{5,6},{6,7},{7,8},{8,9},{9,10},{10,1... | collective-permute-start | bytes 1179656 | tf_op jit(solution)/shard_map/ppermute | solution.py:613
  62.6 21.6 %collective-permute-start.6 = (bf16[12,64,256]{2,1,0:T(8,128)(2,1)}, bf16[12,64,256]{2,1,0:T(8,128)(2,1)S(1)}, u32[]{:S(2)}, u32[]{:S(2)}) collective-permute-start(bf16[12,64,256]{2,1,0:T(8,128)(2,1)} %get-tuple-element.38), channel_id=1, source_target_pairs={{0,31},{1,0},{2,1},{3,2},{4,3},{5,4},{6,5},{7,6},{8,7},{9,8},{10,9... | collective-permute-start | bytes 1179656 | tf_op jit(solution)/shard_map/ppermute | solution.py:613
  68.1 16.1 %collective-permute-start.7 = (bf16[192,64]{1,0:T(8,128)(2,1)}, bf16[192,64]{1,0:T(8,128)(2,1)S(1)}, u32[]{:S(2)}, u32[]{:S(2)}) collective-permute-start(bf16[192,64]{1,0:T(8,128)(2,1)} %get-tuple-element.39.ec), channel_id=1, source_target_pairs={{0,31},{1,30},{2,29},{3,28},{4,27},{5,26},{6,25},{7,24},{8,23},{9,... | collective-permute-start | bytes 73736 | tf_op jit(solution)/shard_map/ppermute | solution.py:613
  68.5 15.6 %collective-permute-start.8 = (bf16[192,64]{1,0:T(8,128)(2,1)}, bf16[192,64]{1,0:T(8,128)(2,1)S(1)}, u32[]{:S(2)}, u32[]{:S(2)}) collective-permute-start(bf16[192,64]{1,0:T(8,128)(2,1)} %get-tuple-element.39.ec), channel_id=1, source_target_pairs={{0,0},{1,31},{2,30},{3,29},{4,28},{5,27},{6,26},{7,25},{8,24},{9,2... | collective-permute-start | bytes 73736 | tf_op jit(solution)/shard_map/ppermute | solution.py:613
  70.0 14.2 %collective-permute-start.9 = (bf16[192,64]{1,0:T(8,128)(2,1)}, bf16[192,64]{1,0:T(8,128)(2,1)S(1)}, u32[]{:S(2)}, u32[]{:S(2)}) collective-permute-start(bf16[192,64]{1,0:T(8,128)(2,1)} %get-tuple-element.39.ec), channel_id=1, source_target_pairs={{0,30},{1,29},{2,28},{3,27},{4,26},{5,25},{6,24},{7,23},{8,22},{9,... | collective-permute-start | bytes 73736 | tf_op jit(solution)/shard_map/ppermute | solution.py:613
  84.1 0.7 copy-start.37
  84.1 0.7 copy-start.38
  84.2 0.8 copy-start.23
  84.2 0.9 copy-start.24
  84.8 0.8 copy-start.4
  85.7 29.0 %copy-start.12 = (bf16[3,64,192]{2,1,0:T(8,128)(2,1)S(1)}, bf16[3,64,192]{2,1,0:T(8,128)(2,1)}, u32[]{:S(2)}) copy-start(bf16[3,64,192]{2,1,0:T(8,128)(2,1)} %param.25) | copy-start | bytes 221188
  85.7 29.2 %copy-start.10 = (bf16[3,64,384]{2,1,0:T(8,128)(2,1)S(1)}, bf16[3,64,384]{2,1,0:T(8,128)(2,1)}, u32[]{:S(2)}) copy-start(bf16[3,64,384]{2,1,0:T(8,128)(2,1)} %param.26) | copy-start | bytes 442372
  85.7 44.8 %copy-start.18 = (bf16[12,64]{1,0:T(8,128)(2,1)S(1)}, bf16[12,64]{1,0:T(8,128)(2,1)}, u32[]{:S(2)}) copy-start(bf16[12,64]{1,0:T(8,128)(2,1)} %param.27) | copy-start | bytes 4612
  111.9 19.1 %copy-start.27 = (bf16[12,64,128]{2,1,0:T(8,128)(2,1)S(1)}, bf16[12,64,128]{2,1,0:T(8,128)(2,1)}, u32[]{:S(2)}) copy-start(bf16[12,64,128]{2,1,0:T(8,128)(2,1)} %get-tuple-element.48) | copy-start | bytes 589828
  111.9 24.2 %copy-start.19 = (f32[64,6]{0,1:T(8,128)S(1)}, f32[64,6]{0,1:T(8,128)}, u32[]{:S(2)}) copy-start(f32[64,6]{0,1:T(8,128)} %param.28) | copy-start | bytes 4612
  111.9 24.4 %copy-start.13 = (bf16[192,64]{1,0:T(8,128)(2,1)S(1)}, bf16[192,64]{1,0:T(8,128)(2,1)}, u32[]{:S(2)}) copy-start(bf16[192,64]{1,0:T(8,128)(2,1)} %get-tuple-element.49.ec) | copy-start | bytes 73732
  111.9 15.9 %all-to-all-start.3 = ((bf16[32,48,128]{2,1,0:T(8,128)(2,1)}), bf16[32,48,128]{2,1,0:T(8,128)(2,1)S(1)}, u32[]{:S(2)}, u32[]{:S(2)}) async-start(bf16[32,48,128]{2,1,0:T(8,128)(2,1)} %get-tuple-element.50), calls=%async_computation.3 | async-start | bytes 786432 | tf_op jit(solution)/shard_map/all_to_all | solution.py:622
  114.7 52.0 %copy-start.17 = (pred[96,96]{1,0:T(32,128)(4,1)S(1)}, pred[96,96]{1,0:T(32,128)(4,1)}, u32[]{:S(2)}) copy-start(pred[96,96]{1,0:T(32,128)(4,1)} %constant.29.clone) | copy-start | bytes 27652
  114.7 52.0 %copy-start.20 = (s32[96,1]{0,1:T(1,128)S(1)}, s32[96,1]{0,1:T(1,128)}, u32[]{:S(2)}) copy-start(s32[96,1]{0,1:T(1,128)} %param.20) | copy-start | bytes 1156
  114.7 52.5 %copy-start.22 = (bf16[12,64,256]{2,1,0:T(8,128)(2,1)S(1)}, bf16[12,64,256]{2,1,0:T(8,128)(2,1)}, u32[]{:S(2)}) copy-start(bf16[12,64,256]{2,1,0:T(8,128)(2,1)} %get-tuple-element.43) | copy-start | bytes 1179652
  127.9 21.9 %copy-start = (bf16[32,48,128]{2,1,0:T(8,128)(2,1)}, bf16[32,48,128]{2,1,0:T(8,128)(2,1)S(1)}, u32[]{:S(2)}) copy-start(bf16[32,48,128]{2,1,0:T(8,128)(2,1)S(1)} %all-to-all-done.3.recv) | copy-start | bytes 1179652
  127.9 34.9 %all-to-all-start.2 = ((bf16[32,64,128]{2,1,0:T(8,128)(2,1)}), bf16[32,64,128]{2,1,0:T(8,128)(2,1)S(1)}, u32[]{:S(2)}, u32[]{:S(2)}) async-start(bf16[32,64,128]{2,1,0:T(8,128)(2,1)} %get-tuple-element.45), calls=%async_computation.2 | async-start | bytes 1048576 | tf_op jit(solution)/shard_map/all_to_all | solution.py:622
  130.5 69.9 %copy-start.2 = (f32[1,1,192,2,256]{4,3,2,1,0:T(2,128)S(1)}, f32[1,1,192,2,256]{4,3,2,1,0:T(2,128)}, u32[]{:S(2)}) copy-start(f32[1,1,192,2,256]{4,3,2,1,0:T(2,128)} %param.22) | copy-start | bytes 1179652
  130.8 19.0 %collective-permute-start.15 = (bf16[12,64,128]{2,1,0:T(8,128)(2,1)}, bf16[12,64,128]{2,1,0:T(8,128)(2,1)S(1)}, u32[]{:S(2)}, u32[]{:S(2)}) collective-permute-start(bf16[12,64,128]{2,1,0:T(8,128)(2,1)} %get-tuple-element.47), channel_id=1, source_target_pairs={{0,1},{1,2},{2,3},{3,4},{4,5},{5,6},{6,7},{7,8},{8,9},{9,10},{10,1... | collective-permute-start | bytes 589832 | tf_op jit(solution)/shard_map/ppermute | solution.py:613
  131.0 18.7 %collective-permute-start.16 = (bf16[12,64,128]{2,1,0:T(8,128)(2,1)S(1)}, bf16[12,64,128]{2,1,0:T(8,128)(2,1)S(1)}, u32[]{:S(2)}, u32[]{:S(2)}) collective-permute-start(bf16[12,64,128]{2,1,0:T(8,128)(2,1)S(1)} %copy-done.27), channel_id=1, source_target_pairs={{0,31},{1,0},{2,1},{3,2},{4,3},{5,4},{6,5},{7,6},{8,7},{9,8},{10,9... | collective-permute-start | bytes 589832 | tf_op jit(solution)/shard_map/ppermute | solution.py:613
  136.4 13.3 %collective-permute-start.17 = (bf16[192,64]{1,0:T(8,128)(2,1)S(1)}, bf16[192,64]{1,0:T(8,128)(2,1)S(1)}, u32[]{:S(2)}, u32[]{:S(2)}) collective-permute-start(bf16[192,64]{1,0:T(8,128)(2,1)S(1)} %copy-done.13), channel_id=1, source_target_pairs={{0,31},{1,30},{2,29},{3,28},{4,27},{5,26},{6,25},{7,24},{8,23},{9,... | collective-permute-start | bytes 73736 | tf_op jit(solution)/shard_map/ppermute | solution.py:613
  136.8 12.9 %collective-permute-start.18 = (bf16[192,64]{1,0:T(8,128)(2,1)S(1)}, bf16[192,64]{1,0:T(8,128)(2,1)S(1)}, u32[]{:S(2)}, u32[]{:S(2)}) collective-permute-start(bf16[192,64]{1,0:T(8,128)(2,1)S(1)} %copy-done.13), channel_id=1, source_target_pairs={{0,0},{1,31},{2,30},{3,29},{4,28},{5,27},{6,26},{7,25},{8,24},{9,2... | collective-permute-start | bytes 73736 | tf_op jit(solution)/shard_map/ppermute | solution.py:613
  137.5 12.2 %collective-permute-start.19 = (bf16[192,64]{1,0:T(8,128)(2,1)S(1)}, bf16[192,64]{1,0:T(8,128)(2,1)S(1)}, u32[]{:S(2)}, u32[]{:S(2)}) collective-permute-start(bf16[192,64]{1,0:T(8,128)(2,1)S(1)} %copy-done.13), channel_id=1, source_target_pairs={{0,30},{1,29},{2,28},{3,27},{4,26},{5,25},{6,24},{7,23},{8,22},{9,... | collective-permute-start | bytes 73736 | tf_op jit(solution)/shard_map/ppermute | solution.py:613
  149.7 0.7 copy-start.8
  149.7 0.8 copy-start.9
  162.8 41.9 %copy-start.3 = (bf16[32,64,128]{2,1,0:T(8,128)(2,1)}, bf16[32,64,128]{2,1,0:T(8,128)(2,1)S(1)}, u32[]{:S(2)}) copy-start(bf16[32,64,128]{2,1,0:T(8,128)(2,1)S(1)} %all-to-all-done.2.recv) | copy-start | bytes 1572868
  162.8 41.9 %all-to-all-start.4 = ((bf16[32,48,128]{2,1,0:T(8,128)(2,1)}), bf16[32,48,128]{2,1,0:T(8,128)(2,1)S(1)}, u32[]{:S(2)}, u32[]{:S(2)}) async-start(bf16[32,48,128]{2,1,0:T(8,128)(2,1)} %get-tuple-element.55), calls=%async_computation.4 | async-start | bytes 786432 | tf_op jit(solution)/shard_map/all_to_all | solution.py:622
  166.9 25.9 %collective-permute-start.10 = (bf16[12,64,256]{2,1,0:T(8,128)(2,1)}, bf16[12,64,256]{2,1,0:T(8,128)(2,1)}, u32[]{:S(2)}, u32[]{:S(2)}) collective-permute-start(bf16[12,64,256]{2,1,0:T(8,128)(2,1)} %get-tuple-element.42), channel_id=1, source_target_pairs={{0,1},{1,2},{2,3},{3,4},{4,5},{5,6},{6,7},{7,8},{8,9},{9,10},{10,1... | collective-permute-start | bytes 1179656 | tf_op jit(solution)/shard_map/ppermute | solution.py:613
  167.2 27.6 %collective-permute-start.11 = (bf16[12,64,256]{2,1,0:T(8,128)(2,1)S(1)}, bf16[12,64,256]{2,1,0:T(8,128)(2,1)}, u32[]{:S(2)}, u32[]{:S(2)}) collective-permute-start(bf16[12,64,256]{2,1,0:T(8,128)(2,1)S(1)} %copy-done.22), channel_id=1, source_target_pairs={{0,31},{1,0},{2,1},{3,2},{4,3},{5,4},{6,5},{7,6},{8,7},{9,8},{10,9... | collective-permute-start | bytes 1179656 | tf_op jit(solution)/shard_map/ppermute | solution.py:613
  172.3 13.6 %collective-permute-start.12 = (bf16[192,64]{1,0:T(8,128)(2,1)}, bf16[192,64]{1,0:T(8,128)(2,1)S(1)}, u32[]{:S(2)}, u32[]{:S(2)}) collective-permute-start(bf16[192,64]{1,0:T(8,128)(2,1)} %get-tuple-element.44.ec), channel_id=1, source_target_pairs={{0,31},{1,30},{2,29},{3,28},{4,27},{5,26},{6,25},{7,24},{8,23},{9,... | collective-permute-start | bytes 73736 | tf_op jit(solution)/shard_map/ppermute | solution.py:613
  172.7 13.8 %collective-permute-start.13 = (bf16[192,64]{1,0:T(8,128)(2,1)}, bf16[192,64]{1,0:T(8,128)(2,1)S(1)}, u32[]{:S(2)}, u32[]{:S(2)}) collective-permute-start(bf16[192,64]{1,0:T(8,128)(2,1)} %get-tuple-element.44.ec), channel_id=1, source_target_pairs={{0,0},{1,31},{2,30},{3,29},{4,28},{5,27},{6,26},{7,25},{8,24},{9,2... | collective-permute-start | bytes 73736 | tf_op jit(solution)/shard_map/ppermute | solution.py:613
  174.1 18.0 %collective-permute-start.14 = (bf16[192,64]{1,0:T(8,128)(2,1)}, bf16[192,64]{1,0:T(8,128)(2,1)S(1)}, u32[]{:S(2)}, u32[]{:S(2)}) collective-permute-start(bf16[192,64]{1,0:T(8,128)(2,1)} %get-tuple-element.44.ec), channel_id=1, source_target_pairs={{0,30},{1,29},{2,28},{3,27},{4,26},{5,25},{6,24},{7,23},{8,22},{9,... | collective-permute-start | bytes 73736 | tf_op jit(solution)/shard_map/ppermute | solution.py:613
  186.5 18.1 %collective-permute-start.20 = (bf16[12,64,128]{2,1,0:T(8,128)(2,1)}, bf16[12,64,128]{2,1,0:T(8,128)(2,1)S(1)}, u32[]{:S(2)}, u32[]{:S(2)}) collective-permute-start(bf16[12,64,128]{2,1,0:T(8,128)(2,1)} %get-tuple-element.52), channel_id=1, source_target_pairs={{0,1},{1,2},{2,3},{3,4},{4,5},{5,6},{6,7},{7,8},{8,9},{9,10},{10,1... | collective-permute-start | bytes 589832 | tf_op jit(solution)/shard_map/ppermute | solution.py:613
  186.5 5.4 %copy-start.31 = (bf16[192,64]{1,0:T(8,128)(2,1)}, bf16[192,64]{1,0:T(8,128)(2,1)S(1)}, u32[]{:S(2)}) copy-start(bf16[192,64]{1,0:T(8,128)(2,1)S(1)} %collective-permute-done.13.ecf) | copy-start | bytes 73732
  186.5 18.1 %collective-permute-start.21 = (bf16[12,64,128]{2,1,0:T(8,128)(2,1)}, bf16[12,64,128]{2,1,0:T(8,128)(2,1)S(1)}, u32[]{:S(2)}, u32[]{:S(2)}) collective-permute-start(bf16[12,64,128]{2,1,0:T(8,128)(2,1)} %get-tuple-element.53), channel_id=1, source_target_pairs={{0,31},{1,0},{2,1},{3,2},{4,3},{5,4},{6,5},{7,6},{8,7},{9,8},{10,9... | collective-permute-start | bytes 589832 | tf_op jit(solution)/shard_map/ppermute | solution.py:613
  192.2 8.2 %copy-start.32 = (bf16[192,64]{1,0:T(8,128)(2,1)}, bf16[192,64]{1,0:T(8,128)(2,1)S(1)}, u32[]{:S(2)}) copy-start(bf16[192,64]{1,0:T(8,128)(2,1)S(1)} %collective-permute-done.14.ecl) | copy-start | bytes 73732
  192.2 10.9 %collective-permute-start.22 = (bf16[192,64]{1,0:T(8,128)(2,1)}, bf16[192,64]{1,0:T(8,128)(2,1)}, u32[]{:S(2)}, u32[]{:S(2)}) collective-permute-start(bf16[192,64]{1,0:T(8,128)(2,1)} %get-tuple-element.54.yec), channel_id=1, source_target_pairs={{0,31},{1,30},{2,29},{3,28},{4,27},{5,26},{6,25},{7,24},{8,23},{9,... | collective-permute-start | bytes 73736 | tf_op jit(solution)/shard_map/ppermute | solution.py:613
  192.8 10.3 %collective-permute-start.23 = (bf16[192,64]{1,0:T(8,128)(2,1)}, bf16[192,64]{1,0:T(8,128)(2,1)}, u32[]{:S(2)}, u32[]{:S(2)}) collective-permute-start(bf16[192,64]{1,0:T(8,128)(2,1)} %get-tuple-element.54.yec), channel_id=1, source_target_pairs={{0,0},{1,31},{2,30},{3,29},{4,28},{5,27},{6,26},{7,25},{8,24},{9,2... | collective-permute-start | bytes 73736 | tf_op jit(solution)/shard_map/ppermute | solution.py:613
  194.9 9.8 %collective-permute-start.24 = (bf16[192,64]{1,0:T(8,128)(2,1)}, bf16[192,64]{1,0:T(8,128)(2,1)S(1)}, u32[]{:S(2)}, u32[]{:S(2)}) collective-permute-start(bf16[192,64]{1,0:T(8,128)(2,1)} %get-tuple-element.54.yec), channel_id=1, source_target_pairs={{0,30},{1,29},{2,28},{3,27},{4,26},{5,25},{6,24},{7,23},{8,22},{9,... | collective-permute-start | bytes 73736 | tf_op jit(solution)/shard_map/ppermute | solution.py:613
  204.6 0.7 copy-start.25
  204.6 0.8 copy-start.26
  204.7 0.9 copy-start.6
  205.5 26.2 %copy-start.21 = (f32[64]{0:T(128)S(1)}, f32[64]{0:T(128)}, u32[]{:S(2)}) copy-start(f32[64]{0:T(128)} %param.29) | copy-start | bytes 772
  227.9 15.8 %all-to-all-start.5 = ((bf16[32,24,256]{2,1,0:T(8,128)(2,1)}), bf16[32,24,256]{2,1,0:T(8,128)(2,1)S(1)}, u32[]{:S(2)}, u32[]{:S(2)}) async-start(bf16[32,24,256]{2,1,0:T(8,128)(2,1)} %get-tuple-element.56), calls=%async_computation.5 | async-start | bytes 786432 | tf_op jit(solution)/shard_map/all_to_all | solution.py:751
  243.7 0.8 copy-start.1
  255.7 10.8 %all-to-all-start.6 = ((bf16[32,8,256]{2,1,0:T(8,128)(2,1)}), bf16[32,8,256]{2,1,0:T(8,128)(2,1)S(1)}, u32[]{:S(2)}, u32[]{:S(2)}) async-start(bf16[32,8,256]{2,1,0:T(8,128)(2,1)} %get-tuple-element.57), calls=%async_computation.6 | async-start | bytes 262144 | tf_op jit(solution)/shard_map/all_to_all | solution.py:782
  (8 other events, 5.1 us)
where the time goes:
time: 270 us; the launch traced here: 269 us
  starting transfers between devices  104 us (39%)
  Pallas kernels  98.1 us (36%)
  waiting for transfers between devices  41.1 us (15%)
  local copies, waits for them, and re-layouts  21.3 us (8%)
    pallas_call x7, Pallas kernels, call(): pl.pallas_call(kernel, out_shape=outs, **grid, in_specs=in_specs, out_spe...  98.1 us
    ppermute x25, starting transfers between devices, move(): lax.ppermute(values, 'tile', [(i, to(i) % tiles) for i in range(tiles)])  77.7 us
    all_to_all x5, starting transfers between devices, exchange(): lax.all_to_all(send, 'tile', split_axis=0, concat_axis=0, tiled=True)  21.6 us
    all_to_all x5, waiting for transfers between devices, exchange(): lax.all_to_all(send, 'tile', split_axis=0, concat_axis=0, tiled=True)  13.4 us
    ppermute x25, waiting for transfers between devices, move(): lax.ppermute(values, 'tile', [(i, to(i) % tiles) for i in range(tiles)])  12.1 us
    all_to_all x1, waiting for transfers between devices, on_one_group(): lax.all_to_all(outgoing, 'tile', split_axis=0, concat_axis=0, tiled=True)  10.2 us
    unnamed x87, local copies, waits for them, and re-layouts  8.42 us
    all_to_all x1, waiting for transfers between devices, on_one_group(): lax.all_to_all(back, 'tile', split_axis=0, concat_axis=0, tiled=True)  5.43 us
  transfers between devices with their start and end apart: 32, of which 9 were waited for; matrix products, arithmetic and copies ran while one was open for 6% of the time, Pallas kernels for 5%

commit v1 on v0

--- a/solution.py
+++ b/solution.py
@@ -217,17 +217,19 @@
         self.per = LANES // chans
         self.groups = faces // self.per
         self.span = rows + 2
-        used = self.groups * self.span
+        self.extra = self.groups * self.span
+        used = max(self.extra + 2 * self.groups, 2 * self.groups * rows)
         self.chunk = used + (-used) % 16
 
     def main(self):
         return jax.ShapeDtypeStruct((self.faces, self.rows, self.chans, self.side), BF)
 
-    def outs(self):
-        edge = jax.ShapeDtypeStruct((self.faces, self.chans, self.side), BF)
+    def edges(self, more=0):
+        edge = jax.ShapeDtypeStruct((self.faces, self.chans, self.side + more), BF)
+        return [edge, edge]
+
+    def sends(self):
         return [
-            edge,
-            edge,
             jax.ShapeDtypeStruct((2 * self.faces * 8, self.chans), BF),
             jax.ShapeDtypeStruct((self.tiles, self.chunk, LANES), BF),
         ]
@@ -247,6 +249,7 @@
             pltpu.VMEM((self.faces, self.chans, self.side), BF),
             pltpu.VMEM((2, self.faces, self.chans, self.side), BF),
             pltpu.VMEM((self.tiles, self.chunk, LANES), F32),
+            pltpu.VMEM((2, self.faces, 8, self.chans), F32),
         ]
 
 
@@ -255,30 +258,33 @@
     return (row == jnp.where(flag == 1, size - 1 - col, col)).astype(F32).astype(BF)
 
 
-def edge_columns(fld, face_rows):
-    row, col = iota((16, fld.side), 0), iota((16, fld.side), 1)
-    total = jnp.zeros((16, fld.chans), F32)
-    for r, cells in enumerate(face_rows):
-        pick = ((row == r) & (col == 0)) | ((row == 8 + r) & (col == fld.side - 1))
-        total = total + mm_nt(pick.astype(F32).astype(BF), cells)
-    return total
-
-
-def pack_sends(fld, stripe, tab, top, bot, ec_out, send_out, cols, stage, strip):
-    last = fld.tiles - 1
-    ec_out[...] = cols[...].reshape(2 * fld.faces * 8, fld.chans).astype(BF)
+def end_picker(side):
+    row, col = iota((16, side), 0), iota((16, side), 1)
+    return (((row == 0) & (col == 0)) | ((row == 1) & (col == side - 1))).astype(F32).astype(BF)
+
+
+def keep_columns(fld, face_rows, f, cols):
+    picked = mm_nt(end_picker(fld.side), jnp.concatenate(face_rows, axis=0))
+    for s in range(2):
+        for r in range(fld.rows):
+            cols[s, f, r : r + 1] = picked[s : s + 1, r * fld.chans : (r + 1) * fld.chans]
+
+
+def pack_sends(fld, stripe, tab, top, bot, off, ec_out, send_out, cols, stage, strip):
+    last, rows, chans = fld.tiles - 1, fld.rows, fld.chans
+    ec_out[...] = cols[...].reshape(2 * fld.faces * 8, chans).astype(BF)
     stage[...] = jnp.zeros_like(stage)
+
+    def lanes(h):
+        return slice((h % fld.per) * chans, (h % fld.per + 1) * chans)
+
     for q in range(2):
         for g in range(fld.faces):
             p = tab[4 * g + q, 0]
-            kind, h = p % 4, p // 4
+            kind, h = p & 3, p >> 2
             piece = cols[jnp.maximum(kind - 2, 0), h]
-            i, j = g // fld.per, g % fld.per
-            stage[
-                q * last,
-                i * fld.span + 1 : i * fld.span + 1 + fld.rows,
-                j * fld.chans : (j + 1) * fld.chans,
-            ] = piece[: fld.rows]
+            at = (g // fld.per) * fld.span + 1
+            stage[q * last, at : at + rows, lanes(g)] = piece[:rows]
 
     @pl.when((stripe == 0) | (stripe == last))
     def _():
@@ -287,62 +293,82 @@
             strip[...] = jnp.zeros_like(strip)
             for j in range(fld.per):
                 h = i * fld.per + j
-                cells = jnp.where(q == 0, top[h].astype(F32), bot[h].astype(F32)).astype(BF)
+                upper = top[h, :, off : off + fld.side].astype(F32)
+                lower = bot[h, :, off : off + fld.side].astype(F32)
+                cells = jnp.where(q == 0, upper, lower).astype(BF)
                 turned = mm_nt(flip_matrix(fld.side, tab[4 * h + q, 1]), cells)
-                strip[1 : fld.side + 1, j * fld.chans : (j + 1) * fld.chans] = turned
+                strip[1 : fld.side + 1, lanes(h)] = turned
             for d in range(1, last):
-                stage[d, i * fld.span : (i + 1) * fld.span, :] = strip[
-                    d * fld.rows : d * fld.rows + fld.span, :
-                ]
+                stage[d, i * fld.span : (i + 1) * fld.span, :] = strip[d * rows : d * rows + fld.span, :]
+
+    for s in range(2):
+        for h in range(fld.faces):
+            at = (s * fld.groups + h // fld.per) * rows
+            stage[last - stripe, at : at + rows, lanes(h)] = cols[s, h, :rows]
+
+    @pl.when(stripe < last)
+    def _():
+        for s in range(2):
+            for h in range(fld.faces):
+                at = fld.extra + s * fld.groups + h // fld.per
+                stage[last - 1 - stripe, at : at + 1, lanes(h)] = cols[s, h, rows - 1 : rows]
+
+    @pl.when(stripe > 0)
+    def _():
+        for s in range(2):
+            for h in range(fld.faces):
+                at = fld.extra + s * fld.groups + h // fld.per
+                stage[last + 1 - stripe, at : at + 1, lanes(h)] = cols[s, h, 0:1]
 
     send_out[...] = stage[...].astype(BF)
 
 
-def gather_halos(fld, stripe, tab, x, up, dn, ec, ecm, ecf, ecl, recv, cand, cols, above, below, pair, got):
+def gather_halos(fld, stripe, tab, x, up, dn, off, ec, recv, cand, cols, above, below, pair, got, mirror):
     faces, rows, chans, side, tiles = fld.faces, fld.rows, fld.chans, fld.side, fld.tiles
     last = tiles - 1
+    groups = fld.groups
     got[...] = recv[...].astype(F32)
     own = ec[...].astype(F32).reshape(2, faces, 8, chans)
-    row, col = iota((faces * 8, faces * 8), 0), iota((faces * 8, faces * 8), 1)
-    turn = ((row // 8 == col // 8) & (row % 8 + col % 8 == rows - 1)).astype(F32).astype(BF)
-    first = ecf[...].astype(F32).reshape(2, faces, 8, chans)
-    final = ecl[...].astype(F32).reshape(2, faces, 8, chans)
+    row, col = iota((groups * rows, groups * rows), 0), iota((groups * rows, groups * rows), 1)
+    turn = ((row // rows == col // rows) & (row % rows + col % rows == rows - 1)).astype(F32).astype(BF)
     prow, pcol = iota((16, side), 0), iota((16, side), 1)
-    ends = ((prow == 0) & (pcol == 0)) | ((prow == 1) & (pcol == side - 1))
-    ends = ends.astype(F32).astype(BF)
-    for h in range(faces):
-        over, under = mm_nt(ends, up[h]), mm_nt(ends, dn[h])
-        for s in range(2):
-            cand[2 + s, h, 0:1] = over[s : s + 1]
-            cand[2 + s, h, rows + 1 : rows + 2] = under[s : s + 1]
+
+    def lanes(h):
+        return slice((h % fld.per) * chans, (h % fld.per + 1) * chans)
+
+    above[...] = up[:, :, off : off + side]
+    below[...] = dn[:, :, off : off + side]
+    over = mm_nt(end_picker(side), above[...].reshape(faces * chans, side))
+    under = mm_nt(end_picker(side), below[...].reshape(faces * chans, side))
+    before = got[jnp.minimum(last + 1 - stripe, last), fld.extra : fld.extra + 2 * groups, :]
+    after = got[jnp.maximum(last - 1 - stripe, 0), fld.extra : fld.extra + 2 * groups, :]
+    for s in range(2):
+        across = got[last - stripe, s * groups * rows : (s + 1) * groups * rows, :]
+        turned = mm(turn, across.astype(BF))
+        for h in range(faces):
+            i = h // fld.per
+            cand[2 + s, h, 0:1] = over[s : s + 1, h * chans : (h + 1) * chans]
+            cand[2 + s, h, rows + 1 : rows + 2] = under[s : s + 1, h * chans : (h + 1) * chans]
             cand[2 + s, h, 1 : rows + 1] = own[s, h, :rows]
-    for s in range(2):
-        turned = mm(turn, ecm[s * faces * 8 : (s + 1) * faces * 8, :]).reshape(faces, 8, chans)
-        for h in range(faces):
-            cand[4 + s, h, 0:1] = first[s, h, 0:1]
-            cand[4 + s, h, rows + 1 : rows + 2] = final[s, h, rows - 1 : rows]
-            cand[4 + s, h, 1 : rows + 1] = turned[h, :rows]
-    above[...] = up[...]
-    below[...] = dn[...]
+            mirror[s, h, :rows] = across[i * rows : (i + 1) * rows, lanes(h)]
+            cand[4 + s, h, 0:1] = before[s * groups + i : s * groups + i + 1, lanes(h)]
+            cand[4 + s, h, rows + 1 : rows + 2] = after[s * groups + i : s * groups + i + 1, lanes(h)]
+            cand[4 + s, h, 1 : rows + 1] = turned[i * rows : (i + 1) * rows, lanes(h)]
     at_edge = (stripe == 0) | (stripe == last)
 
     @pl.when(jnp.logical_not(at_edge))
     def _():
         for q in range(2):
             for h in range(faces):
-                i, j = h // fld.per, h % fld.per
-                cand[q, h, 0 : fld.span] = got[
-                    q * last,
-                    i * fld.span : (i + 1) * fld.span,
-                    j * chans : (j + 1) * chans,
-                ]
+                i = h // fld.per
+                cand[q, h, 0 : fld.span] = got[q * last, i * fld.span : (i + 1) * fld.span, lanes(h)]
 
     @pl.when(at_edge)
     def _():
         q = jnp.where(stripe == 0, 0, 1)
         for h in range(faces):
-            pair[0, h] = jnp.where(q == 0, x[h, 0].astype(F32), dn[h].astype(F32)).astype(BF)
-            pair[1, h] = jnp.where(q == 0, up[h].astype(F32), x[h, rows - 1].astype(F32)).astype(BF)
+            pair[0, h] = jnp.where(q == 0, x[h, 0].astype(F32), below[h].astype(F32)).astype(BF)
+            pair[1, h] = jnp.where(q == 0, above[h].astype(F32), x[h, rows - 1].astype(F32)).astype(BF)
         place = stripe * rows - 1 + prow
         inside = (place >= 0) & (place < side)
         for s in range(2):
@@ -350,7 +376,12 @@
                 want = jnp.where(tab[4 * h + s, 1] == 1, side - 1 - place, place)
                 window = ((pcol == want) & inside).astype(F32).astype(BF)
                 cand[s, h] = mm_nt(window, pair[s, h])
-        for i in range(fld.groups):
+        for g in range(faces):
+            p = tab[4 * g + q, 0]
+            at = (g // fld.per) * fld.span + 1
+            piece = mirror[jnp.maximum((p & 3) - 2, 0), p >> 2]
+            got[last - stripe, at : at + rows, lanes(g)] = piece[:rows]
+        for i in range(groups):
             lined = jnp.concatenate(
                 [got[d, i * fld.span + 1 : i * fld.span + 1 + rows, :] for d in range(tiles)], axis=0
             )
@@ -358,7 +389,7 @@
             for j in range(fld.per):
                 g = i * fld.per + j
                 p = tab[4 * g + q, 0]
-                kind, h = p % 4, p // 4
+                kind, h = p & 3, p >> 2
                 near = pair[jnp.minimum(kind, 1), h].astype(F32)
                 far = lined[j * chans : (j + 1) * chans]
                 cells = jnp.where(kind < 2, near, far).astype(BF)
@@ -380,7 +411,7 @@
     for s in range(2):
         for g in range(faces):
             p = tab[4 * g + 2 + s, 0]
-            kind, h = p % 4, p // 4
+            kind, h = p & 3, p >> 2
             which = jnp.where((kind >= 2) & (tab[4 * g + 2 + s, 1] == 1), kind + 2, kind)
             cols[s, g * GROUP : (g + 1) * GROUP] = jnp.where(live, cand[which, h], 0.0)
 
@@ -437,20 +468,18 @@
             x_out[f, r] = lines[r]
         top[f] = lines[0]
         bot[f] = lines[-1]
-        edges = edge_columns(fld, lines)
-        cols[0, f] = edges[:8]
-        cols[1, f] = edges[8:]
+        keep_columns(fld, lines, f, cols)
         return carry
 
     lax.fori_loop(0, fld.faces, one_face, 0)
-    pack_sends(fld, stripe, tab, top, bot, ec_out, send_out, cols, stage, strip)
-
-
-def level_kernel(fld, out_fld, stripe_ref, tab, x, up, dn, ec, ecm, ecf, ecl, recv, weight, side_weight, *refs):
+    pack_sends(fld, stripe, tab, top, bot, 0, ec_out, send_out, cols, stage, strip)
+
+
+def level_kernel(fld, out_fld, off, stripe_ref, tab, x, up, dn, ec, recv, weight, side_weight, *refs):
     outs, sends, halos = refs[:5], refs[5:8], refs[8:]
     x_out, top, bot, ec_out, send_out = outs
     stripe = stripe_ref[0]
-    gather_halos(fld, stripe, tab, x, up, dn, ec, ecm, ecf, ecl, recv, *halos)
+    gather_halos(fld, stripe, tab, x, up, dn, off, ec, recv, *halos)
     _, cols, above, below = halos[:4]
     terms = column_terms(side_weight, [cols[0].astype(BF), cols[1].astype(BF)], out_fld.chans)
 
@@ -466,23 +495,21 @@
             made.append(cells)
         top[f] = made[0]
         bot[f] = made[-1]
-        edges = edge_columns(out_fld, made)
-        sends[0][0, f] = edges[:8]
-        sends[0][1, f] = edges[8:]
+        keep_columns(out_fld, made, f, sends[0])
         return carry
 
     lax.fori_loop(0, fld.faces, one_face, 0)
-    pack_sends(out_fld, stripe, tab, top, bot, ec_out, send_out, *sends)
-
-
-def encode_kernel(fld, out_fld, low, stripe_ref, tab, x, up, dn, ec, ecm, ecf, ecl, recv, weight, side_weight, pool, *refs):
-    outs, low_outs, sends, low_sends, halos = refs[:5], refs[5:10], refs[10:13], refs[13:16], refs[16:]
-    x_out, top, bot, ec_out, send_out = outs
-    y_out, low_top, low_bot, low_ec, low_send = low_outs
+    pack_sends(out_fld, stripe, tab, top, bot, 0, ec_out, send_out, *sends)
+
+
+def encode_kernel(fld, out_fld, low, stripe_ref, tab, x, up, dn, ec, recv, weight, side_weight, pool, *refs):
+    outs, sends, low_sends, halos = refs[:8], refs[8:11], refs[11:14], refs[14:]
+    x_out, y_out, top, bot, ec_out, send_out, low_ec, low_send = outs
     stripe = stripe_ref[0]
-    gather_halos(fld, stripe, tab, x, up, dn, ec, ecm, ecf, ecl, recv, *halos)
+    gather_halos(fld, stripe, tab, x, up, dn, 0, ec, recv, *halos)
     _, cols, above, below = halos[:4]
     terms = column_terms(side_weight, [cols[0].astype(BF), cols[1].astype(BF)], out_fld.chans)
+    side = fld.side
 
     def one_face(f, carry):
         lines = row_stack(x, above, below, f, fld.rows)
@@ -498,28 +525,24 @@
                 mean = (mm(made[r - 1], pool[...]) + mm(cells, pool[...])).astype(BF)
                 y_out[f, r // 2] = mean
                 pooled.append(mean)
-        top[f] = made[0]
-        bot[f] = made[-1]
-        edges = edge_columns(out_fld, made)
-        sends[0][0, f] = edges[:8]
-        sends[0][1, f] = edges[8:]
-        low_top[f] = pooled[0]
-        low_bot[f] = pooled[-1]
-        edges = edge_columns(low, pooled)
-        low_sends[0][0, f] = edges[:8]
-        low_sends[0][1, f] = edges[8:]
+        top[f, :, :side] = made[0]
+        bot[f, :, :side] = made[-1]
+        keep_columns(out_fld, made, f, sends[0])
+        top[f, :, side:] = pooled[0]
+        bot[f, :, side:] = pooled[-1]
+        keep_columns(low, pooled, f, low_sends[0])
         return carry
 
     lax.fori_loop(0, fld.faces, one_face, 0)
-    pack_sends(low, stripe, tab, low_top, low_bot, low_ec, low_send, *low_sends)
-    pack_sends(out_fld, stripe, tab, top, bot, ec_out, send_out, *sends)
-
-
-def decode_kernel(fld, low, out_ch, vars_out, stripe_ref, tab, x, up, dn, ec, ecm, ecf, ecl, recv, y, yup, ydn, yec, yecm, yecf, yecl, yrecv, weight, side_weight, spread, head, atmos, land, row_key, col_key, pred_out, flux_out, *refs):
-    halos, low_halos, flux = refs[:6], refs[6:12], refs[12]
+    pack_sends(low, stripe, tab, top, bot, side, low_ec, low_send, *low_sends)
+    pack_sends(out_fld, stripe, tab, top, bot, 0, ec_out, send_out, *sends)
+
+
+def decode_kernel(fld, low, out_ch, vars_out, stripe_ref, tab, x, up, dn, ec, recv, y, yup, ydn, yec, yrecv, weight, side_weight, spread, head, atmos, land, row_key, col_key, pred_out, flux_out, *refs):
+    halos, low_halos, flux = refs[:7], refs[7:14], refs[14]
     stripe = stripe_ref[0]
-    gather_halos(low, stripe, tab, y, yup, ydn, yec, yecm, yecf, yecl, yrecv, *low_halos)
-    gather_halos(fld, stripe, tab, x, up, dn, ec, ecm, ecf, ecl, recv, *halos)
+    gather_halos(low, stripe, tab, y, yup, ydn, 0, yec, yrecv, *low_halos)
+    gather_halos(fld, stripe, tab, x, up, dn, 0, ec, recv, *halos)
     _, cols, above, below = halos[:4]
     _, low_cols, low_above, low_below = low_halos[:4]
     size = GROUP * GROUP
@@ -606,21 +629,15 @@
     )(*ins)
 
 
-def exchange(fld, top, bot, ec, send):
-    tiles = fld.tiles
-
-    def move(values, to):
-        return lax.ppermute(values, "tile", [(i, to(i) % tiles) for i in range(tiles)])
-
-    return (
-        move(bot, lambda i: i + 1),
-        move(top, lambda i: i - 1),
-        ec,
-        move(ec, lambda i: tiles - 1 - i),
-        move(ec, lambda i: tiles - i),
-        move(ec, lambda i: tiles - 2 - i),
-        lax.all_to_all(send, "tile", split_axis=0, concat_axis=0, tiled=True),
-    )
+def swap_rows(top, bot):
+    tiles = lax.axis_size("tile")
+    ring = [(i, (i + 1) % tiles) for i in range(tiles)]
+    up = lax.ppermute(bot, "tile", ring)
+    return up, lax.ppermute(top, "tile", [(j, i) for i, j in ring])
+
+
+def swap_chunks(chunks):
+    return lax.all_to_all(chunks, "tile", split_axis=0, concat_axis=0, tiled=True)
 
 
 def packed_weight(weight, chans):
@@ -662,52 +679,51 @@
     perm, pool = jnp.asarray(perm, BF), jnp.asarray(0.25 * spread.T, BF)
     spread = jnp.asarray(spread, BF)
 
-    x0, *edges = call(
+    x0, top, bot, ec, send = call(
         functools.partial(prep_kernel, entry),
-        [entry.main()] + entry.outs(),
+        [entry.main()] + entry.edges() + entry.sends(),
         (stripe, seam_table, atmos_state, perm),
         entry.send_scratch(),
         2 * cells * in_ch * in_ch * rows,
         smem=2,
         name="prep",
     )
-    moved = exchange(entry, *edges)
-    body, sides = packed_weight(conv_input, in_ch)
-    x1, *edges = call(
-        functools.partial(level_kernel, entry, full),
-        [full.main()] + full.outs(),
-        (stripe, seam_table, x0) + moved + (body, sides),
+    got = swap_chunks(send)
+    up, dn = swap_rows(top, bot)
+    x1, top, bot, ec, send = call(
+        functools.partial(level_kernel, entry, full, 0),
+        [full.main()] + full.edges() + full.sends(),
+        (stripe, seam_table, x0, up, dn, ec, got) + packed_weight(conv_input, in_ch),
         full.send_scratch() + entry.halo_scratch(),
         2 * cells * 9 * in_ch * width,
         smem=2,
         name="conv_in",
     )
-    moved = exchange(full, *edges)
-    body, sides = packed_weight(conv_encode, width)
-    made = call(
+    got = swap_chunks(send)
+    up, dn = swap_rows(top, bot)
+    x2, y0, top, bot, ec, send, low_ec, low_send = call(
         functools.partial(encode_kernel, full, full, low),
-        [full.main()] + full.outs() + [low.main()] + low.outs(),
-        (stripe, seam_table, x1) + moved + (body, sides, pool),
+        [full.main(), low.main()] + full.edges(side // 2) + full.sends() + low.sends(),
+        (stripe, seam_table, x1, up, dn, ec, got) + packed_weight(conv_encode, width) + (pool,),
         full.send_scratch() + low.send_scratch() + full.halo_scratch(),
         2 * cells * 9 * width * width,
         smem=2,
         name="encode",
     )
-    x2, *edges = made[:5]
-    y0, *low_edges = made[5:]
-    low_moved = exchange(low, *low_edges)
-    moved = exchange(full, *edges)
-    body, sides = packed_weight(conv_coarse, width)
-    y1, *low_edges = call(
-        functools.partial(level_kernel, low, low),
-        [low.main()] + low.outs(),
-        (stripe, seam_table, y0) + low_moved + (body, sides),
+    low_got = swap_chunks(low_send)
+    up, dn = swap_rows(top, bot)
+    y1, low_top, low_bot, low_ec, low_send = call(
+        functools.partial(level_kernel, low, low, side),
+        [low.main()] + low.edges() + low.sends(),
+        (stripe, seam_table, y0, up, dn, low_ec, low_got) + packed_weight(conv_coarse, width),
         low.send_scratch() + low.halo_scratch(),
         2 * cells * 9 * width * width // 4,
         smem=2,
         name="coarse",
     )
-    low_moved = exchange(low, *low_edges)
+    got = swap_chunks(send)
+    low_got = swap_chunks(low_send)
+    low_up, low_dn = swap_rows(low_top, low_bot)
 
     taps = conv_decode.shape[0]
     split = conv_decode.reshape(taps, width, taps, 2, width)
@@ -737,15 +753,12 @@
             jax.ShapeDtypeStruct((OUT_VARS, faces, rows, side), BF),
             jax.ShapeDtypeStruct((tiles, flux_ch * cap, side), BF),
         ],
-        (stripe, seam_table, x2)
-        + moved
-        + (y1,)
-        + low_moved
+        (stripe, seam_table, x2, up, dn, ec, got, y1, low_up, low_dn, low_ec, low_got)
         + (body, sides, spread, head, atmos_state, land_sea, row_key, col_key),
         full.halo_scratch() + low.halo_scratch() + [pltpu.VMEM((flux_ch, faces, rows, side), F32)],
         2 * cells * 18 * width * width,
         smem=2,
-        specs={22: pl.BlockSpec((OUT_VARS, faces, rows, side), lambda i: (0, 0, 0, 0))},
+        specs={16: pl.BlockSpec((OUT_VARS, faces, rows, side), lambda i: (0, 0, 0, 0))},
         name="decode",
     )
     arrived = lax.all_to_all(outgoing, "tile", split_axis=0, concat_axis=0, tiled=True)

time: 270 us -> 250 us (0.926)
  starting transfers between devices: 104 us -> 41.4 us
  waiting for transfers between devices: 41.1 us -> 64.1 us
  blocking collectives: 0 us -> 16.6 us
  Pallas kernels: 98.1 us -> 102 us
    ppermute x25 -> x8, starting transfers between devices: 77.7 us -> 21.6 us  [the longest x4 20.7 us: swap_rows(): return (up, lax.ppermute(top, 'tile', [(j, i) for i, j in ring]))]
    ppermute x25 -> x8, waiting for transfers between devices: 12.1 us -> 46.2 us  [the longest x4 46.2 us: swap_rows(): up = lax.ppermute(bot, 'tile', ring)]
    all_to_all x0 -> x1, blocking collectives: none -> 16.6 us  [swap_chunks(): lax.all_to_all(chunks, 'tile', split_axis=0, concat_axis=0, tiled=True)]
    all_to_all x5 -> x4, waiting for transfers between devices: 13.4 us -> 2.23 us  [swap_chunks(): lax.all_to_all(chunks, 'tile', split_axis=0, concat_axis=0, tiled=True)]
    all_to_all x5 -> x4, starting transfers between devices: 21.6 us -> 14.6 us  [swap_chunks(): lax.all_to_all(chunks, 'tile', split_axis=0, concat_axis=0, tiled=True)]
    pallas_call x7, Pallas kernels: 98.1 us -> 102 us  [call(): pl.pallas_call(kernel, out_shape=outs, **grid, in_specs=in_specs, out_spe...]
    unnamed x87 -> x57, local copies, waits for them, and re-layouts: 8.42 us -> 8.07 us
  transfers between devices with their start and end apart: 32 -> 14, of which waited for: 9 -> 10; matrix products, arithmetic and copies ran while one was open for 6% -> 7% of each run, Pallas kernels for 5% -> 0%
where the time goes in v1:
time: 250 us; the launch traced here: 249 us
  Pallas kernels  102 us (41%)
  waiting for transfers between devices  64.1 us (26%)
  starting transfers between devices  41.4 us (17%)
  local copies, waits for them, and re-layouts  21 us (8%)
  blocking collectives  16.6 us (7%)
    pallas_call x7, Pallas kernels, call(): pl.pallas_call(kernel, out_shape=outs, **grid, in_specs=in_specs, out_spe...  102 us
    ppermute x4, waiting for transfers between devices, swap_rows(): up = lax.ppermute(bot, 'tile', ring)  46.2 us
    ppermute x4, starting transfers between devices, swap_rows(): return (up, lax.ppermute(top, 'tile', [(j, i) for i, j in ring]))  20.7 us
    all_to_all x1, blocking collectives, swap_chunks(): lax.all_to_all(chunks, 'tile', split_axis=0, concat_axis=0, tiled=True)  16.6 us
    all_to_all x4, starting transfers between devices, swap_chunks(): lax.all_to_all(chunks, 'tile', split_axis=0, concat_axis=0, tiled=True)  14.6 us
    all_to_all x1, waiting for transfers between devices, on_one_group(): lax.all_to_all(outgoing, 'tile', split_axis=0, concat_axis=0, tiled=True)  10.2 us
    unnamed x57, local copies, waits for them, and re-layouts  8.07 us
    all_to_all x1, waiting for transfers between devices, on_one_group(): lax.all_to_all(back, 'tile', split_axis=0, concat_axis=0, tiled=True)  5.43 us
  transfers between devices with their start and end apart: 14, of which 10 were waited for; matrix products, arithmetic and copies ran while one was open for 7% of the time, Pallas kernels for 0%

profile of v1, /device:TPU:0, one launch (start us, length us, event | category | flops | bytes accessed | tf_op | source)
XLA Modules:
  0.0 249.0 jit_solution(15551196411883941142)
XLA Ops:
  0.6 1.4 copy.197.tab
  2.0 8.7 %prep.1 = (bf16[12,8,32,256]{3,2,1,0:T(8,128)(2,1)}, bf16[12,32,256]{2,1,0:T(8,128)(2,1)}, bf16[12,32,256]{2,1,0:T(8,128)(2,1)}, bf16[192,32]{1,0:T(8,128)(2,1)}, bf16[32,48,128]{2,1,0:T(8,128)(2,1)}) custom-call(s32[1]{0:T(128)} %bitcast.stripe_ref, s32[48,2]{1,0:T(8,128)} %copy.197.tab, bf16[32,12,8,256]{3,2,1,0:T(8,128)(2,1)} %atmos.3, ...), custom_call_target="tpu_custom_call" | custom-call | flops 402653184 | bytes 4075908 | tf_op jit(solution)/shard_map/prep/pallas_call | solution.py:618
  10.7 6.8 %all-to-all-start = ((bf16[32,48,128]{2,1,0:T(8,128)(2,1)}), bf16[32,48,128]{2,1,0:T(8,128)(2,1)S(1)}, u32[]{:S(2)}, u32[]{:S(2)}) async-start(bf16[32,48,128]{2,1,0:T(8,128)(2,1)} %get-tuple-element.33), calls=%async_computation | async-start | bytes 786432 | tf_op jit(solution)/shard_map/all_to_all | solution.py:640
  17.5 0.3 collective-permute-start
  17.8 5.1 %collective-permute-start.1 = (bf16[12,32,256]{2,1,0:T(8,128)(2,1)}, bf16[12,32,256]{2,1,0:T(8,128)(2,1)S(1)}, u32[]{:S(2)}, u32[]{:S(2)}) collective-permute-start(bf16[12,32,256]{2,1,0:T(8,128)(2,1)} %get-tuple-element.31), channel_id=1, source_target_pairs={{1,0},{2,1},{3,2},{4,3},{5,4},{6,5},{7,6},{8,7},{9,8},{10,9},{11,1... | collective-permute-start | bytes 589832 | tf_op jit(solution)/shard_map/ppermute | solution.py:636
  22.9 0.9 copy.177
  24.1 0.7 copy.183.side_weight
  25.0 0.7 copy.182.weight
  25.7 6.8 %collective-permute-done.up = bf16[12,32,256]{2,1,0:T(8,128)(2,1)S(1)} collective-permute-done((bf16[12,32,256]{2,1,0:T(8,128)(2,1)}, bf16[12,32,256]{2,1,0:T(8,128)(2,1)S(1)}, u32[]{:S(2)}, u32[]{:S(2)}) %collective-permute-start) | collective-permute-done | bytes 196640 | tf_op jit(solution)/shard_map/ppermute | solution.py:635
  32.5 0.3 all-to-all-done.recv
  32.8 0.4 copy-done.23
  33.2 0.3 copy-done.8
  33.5 17.2 %conv_in.1 = (bf16[12,8,64,256]{3,2,1,0:T(8,128)(2,1)}, bf16[12,64,256]{2,1,0:T(8,128)(2,1)}, bf16[12,64,256]{2,1,0:T(8,128)(2,1)}, bf16[192,64]{1,0:T(8,128)(2,1)}, bf16[32,96,128]{2,1,0:T(8,128)(2,1)}) custom-call(s32[1]{0:T(128)} %bitcast.stripe_ref, s32[48,2]{1,0:T(8,128)} %copy.197.tab, bf16[12,8,32,256]{3,2,1,0:T(8,128)(2,1)} %get-tuple-element.29.x, ...), custom_call_target="tpu_custom_call" | custom-call | flops 905969664 | bytes 7176580 | tf_op jit(solution)/shard_map/conv_in/pallas_call | solution.py:618
  50.8 2.6 %all-to-all-start.1 = ((bf16[32,96,128]{2,1,0:T(8,128)(2,1)}), bf16[32,96,128]{2,1,0:T(8,128)(2,1)S(1)}, u32[]{:S(2)}, u32[]{:S(2)}) async-start(bf16[32,96,128]{2,1,0:T(8,128)(2,1)} %get-tuple-element.38), calls=%async_computation.1 | async-start | bytes 1572864 | tf_op jit(solution)/shard_map/all_to_all | solution.py:640
  53.4 0.2 collective-permute-start.2
  53.6 5.2 %collective-permute-start.3 = (bf16[12,64,256]{2,1,0:T(8,128)(2,1)}, bf16[12,64,256]{2,1,0:T(8,128)(2,1)S(1)}, u32[]{:S(2)}, u32[]{:S(2)}) collective-permute-start(bf16[12,64,256]{2,1,0:T(8,128)(2,1)} %get-tuple-element.36), channel_id=1, source_target_pairs={{1,0},{2,1},{3,2},{4,3},{5,4},{6,5},{7,6},{8,7},{9,8},{10,9},{11,1... | collective-permute-start | bytes 1179656 | tf_op jit(solution)/shard_map/ppermute | solution.py:636
  58.8 0.2 copy.184
  59.2 0.2 copy.185
  59.4 0.8 reshape.149.weight
  60.2 0.6 pad_maximum_fusion.1.side_weight
  60.8 16.3 %collective-permute-done.2.up = bf16[12,64,256]{2,1,0:T(8,128)(2,1)S(1)} collective-permute-done((bf16[12,64,256]{2,1,0:T(8,128)(2,1)}, bf16[12,64,256]{2,1,0:T(8,128)(2,1)S(1)}, u32[]{:S(2)}, u32[]{:S(2)}) %collective-permute-start.2) | collective-permute-done | bytes 393248 | tf_op jit(solution)/shard_map/ppermute | solution.py:635
  77.1 0.9 all-to-all-done.1.recv
  78.0 1.0 copy-done.4
  78.9 28.1 %encode.1 = (bf16[12,8,64,256]{3,2,1,0:T(8,128)(2,1)}, bf16[12,4,64,128]{3,2,1,0:T(8,128)(2,1)}, bf16[12,64,384]{2,1,0:T(8,128)(2,1)}, bf16[12,64,384]{2,1,0:T(8...) custom-call(s32[1]{0:T(128)} %bitcast.stripe_ref, ...), custom_call_target="tpu_custom_call" | custom-call | flops 1811939328 | bytes 11272580 | tf_op jit(solution)/shard_map/encode/pallas_call | solution.py:618
  107.0 2.6 %all-to-all-start.3 = ((bf16[32,48,128]{2,1,0:T(8,128)(2,1)}), bf16[32,48,128]{2,1,0:T(8,128)(2,1)S(1)}, u32[]{:S(2)}, u32[]{:S(2)}) async-start(bf16[32,48,128]{2,1,0:T(8,128)(2,1)} %get-tuple-element.46), calls=%async_computation.3 | async-start | bytes 786432 | tf_op jit(solution)/shard_map/all_to_all | solution.py:640
  109.6 0.2 collective-permute-start.4
  109.8 5.2 %collective-permute-start.5 = (bf16[12,64,384]{2,1,0:T(8,128)(2,1)}, bf16[12,64,384]{2,1,0:T(8,128)(2,1)S(1)}, u32[]{:S(2)}, u32[]{:S(2)}) collective-permute-start(bf16[12,64,384]{2,1,0:T(8,128)(2,1)} %get-tuple-element.41), channel_id=1, source_target_pairs={{1,0},{2,1},{3,2},{4,3},{5,4},{6,5},{7,6},{8,7},{9,8},{10,9},{11,1... | collective-permute-start | bytes 1769480 | tf_op jit(solution)/shard_map/ppermute | solution.py:636
  115.0 0.2 copy.189
  115.5 0.2 copy.190
  115.6 0.8 reshape.151.weight
  116.5 0.6 pad_maximum_fusion.2.side_weight
  117.1 11.8 %collective-permute-done.4.up = bf16[12,64,384]{2,1,0:T(8,128)(2,1)S(1)} collective-permute-done((bf16[12,64,384]{2,1,0:T(8,128)(2,1)}, bf16[12,64,384]{2,1,0:T(8,128)(2,1)S(1)}, u32[]{:S(2)}, u32[]{:S(2)}) %collective-permute-start.4) | collective-permute-done | bytes 589856 | tf_op jit(solution)/shard_map/ppermute | solution.py:635
  128.9 0.2 all-to-all-done.3.recv
  129.1 0.6 copy-done.5
  129.7 0.2 copy-done.6
  130.0 13.0 %coarse.1 = (bf16[12,4,64,128]{3,2,1,0:T(8,128)(2,1)}, bf16[12,64,128]{2,1,0:T(8,128)(2,1)}, bf16[12,64,128]{2,1,0:T(8,128)(2,1)}, bf16[192,64]{1,0:T(8,128)(2,1)}, bf16[32,48,128]{2,1,0:T(8,128)(2,1)}) custom-call(s32[1]{0:T(128)} %bitcast.stripe_ref, s32[48,2]{1,0:T(8,128)} %copy.197.tab, bf16[12,4,64,128]{3,2,1,0:T(8,128)(2,1)} %get-tuple-element.44.x, ...), custom_call_target="tpu_custom_call" | custom-call | flops 452984832 | bytes 4104580 | tf_op jit(solution)/shard_map/coarse/pallas_call | solution.py:618
  143.0 16.6 %all_to_all.35.yrecv = bf16[32,48,128]{2,1,0:T(8,128)(2,1)} all-to-all(bf16[32,48,128]{2,1,0:T(8,128)(2,1)} %get-tuple-element.51), channel_id=1, replica_groups=mesh['face'=1,'tile'=32] {'tile'}, dimensions={0} | all-to-all | bytes 786432 | tf_op jit(solution)/shard_map/all_to_all | solution.py:640
  159.6 2.6 %all-to-all-start.2 = ((bf16[32,96,128]{2,1,0:T(8,128)(2,1)}), bf16[32,96,128]{2,1,0:T(8,128)(2,1)S(1)}, u32[]{:S(2)}, u32[]{:S(2)}) async-start(bf16[32,96,128]{2,1,0:T(8,128)(2,1)} %get-tuple-element.43), calls=%async_computation.2 | async-start | bytes 1572864 | tf_op jit(solution)/shard_map/all_to_all | solution.py:640
  162.3 0.2 reshape.152
  162.5 0.2 convert_reduce_fusion
  163.0 0.2 collective-permute-start.6
  163.2 5.2 %collective-permute-start.7 = (bf16[12,64,128]{2,1,0:T(8,128)(2,1)S(1)}, bf16[12,64,128]{2,1,0:T(8,128)(2,1)S(1)}, u32[]{:S(2)}, u32[]{:S(2)}) collective-permute-start(bf16[12,64,128]{2,1,0:T(8,128)(2,1)S(1)} %copy-done.19), channel_id=1, source_target_pairs={{1,0},{2,1},{3,2},{4,3},{5,4},{6,5},{7,6},{8,7},{9,8},{10,9},{11,1... | collective-permute-start | bytes 589832 | tf_op jit(solution)/shard_map/ppermute | solution.py:636
  168.4 0.4 copy.211
  169.3 1.0 reshape.153.weight
  170.3 0.7 add.47.col_key
  171.0 0.8 mul.112.head
  171.8 0.6 pad_maximum_fusion.3.side_weight
  172.4 11.4 %collective-permute-done.6.yup = bf16[12,64,128]{2,1,0:T(8,128)(2,1)S(1)} collective-permute-done((bf16[12,64,128]{2,1,0:T(8,128)(2,1)S(1)}, bf16[12,64,128]{2,1,0:T(8,128)(2,1)S(1)}, u32[]{:S(2)}, u32[]{:S(2)}) %collective-permute-start.6) | collective-permute-done | bytes 196640 | tf_op jit(solution)/shard_map/ppermute | solution.py:635
  183.9 0.8 all-to-all-done.2.recv
  184.7 0.9 copy-done.3
  185.6 22.4 %decode.1 = (bf16[8,12,8,256]{3,2,1,0:T(8,128)(2,1)}, bf16[32,24,256]{2,1,0:T(8,128)(2,1)}) custom-call(s32[1]{0:T(128)} %bitcast.stripe_ref, s32[48,2]{1,0:T(8,128)} %copy.197.tab, bf16[12,8,64,256]{3,2,1,0:T(8,128)(2,1)} %get-tuple-element.39.x, bf16[12,64,384]{2,1,0:T(8,128)(2,1)} %copy-done.5, bf16[12,64,384]{2,1,0:T(8,128)(2,1)} %copy-done.6, ...), custom_call_target="tpu_custom_call" | custom-call | flops 3623878656 | bytes 9606020 | tf_op jit(solution)/shard_map/decode/pallas_call | solution.py:618
  207.9 2.6 %all-to-all-start.5 = ((bf16[32,24,256]{2,1,0:T(8,128)(2,1)}), bf16[32,24,256]{2,1,0:T(8,128)(2,1)S(1)}, u32[]{:S(2)}, u32[]{:S(2)}) async-start(bf16[32,24,256]{2,1,0:T(8,128)(2,1)} %get-tuple-element.52), calls=%async_computation.5 | async-start | bytes 786432 | tf_op jit(solution)/shard_map/all_to_all | solution.py:764
  211.9 0.8 concatenate.8.into
  212.7 0.8 pad_bitcast_fusion.state
  213.5 10.2 %all-to-all-done.5.recv = bf16[32,24,256]{2,1,0:T(8,128)(2,1)S(1)} async-done(((bf16[32,24,256]{2,1,0:T(8,128)(2,1)}), bf16[32,24,256]{2,1,0:T(8,128)(2,1)S(1)}, u32[]{:S(2)}, u32[]{:S(2)}) %all-to-all-start.5) | async-done | bytes 393248 | tf_op jit(solution)/shard_map/all_to_all | solution.py:764
  223.7 0.8 broadcast_in_dim.8.out_weight
  224.5 11.2 %ocean.1 = (f32[32,8,256]{2,1,0:T(8,128)}, bf16[32,8,256]{2,1,0:T(8,128)(2,1)}) custom-call(bf16[32,24,256]{2,1,0:T(8,128)(2,1)} %copy-done, f32[32,16,256]{2,1,0:T(8,128)} %pad_bitcast_fusion.state, bf16[384,112]{1,0:T(8,128)(2,1)} %concatenate.8.into, f32[384,128]{1,0:T(8,128)} %broadcast_in_dim.8.out_weight), custom_call_target="tpu_custom_call" | custom-call | flops 50331648 | bytes 1593344 | tf_op jit(solution)/shard_map/ocean/pallas_call | solution.py:618
  235.7 2.6 %all-to-all-start.6 = ((bf16[32,8,256]{2,1,0:T(8,128)(2,1)}), bf16[32,8,256]{2,1,0:T(8,128)(2,1)S(1)}, u32[]{:S(2)}, u32[]{:S(2)}) async-start(bf16[32,8,256]{2,1,0:T(8,128)(2,1)} %get-tuple-element.53), calls=%async_computation.6 | async-start | bytes 262144 | tf_op jit(solution)/shard_map/all_to_all | solution.py:795
  238.3 0.7 copy.204.key
  239.0 1.0 stack.48
  240.0 1.1 copy.206
  241.1 5.4 %all-to-all-done.6.back = bf16[32,8,256]{2,1,0:T(8,128)(2,1)S(1)} async-done(((bf16[32,8,256]{2,1,0:T(8,128)(2,1)}), bf16[32,8,256]{2,1,0:T(8,128)(2,1)S(1)}, u32[]{:S(2)}, u32[]{:S(2)}) %all-to-all-start.6) | async-done | bytes 131104 | tf_op jit(solution)/shard_map/all_to_all | solution.py:795
  246.5 0.7 copy-done.7
  247.2 1.8 surface.1
  (95 shorter events, 3.1 us)
Async XLA Ops:
  10.7 22.1 %all-to-all-start = ((bf16[32,48,128]{2,1,0:T(8,128)(2,1)}), bf16[32,48,128]{2,1,0:T(8,128)(2,1)S(1)}, u32[]{:S(2)}, u32[]{:S(2)}) async-start(bf16[32,48,128]{2,1,0:T(8,128)(2,1)} %get-tuple-element.33), calls=%async_computation | async-start | bytes 786432 | tf_op jit(solution)/shard_map/all_to_all | solution.py:640
  17.5 41.3 %copy-start.10 = (bf16[3,64,192]{2,1,0:T(8,128)(2,1)S(1)}, bf16[3,64,192]{2,1,0:T(8,128)(2,1)}, u32[]{:S(2)}) copy-start(bf16[3,64,192]{2,1,0:T(8,128)(2,1)} %param.24) | copy-start | bytes 221188
  17.5 15.0 %collective-permute-start = (bf16[12,32,256]{2,1,0:T(8,128)(2,1)}, bf16[12,32,256]{2,1,0:T(8,128)(2,1)S(1)}, u32[]{:S(2)}, u32[]{:S(2)}) collective-permute-start(bf16[12,32,256]{2,1,0:T(8,128)(2,1)} %get-tuple-element.30), channel_id=1, source_target_pairs={{0,1},{1,2},{2,3},{3,4},{4,5},{5,6},{6,7},{7,8},{8,9},{9,10},{10,1... | collective-permute-start | bytes 589832 | tf_op jit(solution)/shard_map/ppermute | solution.py:635
  17.8 14.7 %collective-permute-start.1 = (bf16[12,32,256]{2,1,0:T(8,128)(2,1)}, bf16[12,32,256]{2,1,0:T(8,128)(2,1)S(1)}, u32[]{:S(2)}, u32[]{:S(2)}) collective-permute-start(bf16[12,32,256]{2,1,0:T(8,128)(2,1)} %get-tuple-element.31), channel_id=1, source_target_pairs={{1,0},{2,1},{3,2},{4,3},{5,4},{6,5},{7,6},{8,7},{9,8},{10,9},{11,1... | collective-permute-start | bytes 589832 | tf_op jit(solution)/shard_map/ppermute | solution.py:636
  32.5 0.7 copy-start.23
  32.5 0.7 copy-start.24
  32.8 0.7 copy-start.8
  50.8 27.2 %all-to-all-start.1 = ((bf16[32,96,128]{2,1,0:T(8,128)(2,1)}), bf16[32,96,128]{2,1,0:T(8,128)(2,1)S(1)}, u32[]{:S(2)}, u32[]{:S(2)}) async-start(bf16[32,96,128]{2,1,0:T(8,128)(2,1)} %get-tuple-element.38), calls=%async_computation.1 | async-start | bytes 1572864 | tf_op jit(solution)/shard_map/all_to_all | solution.py:640
  53.4 23.7 %collective-permute-start.2 = (bf16[12,64,256]{2,1,0:T(8,128)(2,1)}, bf16[12,64,256]{2,1,0:T(8,128)(2,1)S(1)}, u32[]{:S(2)}, u32[]{:S(2)}) collective-permute-start(bf16[12,64,256]{2,1,0:T(8,128)(2,1)} %get-tuple-element.35), channel_id=1, source_target_pairs={{0,1},{1,2},{2,3},{3,4},{4,5},{5,6},{6,7},{7,8},{8,9},{9,10},{10,1... | collective-permute-start | bytes 1179656 | tf_op jit(solution)/shard_map/ppermute | solution.py:635
  53.6 23.5 %collective-permute-start.3 = (bf16[12,64,256]{2,1,0:T(8,128)(2,1)}, bf16[12,64,256]{2,1,0:T(8,128)(2,1)S(1)}, u32[]{:S(2)}, u32[]{:S(2)}) collective-permute-start(bf16[12,64,256]{2,1,0:T(8,128)(2,1)} %get-tuple-element.36), channel_id=1, source_target_pairs={{1,0},{2,1},{3,2},{4,3},{5,4},{6,5},{7,6},{8,7},{9,8},{10,9},{11,1... | collective-permute-start | bytes 1179656 | tf_op jit(solution)/shard_map/ppermute | solution.py:636
  77.1 0.9 copy-start.17
  77.1 0.9 copy-start.18
  78.0 1.0 copy-start.4
  78.9 36.1 %copy-start.11 = (bf16[3,64,192]{2,1,0:T(8,128)(2,1)S(1)}, bf16[3,64,192]{2,1,0:T(8,128)(2,1)}, u32[]{:S(2)}) copy-start(bf16[3,64,192]{2,1,0:T(8,128)(2,1)} %param.25) | copy-start | bytes 221188
  107.0 22.1 %all-to-all-start.3 = ((bf16[32,48,128]{2,1,0:T(8,128)(2,1)}), bf16[32,48,128]{2,1,0:T(8,128)(2,1)S(1)}, u32[]{:S(2)}, u32[]{:S(2)}) async-start(bf16[32,48,128]{2,1,0:T(8,128)(2,1)} %get-tuple-element.46), calls=%async_computation.3 | async-start | bytes 786432 | tf_op jit(solution)/shard_map/all_to_all | solution.py:640
  109.6 19.3 %collective-permute-start.4 = (bf16[12,64,384]{2,1,0:T(8,128)(2,1)}, bf16[12,64,384]{2,1,0:T(8,128)(2,1)S(1)}, u32[]{:S(2)}, u32[]{:S(2)}) collective-permute-start(bf16[12,64,384]{2,1,0:T(8,128)(2,1)} %get-tuple-element.40), channel_id=1, source_target_pairs={{0,1},{1,2},{2,3},{3,4},{4,5},{5,6},{6,7},{7,8},{8,9},{9,10},{10,1... | collective-permute-start | bytes 1769480 | tf_op jit(solution)/shard_map/ppermute | solution.py:635
  109.8 19.1 %collective-permute-start.5 = (bf16[12,64,384]{2,1,0:T(8,128)(2,1)}, bf16[12,64,384]{2,1,0:T(8,128)(2,1)S(1)}, u32[]{:S(2)}, u32[]{:S(2)}) collective-permute-start(bf16[12,64,384]{2,1,0:T(8,128)(2,1)} %get-tuple-element.41), channel_id=1, source_target_pairs={{1,0},{2,1},{3,2},{4,3},{5,4},{6,5},{7,6},{8,7},{9,8},{10,9},{11,1... | collective-permute-start | bytes 1769480 | tf_op jit(solution)/shard_map/ppermute | solution.py:636
  115.2 47.1 %copy-start.9 = (bf16[3,64,384]{2,1,0:T(8,128)(2,1)S(1)}, bf16[3,64,384]{2,1,0:T(8,128)(2,1)}, u32[]{:S(2)}) copy-start(bf16[3,64,384]{2,1,0:T(8,128)(2,1)} %param.26) | copy-start | bytes 442372
  115.4 47.1 %copy-start.12 = (pred[96,96]{1,0:T(32,128)(4,1)S(1)}, pred[96,96]{1,0:T(32,128)(4,1)}, u32[]{:S(2)}) copy-start(pred[96,96]{1,0:T(32,128)(4,1)} %constant.29.clone) | copy-start | bytes 27652
  115.4 47.1 %copy-start.15 = (s32[96,1]{0,1:T(1,128)S(1)}, s32[96,1]{0,1:T(1,128)}, u32[]{:S(2)}) copy-start(s32[96,1]{0,1:T(1,128)} %param.20) | copy-start | bytes 1156
  115.4 47.2 %copy-start.14 = (f32[64,6]{0,1:T(8,128)S(1)}, f32[64,6]{0,1:T(8,128)}, u32[]{:S(2)}) copy-start(f32[64,6]{0,1:T(8,128)} %param.28) | copy-start | bytes 4612
  115.5 47.3 %copy-start.13 = (bf16[12,64]{1,0:T(8,128)(2,1)S(1)}, bf16[12,64]{1,0:T(8,128)(2,1)}, u32[]{:S(2)}) copy-start(bf16[12,64]{1,0:T(8,128)(2,1)} %param.27) | copy-start | bytes 4612
  128.9 0.8 copy-start.5
  128.9 1.0 copy-start.6
  129.1 0.9 copy-start.1
  130.0 38.9 %copy-start.2 = (f32[1,1,192,2,256]{4,3,2,1,0:T(2,128)S(1)}, f32[1,1,192,2,256]{4,3,2,1,0:T(2,128)}, u32[]{:S(2)}) copy-start(f32[1,1,192,2,256]{4,3,2,1,0:T(2,128)} %param.22) | copy-start | bytes 1179652
  143.0 19.9 %copy-start.20 = (bf16[12,64,128]{2,1,0:T(8,128)(2,1)S(1)}, bf16[12,64,128]{2,1,0:T(8,128)(2,1)}, u32[]{:S(2)}) copy-start(bf16[12,64,128]{2,1,0:T(8,128)(2,1)} %get-tuple-element.48) | copy-start | bytes 589828
  143.0 20.2 %copy-start.19 = (bf16[12,64,128]{2,1,0:T(8,128)(2,1)S(1)}, bf16[12,64,128]{2,1,0:T(8,128)(2,1)}, u32[]{:S(2)}) copy-start(bf16[12,64,128]{2,1,0:T(8,128)(2,1)} %get-tuple-element.49) | copy-start | bytes 589828
  159.6 25.0 %all-to-all-start.2 = ((bf16[32,96,128]{2,1,0:T(8,128)(2,1)}), bf16[32,96,128]{2,1,0:T(8,128)(2,1)S(1)}, u32[]{:S(2)}, u32[]{:S(2)}) async-start(bf16[32,96,128]{2,1,0:T(8,128)(2,1)} %get-tuple-element.43), calls=%async_computation.2 | async-start | bytes 1572864 | tf_op jit(solution)/shard_map/all_to_all | solution.py:640
  163.0 20.9 %collective-permute-start.6 = (bf16[12,64,128]{2,1,0:T(8,128)(2,1)S(1)}, bf16[12,64,128]{2,1,0:T(8,128)(2,1)S(1)}, u32[]{:S(2)}, u32[]{:S(2)}) collective-permute-start(bf16[12,64,128]{2,1,0:T(8,128)(2,1)S(1)} %copy-done.20), channel_id=1, source_target_pairs={{0,1},{1,2},{2,3},{3,4},{4,5},{5,6},{6,7},{7,8},{8,9},{9,10},{10,1... | collective-permute-start | bytes 589832 | tf_op jit(solution)/shard_map/ppermute | solution.py:635
  163.2 20.7 %collective-permute-start.7 = (bf16[12,64,128]{2,1,0:T(8,128)(2,1)S(1)}, bf16[12,64,128]{2,1,0:T(8,128)(2,1)S(1)}, u32[]{:S(2)}, u32[]{:S(2)}) collective-permute-start(bf16[12,64,128]{2,1,0:T(8,128)(2,1)S(1)} %copy-done.19), channel_id=1, source_target_pairs={{1,0},{2,1},{3,2},{4,3},{5,4},{6,5},{7,6},{8,7},{9,8},{10,9},{11,1... | collective-permute-start | bytes 589832 | tf_op jit(solution)/shard_map/ppermute | solution.py:636
  183.8 0.8 copy-start.21
  183.8 0.8 copy-start.22
  184.7 0.9 copy-start.3
  185.6 26.2 %copy-start.16 = (f32[64]{0:T(128)S(1)}, f32[64]{0:T(128)}, u32[]{:S(2)}) copy-start(f32[64]{0:T(128)} %param.29) | copy-start | bytes 772
  207.9 15.8 %all-to-all-start.5 = ((bf16[32,24,256]{2,1,0:T(8,128)(2,1)}), bf16[32,24,256]{2,1,0:T(8,128)(2,1)S(1)}, u32[]{:S(2)}, u32[]{:S(2)}) async-start(bf16[32,24,256]{2,1,0:T(8,128)(2,1)} %get-tuple-element.52), calls=%async_computation.5 | async-start | bytes 786432 | tf_op jit(solution)/shard_map/all_to_all | solution.py:764
  223.7 0.8 copy-start
  235.7 10.8 %all-to-all-start.6 = ((bf16[32,8,256]{2,1,0:T(8,128)(2,1)}), bf16[32,8,256]{2,1,0:T(8,128)(2,1)S(1)}, u32[]{:S(2)}, u32[]{:S(2)}) async-start(bf16[32,8,256]{2,1,0:T(8,128)(2,1)} %get-tuple-element.53), calls=%async_computation.6 | async-start | bytes 262144 | tf_op jit(solution)/shard_map/all_to_all | solution.py:795
  246.5 0.7 copy-start.7

commit v2 on v1

--- a/solution.py
+++ b/solution.py
@@ -263,62 +263,70 @@
     return (((row == 0) & (col == 0)) | ((row == 1) & (col == side - 1))).astype(F32).astype(BF)
 
 
-def keep_columns(fld, face_rows, f, cols):
-    picked = mm_nt(end_picker(fld.side), jnp.concatenate(face_rows, axis=0))
-    for s in range(2):
-        for r in range(fld.rows):
-            cols[s, f, r : r + 1] = picked[s : s + 1, r * fld.chans : (r + 1) * fld.chans]
+def column_picker(fld):
+    length = fld.rows * fld.side
+    row, col = iota((16, length), 0), iota((16, length), 1)
+    want = (row & 7) * fld.side + (row >> 3) * (fld.side - 1)
+    return (col == want).astype(F32).astype(BF)
+
+
+def keep_columns(picker, face_rows, f, cols):
+    picked = mm_nt(picker, jnp.concatenate(face_rows, axis=1))
+    cols[0, f] = picked[:8]
+    cols[1, f] = picked[8:]
 
 
 def pack_sends(fld, stripe, tab, top, bot, off, ec_out, send_out, cols, stage, strip):
-    last, rows, chans = fld.tiles - 1, fld.rows, fld.chans
-    ec_out[...] = cols[...].reshape(2 * fld.faces * 8, chans).astype(BF)
-    stage[...] = jnp.zeros_like(stage)
-
-    def lanes(h):
-        return slice((h % fld.per) * chans, (h % fld.per + 1) * chans)
-
+    last, rows, chans, groups, per = fld.tiles - 1, fld.rows, fld.chans, fld.groups, fld.per
+    held = cols[...]
+    ec_out[...] = held.reshape(2 * fld.faces * 8, chans).astype(BF)
+    paired = held.reshape(2, groups, per, 8, chans)
+    packed = jnp.concatenate([paired[:, :, j] for j in range(per)], axis=3)
+    across = packed[:, :, :rows].reshape(2 * groups * rows, LANES)
+    initial = packed[:, :, 0].reshape(2 * groups, LANES)
+    final = packed[:, :, rows - 1].reshape(2 * groups, LANES)
+    pieces = []
     for q in range(2):
         for g in range(fld.faces):
             p = tab[4 * g + q, 0]
-            kind, h = p & 3, p >> 2
-            piece = cols[jnp.maximum(kind - 2, 0), h]
-            at = (g // fld.per) * fld.span + 1
-            stage[q * last, at : at + rows, lanes(g)] = piece[:rows]
+            pieces.append(cols[jnp.maximum((p & 3) - 2, 0), p >> 2][:rows])
+    merged = [jnp.concatenate(pieces[n : n + per], axis=1) for n in range(0, len(pieces), per)]
+    stage[...] = jnp.zeros_like(stage)
+    for q in range(2):
+        for i in range(groups):
+            stage[q * last, i * fld.span + 1 : i * fld.span + 1 + rows, :] = merged[q * groups + i]
+
+    def lanes(h):
+        return slice((h % per) * chans, (h % per + 1) * chans)
 
     @pl.when((stripe == 0) | (stripe == last))
     def _():
         q = jnp.where(stripe == 0, 0, 1)
-        for i in range(fld.groups):
-            strip[...] = jnp.zeros_like(strip)
-            for j in range(fld.per):
-                h = i * fld.per + j
+        for i in range(groups):
+            turned = []
+            for h in range(i * per, (i + 1) * per):
                 upper = top[h, :, off : off + fld.side].astype(F32)
                 lower = bot[h, :, off : off + fld.side].astype(F32)
                 cells = jnp.where(q == 0, upper, lower).astype(BF)
-                turned = mm_nt(flip_matrix(fld.side, tab[4 * h + q, 1]), cells)
-                strip[1 : fld.side + 1, lanes(h)] = turned
-            for d in range(1, last):
-                stage[d, i * fld.span : (i + 1) * fld.span, :] = strip[d * rows : d * rows + fld.span, :]
-
-    for s in range(2):
-        for h in range(fld.faces):
-            at = (s * fld.groups + h // fld.per) * rows
-            stage[last - stripe, at : at + rows, lanes(h)] = cols[s, h, :rows]
+                turned.append(mm_nt(flip_matrix(fld.side, tab[4 * h + q, 1]), cells))
+            strip[0:8] = jnp.zeros((8, LANES), F32)
+            strip[fld.side : fld.side + 8] = jnp.zeros((8, LANES), F32)
+            strip[1 : fld.side + 1, :] = jnp.concatenate(turned, axis=1)
+            for d in range(1, last, 10):
+                here = range(d, min(d + 10, last))
+                taken = [strip[e * rows : e * rows + fld.span, :] for e in here]
+                for e, piece in zip(here, taken):
+                    stage[e, i * fld.span : (i + 1) * fld.span, :] = piece
+
+    stage[last - stripe, : 2 * groups * rows, :] = across
 
     @pl.when(stripe < last)
     def _():
-        for s in range(2):
-            for h in range(fld.faces):
-                at = fld.extra + s * fld.groups + h // fld.per
-                stage[last - 1 - stripe, at : at + 1, lanes(h)] = cols[s, h, rows - 1 : rows]
+        stage[last - 1 - stripe, fld.extra : fld.extra + 2 * groups, :] = final
 
     @pl.when(stripe > 0)
     def _():
-        for s in range(2):
-            for h in range(fld.faces):
-                at = fld.extra + s * fld.groups + h // fld.per
-                stage[last + 1 - stripe, at : at + 1, lanes(h)] = cols[s, h, 0:1]
+        stage[last + 1 - stripe, fld.extra : fld.extra + 2 * groups, :] = initial
 
     send_out[...] = stage[...].astype(BF)
 
@@ -340,6 +348,7 @@
     below[...] = dn[:, :, off : off + side]
     over = mm_nt(end_picker(side), above[...].reshape(faces * chans, side))
     under = mm_nt(end_picker(side), below[...].reshape(faces * chans, side))
+    heads = [got[q * last, : fld.extra, :] for q in range(2)]
     before = got[jnp.minimum(last + 1 - stripe, last), fld.extra : fld.extra + 2 * groups, :]
     after = got[jnp.maximum(last - 1 - stripe, 0), fld.extra : fld.extra + 2 * groups, :]
     for s in range(2):
@@ -361,7 +370,7 @@
         for q in range(2):
             for h in range(faces):
                 i = h // fld.per
-                cand[q, h, 0 : fld.span] = got[q * last, i * fld.span : (i + 1) * fld.span, lanes(h)]
+                cand[q, h, 0 : fld.span] = heads[q][i * fld.span : (i + 1) * fld.span, lanes(h)]
 
     @pl.when(at_edge)
     def _():
@@ -371,16 +380,22 @@
             pair[1, h] = jnp.where(q == 0, above[h].astype(F32), x[h, rows - 1].astype(F32)).astype(BF)
         place = stripe * rows - 1 + prow
         inside = (place >= 0) & (place < side)
+        windows = []
         for s in range(2):
             for h in range(faces):
                 want = jnp.where(tab[4 * h + s, 1] == 1, side - 1 - place, place)
                 window = ((pcol == want) & inside).astype(F32).astype(BF)
-                cand[s, h] = mm_nt(window, pair[s, h])
+                windows.append(mm_nt(window, pair[s, h]))
+        pieces = []
         for g in range(faces):
             p = tab[4 * g + q, 0]
-            at = (g // fld.per) * fld.span + 1
-            piece = mirror[jnp.maximum((p & 3) - 2, 0), p >> 2]
-            got[last - stripe, at : at + rows, lanes(g)] = piece[:rows]
+            pieces.append(mirror[jnp.maximum((p & 3) - 2, 0), p >> 2][:rows])
+        for s in range(2):
+            for h in range(faces):
+                cand[s, h] = windows[s * faces + h]
+        for i in range(groups):
+            merged = jnp.concatenate(pieces[i * fld.per : (i + 1) * fld.per], axis=1)
+            got[last - stripe, i * fld.span + 1 : i * fld.span + 1 + rows, :] = merged
         for i in range(groups):
             lined = jnp.concatenate(
                 [got[d, i * fld.span + 1 : i * fld.span + 1 + rows, :] for d in range(tiles)], axis=0
@@ -403,17 +418,19 @@
                 def _():
                     below[g] = placed
 
-    cols[...] = jnp.zeros_like(cols)
     slot = iota((GROUP, chans), 0)
     live = (slot < fld.span) & jnp.logical_not(
         ((slot == 0) & (stripe == 0)) | ((slot == rows + 1) & (stripe == last))
     )
     for s in range(2):
+        taken = []
         for g in range(faces):
             p = tab[4 * g + 2 + s, 0]
             kind, h = p & 3, p >> 2
             which = jnp.where((kind >= 2) & (tab[4 * g + 2 + s, 1] == 1), kind + 2, kind)
-            cols[s, g * GROUP : (g + 1) * GROUP] = jnp.where(live, cand[which, h], 0.0)
+            taken.append(jnp.where(live, cand[which, h], 0.0))
+        taken.append(jnp.zeros(((GROUP - faces) * GROUP, chans), F32))
+        cols[s] = jnp.concatenate(taken, axis=0)
 
 
 def column_terms(side_weight, cols, out_ch):
@@ -459,6 +476,7 @@
 
 def prep_kernel(fld, stripe_ref, tab, atmos, perm, x_out, top, bot, ec_out, send_out, cols, stage, strip):
     stripe = stripe_ref[0]
+    picker = column_picker(fld)
 
     def one_face(f, carry):
         block = atmos[:, f].astype(F32).reshape(fld.chans * fld.rows, fld.side).astype(BF)
@@ -468,7 +486,7 @@
             x_out[f, r] = lines[r]
         top[f] = lines[0]
         bot[f] = lines[-1]
-        keep_columns(fld, lines, f, cols)
+        keep_columns(picker, lines, f, cols)
         return carry
 
     lax.fori_loop(0, fld.faces, one_face, 0)
@@ -482,6 +500,7 @@
     gather_halos(fld, stripe, tab, x, up, dn, off, ec, recv, *halos)
     _, cols, above, below = halos[:4]
     terms = column_terms(side_weight, [cols[0].astype(BF), cols[1].astype(BF)], out_fld.chans)
+    picker = column_picker(out_fld)
 
     def one_face(f, carry):
         lines = row_stack(x, above, below, f, fld.rows)
@@ -495,7 +514,7 @@
             made.append(cells)
         top[f] = made[0]
         bot[f] = made[-1]
-        keep_columns(out_fld, made, f, sends[0])
+        keep_columns(picker, made, f, sends[0])
         return carry
 
     lax.fori_loop(0, fld.faces, one_face, 0)
@@ -510,6 +529,7 @@
     _, cols, above, below = halos[:4]
     terms = column_terms(side_weight, [cols[0].astype(BF), cols[1].astype(BF)], out_fld.chans)
     side = fld.side
+    picker, low_picker = column_picker(out_fld), column_picker(low)
 
     def one_face(f, carry):
         lines = row_stack(x, above, below, f, fld.rows)
@@ -527,10 +547,10 @@
                 pooled.append(mean)
         top[f, :, :side] = made[0]
         bot[f, :, :side] = made[-1]
-        keep_columns(out_fld, made, f, sends[0])
+        keep_columns(picker, made, f, sends[0])
         top[f, :, side:] = pooled[0]
         bot[f, :, side:] = pooled[-1]
-        keep_columns(low, pooled, f, low_sends[0])
+        keep_columns(low_picker, pooled, f, low_sends[0])
         return carry
 
     lax.fori_loop(0, fld.faces, one_face, 0)
@@ -717,7 +737,7 @@
         [low.main()] + low.edges() + low.sends(),
         (stripe, seam_table, y0, up, dn, low_ec, low_got) + packed_weight(conv_coarse, width),
         low.send_scratch() + low.halo_scratch(),
-        2 * cells * 9 * width * width // 4,
+        10e9,
         smem=2,
         name="coarse",
     )

time: 250 us -> 246 us (0.984)
  Pallas kernels: 102 us -> 98.5 us
    pallas_call x7, Pallas kernels: 102 us -> 98.5 us  [call(): pl.pallas_call(kernel, out_shape=outs, **grid, in_specs=in_specs, out_spe...]
where the time goes in v2:
time: 246 us; the launch traced here: 245 us
  Pallas kernels  98.5 us (40%)
  waiting for transfers between devices  64.1 us (26%)
  starting transfers between devices  41.3 us (17%)
  local copies, waits for them, and re-layouts  21 us (9%)
  blocking collectives  16.6 us (7%)
  other arithmetic  2.48 us (1%)
    pallas_call x7, Pallas kernels, call(): pl.pallas_call(kernel, out_shape=outs, **grid, in_specs=in_specs, out_spe...  98.5 us
    ppermute x4, waiting for transfers between devices, swap_rows(): up = lax.ppermute(bot, 'tile', ring)  46.3 us
    ppermute x4, starting transfers between devices, swap_rows(): return (up, lax.ppermute(top, 'tile', [(j, i) for i, j in ring]))  20.7 us
    all_to_all x1, blocking collectives, swap_chunks(): lax.all_to_all(chunks, 'tile', split_axis=0, concat_axis=0, tiled=True)  16.6 us
    all_to_all x4, starting transfers between devices, swap_chunks(): lax.all_to_all(chunks, 'tile', split_axis=0, concat_axis=0, tiled=True)  14.6 us
    all_to_all x1, waiting for transfers between devices, on_one_group(): lax.all_to_all(outgoing, 'tile', split_axis=0, concat_axis=0, tiled=True)  10.2 us
    unnamed x57, local copies, waits for them, and re-layouts  8.06 us
    all_to_all x1, waiting for transfers between devices, on_one_group(): lax.all_to_all(back, 'tile', split_axis=0, concat_axis=0, tiled=True)  5.43 us
  transfers between devices with their start and end apart: 14, of which 10 were waited for; matrix products, arithmetic and copies ran while one was open for 7% of the time, Pallas kernels for 0%

profile of v2, /device:TPU:0, one launch (start us, length us, event | category | flops | bytes accessed | tf_op | source)
XLA Modules:
  0.0 245.2 jit_solution(14660291726515652503)
XLA Ops:
  0.6 1.4 copy.197.tab
  2.0 7.7 %prep.1 = (bf16[12,8,32,256]{3,2,1,0:T(8,128)(2,1)}, bf16[12,32,256]{2,1,0:T(8,128)(2,1)}, bf16[12,32,256]{2,1,0:T(8,128)(2,1)}, bf16[192,32]{1,0:T(8,128)(2,1)}, bf16[32,48,128]{2,1,0:T(8,128)(2,1)}) custom-call(s32[1]{0:T(128)} %bitcast.stripe_ref, s32[48,2]{1,0:T(8,128)} %copy.197.tab, bf16[32,12,8,256]{3,2,1,0:T(8,128)(2,1)} %atmos.3, ...), custom_call_target="tpu_custom_call" | custom-call | flops 402653184 | bytes 4075908 | tf_op jit(solution)/shard_map/prep/pallas_call | solution.py:638
  9.7 6.7 %all-to-all-start = ((bf16[32,48,128]{2,1,0:T(8,128)(2,1)}), bf16[32,48,128]{2,1,0:T(8,128)(2,1)S(1)}, u32[]{:S(2)}, u32[]{:S(2)}) async-start(bf16[32,48,128]{2,1,0:T(8,128)(2,1)} %get-tuple-element.33), calls=%async_computation | async-start | bytes 786432 | tf_op jit(solution)/shard_map/all_to_all | solution.py:660
  16.5 0.3 collective-permute-start
  16.8 5.1 %collective-permute-start.1 = (bf16[12,32,256]{2,1,0:T(8,128)(2,1)}, bf16[12,32,256]{2,1,0:T(8,128)(2,1)S(1)}, u32[]{:S(2)}, u32[]{:S(2)}) collective-permute-start(bf16[12,32,256]{2,1,0:T(8,128)(2,1)} %get-tuple-element.31), channel_id=1, source_target_pairs={{1,0},{2,1},{3,2},{4,3},{5,4},{6,5},{7,6},{8,7},{9,8},{10,9},{11,1... | collective-permute-start | bytes 589832 | tf_op jit(solution)/shard_map/ppermute | solution.py:656
  21.9 0.9 copy.177
  23.1 0.7 copy.183.side_weight
  24.0 0.7 copy.182.weight
  24.7 6.8 %collective-permute-done.up = bf16[12,32,256]{2,1,0:T(8,128)(2,1)S(1)} collective-permute-done((bf16[12,32,256]{2,1,0:T(8,128)(2,1)}, bf16[12,32,256]{2,1,0:T(8,128)(2,1)S(1)}, u32[]{:S(2)}, u32[]{:S(2)}) %collective-permute-start) | collective-permute-done | bytes 196640 | tf_op jit(solution)/shard_map/ppermute | solution.py:655
  31.5 0.3 all-to-all-done.recv
  31.8 0.4 copy-done.23
  32.2 0.3 copy-done.5
  32.5 16.6 %conv_in.1 = (bf16[12,8,64,256]{3,2,1,0:T(8,128)(2,1)}, bf16[12,64,256]{2,1,0:T(8,128)(2,1)}, bf16[12,64,256]{2,1,0:T(8,128)(2,1)}, bf16[192,64]{1,0:T(8,128)(2,1)}, bf16[32,96,128]{2,1,0:T(8,128)(2,1)}) custom-call(s32[1]{0:T(128)} %bitcast.stripe_ref, s32[48,2]{1,0:T(8,128)} %copy.197.tab, bf16[12,8,32,256]{3,2,1,0:T(8,128)(2,1)} %get-tuple-element.29.x, ...), custom_call_target="tpu_custom_call" | custom-call | flops 905969664 | bytes 7176580 | tf_op jit(solution)/shard_map/conv_in/pallas_call | solution.py:638
  49.1 2.6 %all-to-all-start.1 = ((bf16[32,96,128]{2,1,0:T(8,128)(2,1)}), bf16[32,96,128]{2,1,0:T(8,128)(2,1)S(1)}, u32[]{:S(2)}, u32[]{:S(2)}) async-start(bf16[32,96,128]{2,1,0:T(8,128)(2,1)} %get-tuple-element.38), calls=%async_computation.1 | async-start | bytes 1572864 | tf_op jit(solution)/shard_map/all_to_all | solution.py:660
  51.8 0.2 collective-permute-start.2
  51.9 5.2 %collective-permute-start.3 = (bf16[12,64,256]{2,1,0:T(8,128)(2,1)}, bf16[12,64,256]{2,1,0:T(8,128)(2,1)S(1)}, u32[]{:S(2)}, u32[]{:S(2)}) collective-permute-start(bf16[12,64,256]{2,1,0:T(8,128)(2,1)} %get-tuple-element.36), channel_id=1, source_target_pairs={{1,0},{2,1},{3,2},{4,3},{5,4},{6,5},{7,6},{8,7},{9,8},{10,9},{11,1... | collective-permute-start | bytes 1179656 | tf_op jit(solution)/shard_map/ppermute | solution.py:656
  57.2 0.2 copy.184
  57.6 0.2 copy.185
  57.7 0.8 reshape.149.weight
  58.5 0.6 pad_maximum_fusion.1.side_weight
  59.2 16.3 %collective-permute-done.2.up = bf16[12,64,256]{2,1,0:T(8,128)(2,1)S(1)} collective-permute-done((bf16[12,64,256]{2,1,0:T(8,128)(2,1)}, bf16[12,64,256]{2,1,0:T(8,128)(2,1)S(1)}, u32[]{:S(2)}, u32[]{:S(2)}) %collective-permute-start.2) | collective-permute-done | bytes 393248 | tf_op jit(solution)/shard_map/ppermute | solution.py:655
  75.5 0.9 all-to-all-done.1.recv
  76.4 1.0 copy-done.3
  77.3 26.9 %encode.1 = (bf16[12,8,64,256]{3,2,1,0:T(8,128)(2,1)}, bf16[12,4,64,128]{3,2,1,0:T(8,128)(2,1)}, bf16[12,64,384]{2,1,0:T(8,128)(2,1)}, bf16[12,64,384]{2,1,0:T(8...) custom-call(s32[1]{0:T(128)} %bitcast.stripe_ref, ...), custom_call_target="tpu_custom_call" | custom-call | flops 1811939328 | bytes 11272580 | tf_op jit(solution)/shard_map/encode/pallas_call | solution.py:638
  104.2 2.6 %all-to-all-start.3 = ((bf16[32,48,128]{2,1,0:T(8,128)(2,1)}), bf16[32,48,128]{2,1,0:T(8,128)(2,1)S(1)}, u32[]{:S(2)}, u32[]{:S(2)}) async-start(bf16[32,48,128]{2,1,0:T(8,128)(2,1)} %get-tuple-element.46), calls=%async_computation.3 | async-start | bytes 786432 | tf_op jit(solution)/shard_map/all_to_all | solution.py:660
  106.8 0.2 collective-permute-start.4
  107.0 5.2 %collective-permute-start.5 = (bf16[12,64,384]{2,1,0:T(8,128)(2,1)}, bf16[12,64,384]{2,1,0:T(8,128)(2,1)S(1)}, u32[]{:S(2)}, u32[]{:S(2)}) collective-permute-start(bf16[12,64,384]{2,1,0:T(8,128)(2,1)} %get-tuple-element.41), channel_id=1, source_target_pairs={{1,0},{2,1},{3,2},{4,3},{5,4},{6,5},{7,6},{8,7},{9,8},{10,9},{11,1... | collective-permute-start | bytes 1769480 | tf_op jit(solution)/shard_map/ppermute | solution.py:656
  112.2 0.2 copy.189
  112.6 0.2 copy.190
  112.8 0.8 reshape.151.weight
  113.6 0.6 pad_maximum_fusion.2.side_weight
  114.2 11.8 %collective-permute-done.4.up = bf16[12,64,384]{2,1,0:T(8,128)(2,1)S(1)} collective-permute-done((bf16[12,64,384]{2,1,0:T(8,128)(2,1)}, bf16[12,64,384]{2,1,0:T(8,128)(2,1)S(1)}, u32[]{:S(2)}, u32[]{:S(2)}) %collective-permute-start.4) | collective-permute-done | bytes 589856 | tf_op jit(solution)/shard_map/ppermute | solution.py:655
  126.1 0.2 all-to-all-done.3.recv
  126.3 0.6 copy-done.15
  126.9 0.2 copy-done.16
  127.2 12.0 %coarse.1 = (bf16[12,4,64,128]{3,2,1,0:T(8,128)(2,1)}, bf16[12,64,128]{2,1,0:T(8,128)(2,1)}, bf16[12,64,128]{2,1,0:T(8,128)(2,1)}, bf16[192,64]{1,0:T(8,128)(2,1)}, bf16[32,48,128]{2,1,0:T(8,128)(2,1)}) custom-call(s32[1]{0:T(128)} %bitcast.stripe_ref, s32[48,2]{1,0:T(8,128)} %copy.197.tab, bf16[12,4,64,128]{3,2,1,0:T(8,128)(2,1)} %get-tuple-element.44.x, ...), custom_call_target="tpu_custom_call" | custom-call | flops 10000000000 | bytes 4104580 | tf_op jit(solution)/shard_map/coarse/pallas_call | solution.py:638
  139.2 16.6 %all_to_all.35.yrecv = bf16[32,48,128]{2,1,0:T(8,128)(2,1)} all-to-all(bf16[32,48,128]{2,1,0:T(8,128)(2,1)} %get-tuple-element.51), channel_id=1, replica_groups=mesh['face'=1,'tile'=32] {'tile'}, dimensions={0} | all-to-all | bytes 786432 | tf_op jit(solution)/shard_map/all_to_all | solution.py:660
  155.8 2.6 %all-to-all-start.2 = ((bf16[32,96,128]{2,1,0:T(8,128)(2,1)}), bf16[32,96,128]{2,1,0:T(8,128)(2,1)S(1)}, u32[]{:S(2)}, u32[]{:S(2)}) async-start(bf16[32,96,128]{2,1,0:T(8,128)(2,1)} %get-tuple-element.43), calls=%async_computation.2 | async-start | bytes 1572864 | tf_op jit(solution)/shard_map/all_to_all | solution.py:660
  158.5 0.2 reshape.152
  158.7 0.2 convert_reduce_fusion
  159.1 0.2 collective-permute-start.6
  159.4 5.2 %collective-permute-start.7 = (bf16[12,64,128]{2,1,0:T(8,128)(2,1)S(1)}, bf16[12,64,128]{2,1,0:T(8,128)(2,1)S(1)}, u32[]{:S(2)}, u32[]{:S(2)}) collective-permute-start(bf16[12,64,128]{2,1,0:T(8,128)(2,1)S(1)} %copy-done.19), channel_id=1, source_target_pairs={{1,0},{2,1},{3,2},{4,3},{5,4},{6,5},{7,6},{8,7},{9,8},{10,9},{11,1... | collective-permute-start | bytes 589832 | tf_op jit(solution)/shard_map/ppermute | solution.py:656
  164.6 0.4 copy.211
  165.5 1.0 reshape.153.weight
  166.5 0.7 add.47.col_key
  167.2 0.8 mul.112.head
  168.0 0.6 pad_maximum_fusion.3.side_weight
  168.6 11.4 %collective-permute-done.6.yup = bf16[12,64,128]{2,1,0:T(8,128)(2,1)S(1)} collective-permute-done((bf16[12,64,128]{2,1,0:T(8,128)(2,1)S(1)}, bf16[12,64,128]{2,1,0:T(8,128)(2,1)S(1)}, u32[]{:S(2)}, u32[]{:S(2)}) %collective-permute-start.6) | collective-permute-done | bytes 196640 | tf_op jit(solution)/shard_map/ppermute | solution.py:655
  180.0 0.8 all-to-all-done.2.recv
  180.8 0.9 copy-done.2
  181.7 22.4 %decode.1 = (bf16[8,12,8,256]{3,2,1,0:T(8,128)(2,1)}, bf16[32,24,256]{2,1,0:T(8,128)(2,1)}) custom-call(s32[1]{0:T(128)} %bitcast.stripe_ref, s32[48,2]{1,0:T(8,128)} %copy.197.tab, bf16[12,8,64,256]{3,2,1,0:T(8,128)(2,1)} %get-tuple-element.39.x, bf16[12,64,384]{2,1,0:T(8,128)(2,1)} %copy-done.15, bf16[12,64,384]{2,1,0:T(8,128)(2,1)} %copy-done.16, ...), custom_call_target="tpu_custom_call" | custom-call | flops 3623878656 | bytes 9606020 | tf_op jit(solution)/shard_map/decode/pallas_call | solution.py:638
  204.1 2.6 %all-to-all-start.5 = ((bf16[32,24,256]{2,1,0:T(8,128)(2,1)}), bf16[32,24,256]{2,1,0:T(8,128)(2,1)S(1)}, u32[]{:S(2)}, u32[]{:S(2)}) async-start(bf16[32,24,256]{2,1,0:T(8,128)(2,1)} %get-tuple-element.52), calls=%async_computation.5 | async-start | bytes 786432 | tf_op jit(solution)/shard_map/all_to_all | solution.py:784
  208.0 0.8 concatenate.8.into
  208.9 0.8 pad_bitcast_fusion.state
  209.7 10.2 %all-to-all-done.5.recv = bf16[32,24,256]{2,1,0:T(8,128)(2,1)S(1)} async-done(((bf16[32,24,256]{2,1,0:T(8,128)(2,1)}), bf16[32,24,256]{2,1,0:T(8,128)(2,1)S(1)}, u32[]{:S(2)}, u32[]{:S(2)}) %all-to-all-start.5) | async-done | bytes 393248 | tf_op jit(solution)/shard_map/all_to_all | solution.py:784
  219.9 0.8 broadcast_in_dim.8.out_weight
  220.7 11.2 %ocean.1 = (f32[32,8,256]{2,1,0:T(8,128)}, bf16[32,8,256]{2,1,0:T(8,128)(2,1)}) custom-call(bf16[32,24,256]{2,1,0:T(8,128)(2,1)} %copy-done, f32[32,16,256]{2,1,0:T(8,128)} %pad_bitcast_fusion.state, bf16[384,112]{1,0:T(8,128)(2,1)} %concatenate.8.into, f32[384,128]{1,0:T(8,128)} %broadcast_in_dim.8.out_weight), custom_call_target="tpu_custom_call" | custom-call | flops 50331648 | bytes 1593344 | tf_op jit(solution)/shard_map/ocean/pallas_call | solution.py:638
  231.9 2.6 %all-to-all-start.6 = ((bf16[32,8,256]{2,1,0:T(8,128)(2,1)}), bf16[32,8,256]{2,1,0:T(8,128)(2,1)S(1)}, u32[]{:S(2)}, u32[]{:S(2)}) async-start(bf16[32,8,256]{2,1,0:T(8,128)(2,1)} %get-tuple-element.53), calls=%async_computation.6 | async-start | bytes 262144 | tf_op jit(solution)/shard_map/all_to_all | solution.py:815
  234.5 0.7 copy.204.key
  235.2 1.0 stack.48
  236.2 1.1 copy.206
  237.3 5.4 %all-to-all-done.6.back = bf16[32,8,256]{2,1,0:T(8,128)(2,1)S(1)} async-done(((bf16[32,8,256]{2,1,0:T(8,128)(2,1)}), bf16[32,8,256]{2,1,0:T(8,128)(2,1)S(1)}, u32[]{:S(2)}, u32[]{:S(2)}) %all-to-all-start.6) | async-done | bytes 131104 | tf_op jit(solution)/shard_map/all_to_all | solution.py:815
  242.7 0.7 copy-done.4
  243.3 1.8 surface.1
  (95 shorter events, 3.1 us)
Async XLA Ops:
  9.7 22.0 %all-to-all-start = ((bf16[32,48,128]{2,1,0:T(8,128)(2,1)}), bf16[32,48,128]{2,1,0:T(8,128)(2,1)S(1)}, u32[]{:S(2)}, u32[]{:S(2)}) async-start(bf16[32,48,128]{2,1,0:T(8,128)(2,1)} %get-tuple-element.33), calls=%async_computation | async-start | bytes 786432 | tf_op jit(solution)/shard_map/all_to_all | solution.py:660
  16.5 40.7 %copy-start.8 = (bf16[3,64,192]{2,1,0:T(8,128)(2,1)S(1)}, bf16[3,64,192]{2,1,0:T(8,128)(2,1)}, u32[]{:S(2)}) copy-start(bf16[3,64,192]{2,1,0:T(8,128)(2,1)} %param.24) | copy-start | bytes 221188
  16.5 15.0 %collective-permute-start = (bf16[12,32,256]{2,1,0:T(8,128)(2,1)}, bf16[12,32,256]{2,1,0:T(8,128)(2,1)S(1)}, u32[]{:S(2)}, u32[]{:S(2)}) collective-permute-start(bf16[12,32,256]{2,1,0:T(8,128)(2,1)} %get-tuple-element.30), channel_id=1, source_target_pairs={{0,1},{1,2},{2,3},{3,4},{4,5},{5,6},{6,7},{7,8},{8,9},{9,10},{10,1... | collective-permute-start | bytes 589832 | tf_op jit(solution)/shard_map/ppermute | solution.py:655
  16.8 14.7 %collective-permute-start.1 = (bf16[12,32,256]{2,1,0:T(8,128)(2,1)}, bf16[12,32,256]{2,1,0:T(8,128)(2,1)S(1)}, u32[]{:S(2)}, u32[]{:S(2)}) collective-permute-start(bf16[12,32,256]{2,1,0:T(8,128)(2,1)} %get-tuple-element.31), channel_id=1, source_target_pairs={{1,0},{2,1},{3,2},{4,3},{5,4},{6,5},{7,6},{8,7},{9,8},{10,9},{11,1... | collective-permute-start | bytes 589832 | tf_op jit(solution)/shard_map/ppermute | solution.py:656
  31.5 0.7 copy-start.23
  31.5 0.7 copy-start.24
  31.8 0.7 copy-start.5
  49.1 27.2 %all-to-all-start.1 = ((bf16[32,96,128]{2,1,0:T(8,128)(2,1)}), bf16[32,96,128]{2,1,0:T(8,128)(2,1)S(1)}, u32[]{:S(2)}, u32[]{:S(2)}) async-start(bf16[32,96,128]{2,1,0:T(8,128)(2,1)} %get-tuple-element.38), calls=%async_computation.1 | async-start | bytes 1572864 | tf_op jit(solution)/shard_map/all_to_all | solution.py:660
  51.8 23.7 %collective-permute-start.2 = (bf16[12,64,256]{2,1,0:T(8,128)(2,1)}, bf16[12,64,256]{2,1,0:T(8,128)(2,1)S(1)}, u32[]{:S(2)}, u32[]{:S(2)}) collective-permute-start(bf16[12,64,256]{2,1,0:T(8,128)(2,1)} %get-tuple-element.35), channel_id=1, source_target_pairs={{0,1},{1,2},{2,3},{3,4},{4,5},{5,6},{6,7},{7,8},{8,9},{9,10},{10,1... | collective-permute-start | bytes 1179656 | tf_op jit(solution)/shard_map/ppermute | solution.py:655
  51.9 23.5 %collective-permute-start.3 = (bf16[12,64,256]{2,1,0:T(8,128)(2,1)}, bf16[12,64,256]{2,1,0:T(8,128)(2,1)S(1)}, u32[]{:S(2)}, u32[]{:S(2)}) collective-permute-start(bf16[12,64,256]{2,1,0:T(8,128)(2,1)} %get-tuple-element.36), channel_id=1, source_target_pairs={{1,0},{2,1},{3,2},{4,3},{5,4},{6,5},{7,6},{8,7},{9,8},{10,9},{11,1... | collective-permute-start | bytes 1179656 | tf_op jit(solution)/shard_map/ppermute | solution.py:656
  75.5 0.9 copy-start.17
  75.5 0.9 copy-start.18
  76.4 1.0 copy-start.3
  77.3 34.9 %copy-start.9 = (bf16[3,64,192]{2,1,0:T(8,128)(2,1)S(1)}, bf16[3,64,192]{2,1,0:T(8,128)(2,1)}, u32[]{:S(2)}) copy-start(bf16[3,64,192]{2,1,0:T(8,128)(2,1)} %param.25) | copy-start | bytes 221188
  104.2 22.1 %all-to-all-start.3 = ((bf16[32,48,128]{2,1,0:T(8,128)(2,1)}), bf16[32,48,128]{2,1,0:T(8,128)(2,1)S(1)}, u32[]{:S(2)}, u32[]{:S(2)}) async-start(bf16[32,48,128]{2,1,0:T(8,128)(2,1)} %get-tuple-element.46), calls=%async_computation.3 | async-start | bytes 786432 | tf_op jit(solution)/shard_map/all_to_all | solution.py:660
  106.8 19.3 %collective-permute-start.4 = (bf16[12,64,384]{2,1,0:T(8,128)(2,1)}, bf16[12,64,384]{2,1,0:T(8,128)(2,1)S(1)}, u32[]{:S(2)}, u32[]{:S(2)}) collective-permute-start(bf16[12,64,384]{2,1,0:T(8,128)(2,1)} %get-tuple-element.40), channel_id=1, source_target_pairs={{0,1},{1,2},{2,3},{3,4},{4,5},{5,6},{6,7},{7,8},{8,9},{9,10},{10,1... | collective-permute-start | bytes 1769480 | tf_op jit(solution)/shard_map/ppermute | solution.py:655
  107.0 19.1 %collective-permute-start.5 = (bf16[12,64,384]{2,1,0:T(8,128)(2,1)}, bf16[12,64,384]{2,1,0:T(8,128)(2,1)S(1)}, u32[]{:S(2)}, u32[]{:S(2)}) collective-permute-start(bf16[12,64,384]{2,1,0:T(8,128)(2,1)} %get-tuple-element.41), channel_id=1, source_target_pairs={{1,0},{2,1},{3,2},{4,3},{5,4},{6,5},{7,6},{8,7},{9,8},{10,9},{11,1... | collective-permute-start | bytes 1769480 | tf_op jit(solution)/shard_map/ppermute | solution.py:656
  126.1 0.8 copy-start.15
  126.1 1.0 copy-start.16
  126.3 0.9 copy-start.6
  127.2 31.3 %copy-start.7 = (bf16[3,64,384]{2,1,0:T(8,128)(2,1)S(1)}, bf16[3,64,384]{2,1,0:T(8,128)(2,1)}, u32[]{:S(2)}) copy-start(bf16[3,64,384]{2,1,0:T(8,128)(2,1)} %param.26) | copy-start | bytes 442372
  127.2 31.5 %copy-start.10 = (pred[96,96]{1,0:T(32,128)(4,1)S(1)}, pred[96,96]{1,0:T(32,128)(4,1)}, u32[]{:S(2)}) copy-start(pred[96,96]{1,0:T(32,128)(4,1)} %constant.29.clone) | copy-start | bytes 27652
  127.2 31.5 %copy-start.13 = (s32[96,1]{0,1:T(1,128)S(1)}, s32[96,1]{0,1:T(1,128)}, u32[]{:S(2)}) copy-start(s32[96,1]{0,1:T(1,128)} %param.20) | copy-start | bytes 1156
  127.2 31.7 %copy-start.12 = (f32[64,6]{0,1:T(8,128)S(1)}, f32[64,6]{0,1:T(8,128)}, u32[]{:S(2)}) copy-start(f32[64,6]{0,1:T(8,128)} %param.28) | copy-start | bytes 4612
  127.2 31.7 %copy-start.11 = (bf16[12,64]{1,0:T(8,128)(2,1)S(1)}, bf16[12,64]{1,0:T(8,128)(2,1)}, u32[]{:S(2)}) copy-start(bf16[12,64]{1,0:T(8,128)(2,1)} %param.27) | copy-start | bytes 4612
  139.2 20.0 %copy-start.20 = (bf16[12,64,128]{2,1,0:T(8,128)(2,1)S(1)}, bf16[12,64,128]{2,1,0:T(8,128)(2,1)}, u32[]{:S(2)}) copy-start(bf16[12,64,128]{2,1,0:T(8,128)(2,1)} %get-tuple-element.48) | copy-start | bytes 589828
  139.2 20.2 %copy-start.19 = (bf16[12,64,128]{2,1,0:T(8,128)(2,1)S(1)}, bf16[12,64,128]{2,1,0:T(8,128)(2,1)}, u32[]{:S(2)}) copy-start(bf16[12,64,128]{2,1,0:T(8,128)(2,1)} %get-tuple-element.49) | copy-start | bytes 589828
  139.2 25.9 %copy-start.1 = (f32[1,1,192,2,256]{4,3,2,1,0:T(2,128)S(1)}, f32[1,1,192,2,256]{4,3,2,1,0:T(2,128)}, u32[]{:S(2)}) copy-start(f32[1,1,192,2,256]{4,3,2,1,0:T(2,128)} %param.22) | copy-start | bytes 1179652
  155.8 25.0 %all-to-all-start.2 = ((bf16[32,96,128]{2,1,0:T(8,128)(2,1)}), bf16[32,96,128]{2,1,0:T(8,128)(2,1)S(1)}, u32[]{:S(2)}, u32[]{:S(2)}) async-start(bf16[32,96,128]{2,1,0:T(8,128)(2,1)} %get-tuple-element.43), calls=%async_computation.2 | async-start | bytes 1572864 | tf_op jit(solution)/shard_map/all_to_all | solution.py:660
  159.1 20.9 %collective-permute-start.6 = (bf16[12,64,128]{2,1,0:T(8,128)(2,1)S(1)}, bf16[12,64,128]{2,1,0:T(8,128)(2,1)S(1)}, u32[]{:S(2)}, u32[]{:S(2)}) collective-permute-start(bf16[12,64,128]{2,1,0:T(8,128)(2,1)S(1)} %copy-done.20), channel_id=1, source_target_pairs={{0,1},{1,2},{2,3},{3,4},{4,5},{5,6},{6,7},{7,8},{8,9},{9,10},{10,1... | collective-permute-start | bytes 589832 | tf_op jit(solution)/shard_map/ppermute | solution.py:655
  159.4 20.7 %collective-permute-start.7 = (bf16[12,64,128]{2,1,0:T(8,128)(2,1)S(1)}, bf16[12,64,128]{2,1,0:T(8,128)(2,1)S(1)}, u32[]{:S(2)}, u32[]{:S(2)}) collective-permute-start(bf16[12,64,128]{2,1,0:T(8,128)(2,1)S(1)} %copy-done.19), channel_id=1, source_target_pairs={{1,0},{2,1},{3,2},{4,3},{5,4},{6,5},{7,6},{8,7},{9,8},{10,9},{11,1... | collective-permute-start | bytes 589832 | tf_op jit(solution)/shard_map/ppermute | solution.py:656
  180.0 0.8 copy-start.21
  180.0 0.8 copy-start.22
  180.8 0.9 copy-start.2
  181.7 26.2 %copy-start.14 = (f32[64]{0:T(128)S(1)}, f32[64]{0:T(128)}, u32[]{:S(2)}) copy-start(f32[64]{0:T(128)} %param.29) | copy-start | bytes 772
  204.1 15.8 %all-to-all-start.5 = ((bf16[32,24,256]{2,1,0:T(8,128)(2,1)}), bf16[32,24,256]{2,1,0:T(8,128)(2,1)S(1)}, u32[]{:S(2)}, u32[]{:S(2)}) async-start(bf16[32,24,256]{2,1,0:T(8,128)(2,1)} %get-tuple-element.52), calls=%async_computation.5 | async-start | bytes 786432 | tf_op jit(solution)/shard_map/all_to_all | solution.py:784
  219.9 0.8 copy-start
  231.9 10.8 %all-to-all-start.6 = ((bf16[32,8,256]{2,1,0:T(8,128)(2,1)}), bf16[32,8,256]{2,1,0:T(8,128)(2,1)S(1)}, u32[]{:S(2)}, u32[]{:S(2)}) async-start(bf16[32,8,256]{2,1,0:T(8,128)(2,1)} %get-tuple-element.53), calls=%async_computation.6 | async-start | bytes 262144 | tf_op jit(solution)/shard_map/all_to_all | solution.py:815
  242.7 0.7 copy-start.4

commit v3 on v2

--- a/solution.py
+++ b/solution.py
@@ -239,6 +239,7 @@
             pltpu.VMEM((2, self.faces, 8, self.chans), F32),
             pltpu.VMEM((self.tiles, self.chunk, LANES), F32),
             pltpu.VMEM((self.side + 8, LANES), F32),
+            pltpu.VMEM((16, self.rows * self.side), BF),
         ]
 
     def halo_scratch(self):
@@ -276,7 +277,7 @@
     cols[1, f] = picked[8:]
 
 
-def pack_sends(fld, stripe, tab, top, bot, off, ec_out, send_out, cols, stage, strip):
+def pack_sends(fld, stripe, tab, top, bot, off, ec_out, send_out, cols, stage, strip, picker):
     last, rows, chans, groups, per = fld.tiles - 1, fld.rows, fld.chans, fld.groups, fld.per
     held = cols[...]
     ec_out[...] = held.reshape(2 * fld.faces * 8, chans).astype(BF)
@@ -331,7 +332,7 @@
     send_out[...] = stage[...].astype(BF)
 
 
-def gather_halos(fld, stripe, tab, x, up, dn, off, ec, recv, cand, cols, above, below, pair, got, mirror):
+def gather_halos(fld, stripe, tab, top, bot, up, dn, off, ec, recv, cand, cols, above, below, pair, got, mirror):
     faces, rows, chans, side, tiles = fld.faces, fld.rows, fld.chans, fld.side, fld.tiles
     last = tiles - 1
     groups = fld.groups
@@ -344,8 +345,9 @@
     def lanes(h):
         return slice((h % fld.per) * chans, (h % fld.per + 1) * chans)
 
-    above[...] = up[:, :, off : off + side]
-    below[...] = dn[:, :, off : off + side]
+    here = slice(off, off + side)
+    above[...] = up[:, :, here]
+    below[...] = dn[:, :, here]
     over = mm_nt(end_picker(side), above[...].reshape(faces * chans, side))
     under = mm_nt(end_picker(side), below[...].reshape(faces * chans, side))
     heads = [got[q * last, : fld.extra, :] for q in range(2)]
@@ -376,8 +378,8 @@
     def _():
         q = jnp.where(stripe == 0, 0, 1)
         for h in range(faces):
-            pair[0, h] = jnp.where(q == 0, x[h, 0].astype(F32), below[h].astype(F32)).astype(BF)
-            pair[1, h] = jnp.where(q == 0, above[h].astype(F32), x[h, rows - 1].astype(F32)).astype(BF)
+            pair[0, h] = jnp.where(q == 0, top[h, :, here].astype(F32), below[h].astype(F32)).astype(BF)
+            pair[1, h] = jnp.where(q == 0, above[h].astype(F32), bot[h, :, here].astype(F32)).astype(BF)
         place = stripe * rows - 1 + prow
         inside = (place >= 0) & (place < side)
         windows = []
@@ -470,131 +472,116 @@
 
 
 def row_stack(x, above, below, f, rows):
-    lines = [above[f]] + [x[f, r] for r in range(rows)] + [below[f]]
+    lines = [above[f]] + [x[0, r] for r in range(rows)] + [below[f]]
     return lambda r: lines[r : r + 3]
 
 
-def prep_kernel(fld, stripe_ref, tab, atmos, perm, x_out, top, bot, ec_out, send_out, cols, stage, strip):
-    stripe = stripe_ref[0]
-    picker = column_picker(fld)
-
-    def one_face(f, carry):
-        block = atmos[:, f].astype(F32).reshape(fld.chans * fld.rows, fld.side).astype(BF)
-        moved = mm(perm[...], block).astype(BF)
-        lines = [moved[r * fld.chans : (r + 1) * fld.chans] for r in range(fld.rows)]
-        for r in range(fld.rows):
-            x_out[f, r] = lines[r]
-        top[f] = lines[0]
-        bot[f] = lines[-1]
-        keep_columns(picker, lines, f, cols)
-        return carry
-
-    lax.fori_loop(0, fld.faces, one_face, 0)
-    pack_sends(fld, stripe, tab, top, bot, 0, ec_out, send_out, cols, stage, strip)
-
-
-def level_kernel(fld, out_fld, off, stripe_ref, tab, x, up, dn, ec, recv, weight, side_weight, *refs):
-    outs, sends, halos = refs[:5], refs[5:8], refs[8:]
-    x_out, top, bot, ec_out, send_out = outs
-    stripe = stripe_ref[0]
-    gather_halos(fld, stripe, tab, x, up, dn, off, ec, recv, *halos)
+def prep_kernel(fld, stripe_ref, tab, atmos, perm, x_out, top, bot, ec_out, send_out, *sends):
+    stripe, f = stripe_ref[0], pl.program_id(0)
+
+    @pl.when(f == 0)
+    def _():
+        sends[3][...] = column_picker(fld)
+
+    block = atmos[...].astype(F32).reshape(fld.chans * fld.rows, fld.side).astype(BF)
+    moved = mm(perm[...], block).astype(BF)
+    lines = [moved[r * fld.chans : (r + 1) * fld.chans] for r in range(fld.rows)]
+    for r in range(fld.rows):
+        x_out[0, r] = lines[r]
+    top[f] = lines[0]
+    bot[f] = lines[-1]
+    keep_columns(sends[3][...], lines, f, sends[0])
+
+    @pl.when(f == fld.faces - 1)
+    def _():
+        pack_sends(fld, stripe, tab, top, bot, 0, ec_out, send_out, *sends)
+
+
+def level_kernel(fld, out_fld, low, off, stripe_ref, tab, x, old_top, old_bot, up, dn, ec, recv, weight, side_weight, *refs):
+    stripe, f = stripe_ref[0], pl.program_id(0)
+    if low is None:
+        outs, sends, halos = refs[:5], refs[5:9], refs[9:]
+        x_out, top, bot, ec_out, send_out = outs
+    else:
+        pool, outs, sends, low_sends, halos = refs[0], refs[1:9], refs[9:13], refs[13:17], refs[17:]
+        x_out, y_out, top, bot, ec_out, send_out, low_ec, low_send = outs
+    *halos, ends_ref = halos
     _, cols, above, below = halos[:4]
-    terms = column_terms(side_weight, [cols[0].astype(BF), cols[1].astype(BF)], out_fld.chans)
-    picker = column_picker(out_fld)
-
-    def one_face(f, carry):
-        lines = row_stack(x, above, below, f, fld.rows)
-        ends = face_terms(terms, f)
-        made = []
-        for r in range(fld.rows):
-            cells = conv_row(
-                weight[...], jnp.concatenate(lines(r), axis=0), ends, r, out_fld.chans
-            )
-            x_out[f, r] = cells
-            made.append(cells)
-        top[f] = made[0]
-        bot[f] = made[-1]
-        keep_columns(picker, made, f, sends[0])
-        return carry
-
-    lax.fori_loop(0, fld.faces, one_face, 0)
-    pack_sends(out_fld, stripe, tab, top, bot, 0, ec_out, send_out, *sends)
-
-
-def encode_kernel(fld, out_fld, low, stripe_ref, tab, x, up, dn, ec, recv, weight, side_weight, pool, *refs):
-    outs, sends, low_sends, halos = refs[:8], refs[8:11], refs[11:14], refs[14:]
-    x_out, y_out, top, bot, ec_out, send_out, low_ec, low_send = outs
-    stripe = stripe_ref[0]
-    gather_halos(fld, stripe, tab, x, up, dn, 0, ec, recv, *halos)
-    _, cols, above, below = halos[:4]
-    terms = column_terms(side_weight, [cols[0].astype(BF), cols[1].astype(BF)], out_fld.chans)
     side = fld.side
-    picker, low_picker = column_picker(out_fld), column_picker(low)
-
-    def one_face(f, carry):
-        lines = row_stack(x, above, below, f, fld.rows)
-        ends = face_terms(terms, f)
-        made, pooled = [], []
-        for r in range(fld.rows):
-            cells = conv_row(
-                weight[...], jnp.concatenate(lines(r), axis=0), ends, r, out_fld.chans
-            )
-            x_out[f, r] = cells
-            made.append(cells)
-            if r % 2 == 1:
-                mean = (mm(made[r - 1], pool[...]) + mm(cells, pool[...])).astype(BF)
-                y_out[f, r // 2] = mean
-                pooled.append(mean)
-        top[f, :, :side] = made[0]
-        bot[f, :, :side] = made[-1]
-        keep_columns(picker, made, f, sends[0])
+
+    @pl.when(f == 0)
+    def _():
+        gather_halos(fld, stripe, tab, old_top, old_bot, up, dn, off, ec, recv, *halos)
+        terms = column_terms(side_weight, [cols[0].astype(BF), cols[1].astype(BF)], out_fld.chans)
+        ends_ref[0], ends_ref[1] = terms
+        sends[3][...] = column_picker(out_fld)
+        if low is not None:
+            low_sends[3][...] = column_picker(low)
+
+    lines = row_stack(x, above, below, f, fld.rows)
+    ends = face_terms([ends_ref[0], ends_ref[1]], f)
+    made, pooled = [], []
+    for r in range(fld.rows):
+        cells = conv_row(weight[...], jnp.concatenate(lines(r), axis=0), ends, r, out_fld.chans)
+        x_out[0, r] = cells
+        made.append(cells)
+        if low is not None and r % 2 == 1:
+            mean = (mm(made[r - 1], pool[...]) + mm(cells, pool[...])).astype(BF)
+            y_out[0, r // 2] = mean
+            pooled.append(mean)
+    top[f, :, :side] = made[0]
+    bot[f, :, :side] = made[-1]
+    keep_columns(sends[3][...], made, f, sends[0])
+    if low is not None:
         top[f, :, side:] = pooled[0]
         bot[f, :, side:] = pooled[-1]
-        keep_columns(low_picker, pooled, f, low_sends[0])
-        return carry
-
-    lax.fori_loop(0, fld.faces, one_face, 0)
-    pack_sends(low, stripe, tab, top, bot, side, low_ec, low_send, *low_sends)
-    pack_sends(out_fld, stripe, tab, top, bot, 0, ec_out, send_out, *sends)
-
-
-def decode_kernel(fld, low, out_ch, vars_out, stripe_ref, tab, x, up, dn, ec, recv, y, yup, ydn, yec, yrecv, weight, side_weight, spread, head, atmos, land, row_key, col_key, pred_out, flux_out, *refs):
-    halos, low_halos, flux = refs[:7], refs[7:14], refs[14]
-    stripe = stripe_ref[0]
-    gather_halos(low, stripe, tab, y, yup, ydn, 0, yec, yrecv, *low_halos)
-    gather_halos(fld, stripe, tab, x, up, dn, 0, ec, recv, *halos)
+        keep_columns(low_sends[3][...], pooled, f, low_sends[0])
+
+    @pl.when(f == fld.faces - 1)
+    def _():
+        if low is not None:
+            pack_sends(low, stripe, tab, top, bot, side, low_ec, low_send, *low_sends)
+        pack_sends(out_fld, stripe, tab, top, bot, 0, ec_out, send_out, *sends)
+
+
+def decode_kernel(fld, low, out_ch, vars_out, stripe_ref, tab, x, top, bot, up, dn, ec, recv, y, low_top, low_bot, yup, ydn, yec, yrecv, weight, side_weight, spread, head, atmos, land, row_key, col_key, pred_out, flux_out, *refs):
+    halos, low_halos, flux, ends_ref = refs[:7], refs[7:14], refs[14], refs[15]
+    stripe, f = stripe_ref[0], pl.program_id(0)
     _, cols, above, below = halos[:4]
     _, low_cols, low_above, low_below = low_halos[:4]
-    size = GROUP * GROUP
-    row, col = iota((size, size), 0), iota((size, size), 1)
-    widen = (col == (row // GROUP) * GROUP + (row % GROUP + 1) // 2).astype(F32).astype(BF)
-    joined = []
-    for s in range(2):
-        wide = mm(widen, low_cols[s].astype(BF))
-        joined.append(jnp.concatenate([cols[s], wide], axis=1).astype(BF))
-    terms = column_terms(side_weight, joined, out_ch)
-
-    def one_face(f, carry):
-        lines = row_stack(x, above, below, f, fld.rows)
-        ends = face_terms(terms, f)
-        low_lines = [low_above[f]] + [y[f, r] for r in range(low.rows)] + [low_below[f]]
-        wide = [mm(cells, spread[...]).astype(BF) for cells in low_lines]
-        made = []
-        for r in range(fld.rows):
-            picked = [wide[(r + a + 1) // 2] for a in range(3)]
-            made.append(
-                conv_row(weight[...], jnp.concatenate(lines(r) + picked, axis=0), ends, r, out_ch)
-            )
-        result = mm(head[...], jnp.concatenate(made, axis=0)).reshape(-1, fld.rows, fld.side)
-        pred_out[:, f] = (atmos[:, f].astype(F32) + result[:vars_out]).astype(BF)
-        sea = land[f] == 1
-        flux[:, f] = jnp.where(sea[None], result[vars_out:], 0.0)
-        return carry
-
-    lax.fori_loop(0, fld.faces, one_face, 0)
-    chosen = (row_key[...] == col_key[...]).astype(F32).astype(BF)
-    tiles = flux[...].reshape(-1, fld.side).astype(BF)
-    flux_out[...] = mm(chosen, tiles).astype(BF).reshape(flux_out.shape)
+
+    @pl.when(f == 0)
+    def _():
+        gather_halos(low, stripe, tab, low_top, low_bot, yup, ydn, 0, yec, yrecv, *low_halos)
+        gather_halos(fld, stripe, tab, top, bot, up, dn, 0, ec, recv, *halos)
+        size = GROUP * GROUP
+        row, col = iota((size, size), 0), iota((size, size), 1)
+        widen = (col == (row // GROUP) * GROUP + (row % GROUP + 1) // 2).astype(F32).astype(BF)
+        joined = []
+        for s in range(2):
+            wide = mm(widen, low_cols[s].astype(BF))
+            joined.append(jnp.concatenate([cols[s], wide], axis=1).astype(BF))
+        ends_ref[0], ends_ref[1] = column_terms(side_weight, joined, out_ch)
+
+    lines = row_stack(x, above, below, f, fld.rows)
+    ends = face_terms([ends_ref[0], ends_ref[1]], f)
+    low_lines = [low_above[f]] + [y[0, r] for r in range(low.rows)] + [low_below[f]]
+    wide = [mm(cells, spread[...]).astype(BF) for cells in low_lines]
+    made = []
+    for r in range(fld.rows):
+        picked = [wide[(r + a + 1) // 2] for a in range(3)]
+        made.append(
+            conv_row(weight[...], jnp.concatenate(lines(r) + picked, axis=0), ends, r, out_ch)
+        )
+    result = mm(head[...], jnp.concatenate(made, axis=0)).reshape(-1, fld.rows, fld.side)
+    pred_out[:, 0] = (atmos[:, 0].astype(F32) + result[:vars_out]).astype(BF)
+    flux[:, f] = jnp.where((land[0] == 1)[None], result[vars_out:], 0.0)
+
+    @pl.when(f == fld.faces - 1)
+    def _():
+        chosen = (row_key[...] == col_key[...]).astype(F32).astype(BF)
+        tiles = flux[...].reshape(-1, fld.side).astype(BF)
+        flux_out[...] = mm(chosen, tiles).astype(BF).reshape(flux_out.shape)
 
 
 def ocean_kernel(cap, recv, state, into, out_weight, sea_out, back_out):
@@ -628,22 +615,22 @@
     out[0] = jnp.where(land[...] == 1, sea, pred[0].astype(F32)).astype(BF)
 
 
-def call(kernel, outs, ins, scratch, flops, smem=0, specs=None, aliases=None, out_specs=None, name=None):
+def call(kernel, outs, ins, scratch, flops, smem=0, steps=1, specs=None, aliases=None, out_specs=None, name=None):
     whole = pl.BlockSpec(memory_space=pltpu.VMEM)
     in_specs = [pl.BlockSpec(memory_space=pltpu.SMEM)] * smem + [whole] * (len(ins) - smem)
     for position, spec in (specs or {}).items():
         in_specs[position] = spec
-    grid = {"grid": (1,)} if specs else {}
+    grid = {"grid": (steps,)} if specs else {}
     moved = sum(int(np.prod(a.shape)) * a.dtype.itemsize for a in list(ins) + list(outs))
     return pl.pallas_call(
         kernel,
         out_shape=outs,
         **grid,
         in_specs=in_specs,
-        out_specs=out_specs or [whole] * len(outs),
+        out_specs=[(out_specs or {}).get(n, whole) for n in range(len(outs))],
         scratch_shapes=scratch,
         input_output_aliases=aliases or {},
-        compiler_params=pltpu.CompilerParams(vmem_limit_bytes=56 * 1024 * 1024),
+        compiler_params=pltpu.CompilerParams(vmem_limit_bytes=30 * 1024 * 1024),
         cost_estimate=pl.CostEstimate(flops=int(flops), bytes_accessed=int(moved), transcendentals=0),
         name=name,
     )(*ins)
@@ -699,6 +686,11 @@
     perm, pool = jnp.asarray(perm, BF), jnp.asarray(0.25 * spread.T, BF)
     spread = jnp.asarray(spread, BF)
 
+    def one(shape, dim=0):
+        block = tuple(1 if n == dim else size for n, size in enumerate(shape))
+        return pl.BlockSpec(block, lambda i: tuple(i if n == dim else 0 for n in range(len(shape))))
+
+    ends = [pltpu.VMEM((2, width, GROUP * GROUP), F32)]
     x0, top, bot, ec, send = call(
         functools.partial(prep_kernel, entry),
         [entry.main()] + entry.edges() + entry.sends(),
@@ -706,42 +698,54 @@
         entry.send_scratch(),
         2 * cells * in_ch * in_ch * rows,
         smem=2,
+        steps=faces,
+        specs={2: one(atmos_state.shape, 1)},
+        out_specs={0: one(entry.main().shape)},
         name="prep",
     )
     got = swap_chunks(send)
     up, dn = swap_rows(top, bot)
     x1, top, bot, ec, send = call(
-        functools.partial(level_kernel, entry, full, 0),
+        functools.partial(level_kernel, entry, full, None, 0),
         [full.main()] + full.edges() + full.sends(),
-        (stripe, seam_table, x0, up, dn, ec, got) + packed_weight(conv_input, in_ch),
-        full.send_scratch() + entry.halo_scratch(),
+        (stripe, seam_table, x0, top, bot, up, dn, ec, got) + packed_weight(conv_input, in_ch),
+        full.send_scratch() + entry.halo_scratch() + ends,
         2 * cells * 9 * in_ch * width,
         smem=2,
+        steps=faces,
+        specs={2: one(x0.shape)},
+        out_specs={0: one(full.main().shape)},
         name="conv_in",
     )
     got = swap_chunks(send)
     up, dn = swap_rows(top, bot)
     x2, y0, top, bot, ec, send, low_ec, low_send = call(
-        functools.partial(encode_kernel, full, full, low),
+        functools.partial(level_kernel, full, full, low, 0),
         [full.main(), low.main()] + full.edges(side // 2) + full.sends() + low.sends(),
-        (stripe, seam_table, x1, up, dn, ec, got) + packed_weight(conv_encode, width) + (pool,),
-        full.send_scratch() + low.send_scratch() + full.halo_scratch(),
+        (stripe, seam_table, x1, top, bot, up, dn, ec, got) + packed_weight(conv_encode, width) + (pool,),
+        full.send_scratch() + low.send_scratch() + full.halo_scratch() + ends,
         2 * cells * 9 * width * width,
         smem=2,
+        steps=faces,
+        specs={2: one(x1.shape)},
+        out_specs={0: one(full.main().shape), 1: one(low.main().shape)},
         name="encode",
     )
     low_got = swap_chunks(low_send)
     up, dn = swap_rows(top, bot)
     y1, low_top, low_bot, low_ec, low_send = call(
-        functools.partial(level_kernel, low, low, side),
+        functools.partial(level_kernel, low, low, None, side),
         [low.main()] + low.edges() + low.sends(),
-        (stripe, seam_table, y0, up, dn, low_ec, low_got) + packed_weight(conv_coarse, width),
-        low.send_scratch() + low.halo_scratch(),
+        (stripe, seam_table, y0, top, bot, up, dn, low_ec, low_got) + packed_weight(conv_coarse, width),
+        low.send_scratch() + low.halo_scratch() + ends,
         10e9,
         smem=2,
+        steps=faces,
+        specs={2: one(y0.shape)},
+        out_specs={0: one(low.main().shape)},
         name="coarse",
     )
-    got = swap_chunks(send)
+    low_send, got = lax.optimization_barrier((low_send, swap_chunks(send)))
     low_got = swap_chunks(low_send)
     low_up, low_dn = swap_rows(low_top, low_bot)
 
@@ -773,12 +777,23 @@
             jax.ShapeDtypeStruct((OUT_VARS, faces, rows, side), BF),
             jax.ShapeDtypeStruct((tiles, flux_ch * cap, side), BF),
         ],
-        (stripe, seam_table, x2, up, dn, ec, got, y1, low_up, low_dn, low_ec, low_got)
+        (stripe, seam_table, x2, top, bot, up, dn, ec, got)
+        + (y1, low_top, low_bot, low_up, low_dn, low_ec, low_got)
         + (body, sides, spread, head, atmos_state, land_sea, row_key, col_key),
-        full.halo_scratch() + low.halo_scratch() + [pltpu.VMEM((flux_ch, faces, rows, side), F32)],
+        full.halo_scratch()
+        + low.halo_scratch()
+        + [pltpu.VMEM((flux_ch, faces, rows, side), F32)]
+        + ends,
         2 * cells * 18 * width * width,
         smem=2,
-        specs={16: pl.BlockSpec((OUT_VARS, faces, rows, side), lambda i: (0, 0, 0, 0))},
+        steps=faces,
+        specs={
+            2: one(x2.shape),
+            9: one(y1.shape),
+            20: pl.BlockSpec((OUT_VARS, 1, rows, side), lambda i: (0, i, 0, 0)),
+            21: one(land_sea.shape),
+        },
+        out_specs={0: one((OUT_VARS, faces, rows, side), 1)},
         name="decode",
     )
     arrived = lax.all_to_all(outgoing, "tile", split_axis=0, concat_axis=0, tiled=True)
@@ -822,7 +837,7 @@
         [],
         2 * count * tiles * 8 * side,
         specs={3: first},
-        out_specs=[first],
+        out_specs={0: first},
         aliases={3: 0},
         name="surface",
     )

time: 246 us -> 245 us (level)
  local copies, waits for them, and re-layouts: 21 us -> 45.6 us
  blocking collectives: 16.6 us -> 0 us
  Pallas kernels: 98.5 us -> 89.9 us
  waiting for transfers between devices: 64.1 us -> 59.6 us
  starting transfers between devices: 41.3 us -> 45.3 us
    unnamed x57 -> x87, local copies, waits for them, and re-layouts: 8.06 us -> 31.8 us
    ppermute x4, waiting for transfers between devices: 46.3 us -> 24.7 us  [swap_rows(): up = lax.ppermute(bot, 'tile', ring)]
    all_to_all x1 -> x0, blocking collectives: 16.6 us -> none  [swap_chunks(): lax.all_to_all(chunks, 'tile', split_axis=0, concat_axis=0, tiled=True)]
    all_to_all x4 -> x5, waiting for transfers between devices: 2.23 us -> 18 us  [swap_chunks(): lax.all_to_all(chunks, 'tile', split_axis=0, concat_axis=0, tiled=True)]
    pallas_call x7, Pallas kernels: 98.5 us -> 89.9 us  [call(): pl.pallas_call(kernel, out_shape=outs, **grid, in_specs=in_specs, out_spe...]
    all_to_all x4 -> x5, starting transfers between devices: 14.6 us -> 18.5 us  [swap_chunks(): lax.all_to_all(chunks, 'tile', split_axis=0, concat_axis=0, tiled=True)]
    reshape x2, local copies, waits for them, and re-layouts: 0.58 us -> 3.07 us  [on_one_group(): split = conv_decode.reshape(taps, width, taps, 2, width)]
  transfers between devices with their start and end apart: 14 -> 15, of which waited for: 10 -> 7; matrix products, arithmetic and copies ran while one was open for 7% -> 9% of each run, Pallas kernels for 0% -> 5%
where the time goes in v3:
time: 245 us; the launch traced here: 244 us
  Pallas kernels  89.9 us (37%)
  waiting for transfers between devices  59.6 us (24%)
  local copies, waits for them, and re-layouts  45.6 us (19%)
  starting transfers between devices  45.3 us (18%)
    pallas_call x7, Pallas kernels, call(): pl.pallas_call(kernel, out_shape=outs, **grid, in_specs=in_specs, out_spe...  89.9 us
    unnamed x87, local copies, waits for them, and re-layouts  31.8 us
    ppermute x4, waiting for transfers between devices, swap_rows(): up = lax.ppermute(bot, 'tile', ring)  24.7 us
    ppermute x4, starting transfers between devices, swap_rows(): return (up, lax.ppermute(top, 'tile', [(j, i) for i, j in ring]))  20.6 us
    all_to_all x5, starting transfers between devices, swap_chunks(): lax.all_to_all(chunks, 'tile', split_axis=0, concat_axis=0, tiled=True)  18.5 us
    all_to_all x5, waiting for transfers between devices, swap_chunks(): lax.all_to_all(chunks, 'tile', split_axis=0, concat_axis=0, tiled=True)  18 us
    all_to_all x1, waiting for transfers between devices, on_one_group(): lax.all_to_all(outgoing, 'tile', split_axis=0, concat_axis=0, tiled=True)  10 us
    all_to_all x1, waiting for transfers between devices, on_one_group(): lax.all_to_all(back, 'tile', split_axis=0, concat_axis=0, tiled=True)  6.98 us
  transfers between devices with their start and end apart: 15, of which 7 were waited for; matrix products, arithmetic and copies ran while one was open for 9% of the time, Pallas kernels for 5%

profile of v3, /device:TPU:0, one launch (start us, length us, event | category | flops | bytes accessed | tf_op | source)
XLA Modules:
  0.0 243.7 jit_solution(17809102775889788053)
XLA Ops:
  0.6 0.8 copy.197.tab
  1.4 1.4 copy-done
  2.8 0.9 copy-done.2
  3.7 6.9 %prep.1 = (bf16[12,8,32,256]{3,2,1,0:T(8,128)(2,1)S(1)}, bf16[12,32,256]{2,1,0:T(8,128)(2,1)S(1)}, bf16[12,32,256]{2,1,0:T(8,128)(2,1)S(1)}, bf16[192,32]{1,0:T(8,128)(2,1)S(1)}, bf16[32,48,128]{2,1,0:T(8,128)(2,1)}) custom-call(s32[1]{0:T(128)} %bitcast.stripe_ref, s32[48,2]{1,0:T(8,128)S(1)} %copy.197.tab, bf16[32,12,8,256]{3,2,1,0:T(8,128)(2,1)S(1)} %copy-done, ...), custom_call_target="tpu_custom_call" | custom-call | flops 402653184 | bytes 4075908 | tf_op jit(solution)/shard_map/prep/pallas_call | solution.py:625
  10.6 6.7 %all-to-all-start = ((bf16[32,48,128]{2,1,0:T(8,128)(2,1)}), bf16[32,48,128]{2,1,0:T(8,128)(2,1)S(1)}, u32[]{:S(2)}, u32[]{:S(2)}) async-start(bf16[32,48,128]{2,1,0:T(8,128)(2,1)} %get-tuple-element.35), calls=%async_computation | async-start | bytes 786432 | tf_op jit(solution)/shard_map/all_to_all | solution.py:647
  17.7 5.1 %collective-permute-start.1 = (bf16[12,32,256]{2,1,0:T(8,128)(2,1)S(1)}, bf16[12,32,256]{2,1,0:T(8,128)(2,1)S(1)}, u32[]{:S(2)}, u32[]{:S(2)}) collective-permute-start(bf16[12,32,256]{2,1,0:T(8,128)(2,1)S(1)} %get-tuple-element.32.old_top), channel_id=1, source_target_pairs={{1,0},{2,1},{3,2},{4,3},{5,4},{6,5},{7,6},{8,7},{9,8},{10,9},{11,1... | collective-permute-start | bytes 589832 | tf_op jit(solution)/shard_map/ppermute | solution.py:643
  22.8 0.9 copy.177
  24.4 8.0 %collective-permute-done.up = bf16[12,32,256]{2,1,0:T(8,128)(2,1)S(1)} collective-permute-done((bf16[12,32,256]{2,1,0:T(8,128)(2,1)S(1)}, bf16[12,32,256]{2,1,0:T(8,128)(2,1)S(1)}, u32[]{:S(2)}, u32[]{:S(2)}) %collective-permute-start) | collective-permute-done | bytes 196640 | tf_op jit(solution)/shard_map/ppermute | solution.py:642
  32.4 0.7 copy-done.14
  33.1 0.7 copy-done.16
  33.8 0.9 copy-done.15
  34.7 0.9 copy-done.17
  35.6 14.6 %conv_in.1 = (bf16[12,8,64,256]{3,2,1,0:T(8,128)(2,1)S(1)}, bf16[12,64,256]{2,1,0:T(8,128)(2,1)S(1)}, bf16[12,64,256]{2,1,0:T(8,128)(2,1)S(1)}, bf16[192,64]{1,0:T(8,128)(2,1)S(1)}, bf16[32,96,128]{2,1,0:T(8,128)(2,1)}) custom-call(s32[1]{0:T(128)} %bitcast.stripe_ref, s32[48,2]{1,0:T(8,128)S(1)} %copy.197.tab, ...), custom_call_target="tpu_custom_call" | custom-call | flops 905969664 | bytes 7569796 | tf_op jit(solution)/shard_map/conv_in/pallas_call | solution.py:625
  50.2 1.6 copy-done.21
  51.8 2.6 %all-to-all-start.1 = ((bf16[32,96,128]{2,1,0:T(8,128)(2,1)}), bf16[32,96,128]{2,1,0:T(8,128)(2,1)S(1)}, u32[]{:S(2)}, u32[]{:S(2)}) async-start(bf16[32,96,128]{2,1,0:T(8,128)(2,1)} %get-tuple-element.40), calls=%async_computation.1 | async-start | bytes 1572864 | tf_op jit(solution)/shard_map/all_to_all | solution.py:647
  54.6 5.2 %collective-permute-start.3 = (bf16[12,64,256]{2,1,0:T(8,128)(2,1)S(1)}, bf16[12,64,256]{2,1,0:T(8,128)(2,1)S(1)}, u32[]{:S(2)}, u32[]{:S(2)}) collective-permute-start(bf16[12,64,256]{2,1,0:T(8,128)(2,1)S(1)} %get-tuple-element.37.old_top), channel_id=1, source_target_pairs={{1,0},{2,1},{3,2},{4,3},{5,4},{6,5},{7,6},{8,7},{9,8},{10,9},{11,1... | collective-permute-start | bytes 1179656 | tf_op jit(solution)/shard_map/ppermute | solution.py:643
  59.8 1.0 copy.184
  61.5 16.6 %collective-permute-done.2.up = bf16[12,64,256]{2,1,0:T(8,128)(2,1)S(1)} collective-permute-done((bf16[12,64,256]{2,1,0:T(8,128)(2,1)S(1)}, bf16[12,64,256]{2,1,0:T(8,128)(2,1)S(1)}, u32[]{:S(2)}, u32[]{:S(2)}) %collective-permute-start.2) | collective-permute-done | bytes 393248 | tf_op jit(solution)/shard_map/ppermute | solution.py:642
  78.1 0.8 copy-done.12
  79.1 1.0 copy-done.9
  80.1 1.0 copy-done.11
  81.0 1.0 copy-done.13
  82.0 1.9 copy-done.22
  83.9 24.0 %encode.1 = (bf16[12,8,64,256]{3,2,1,0:T(8,128)(2,1)S(1)}, bf16[12,4,64,128]{3,2,1,0:T(8,128)(2,1)S(1)}, bf16[12,64,384]{2,1,0:T(8,128)(2,1)S(1)}, bf16[12,64,38...) custom-call(s32[1]{0:T(128)} %bitcast.stripe_ref, ...), custom_call_target="tpu_custom_call" | custom-call | flops 1811939328 | bytes 12059012 | tf_op jit(solution)/shard_map/encode/pallas_call | solution.py:625
  107.9 1.6 copy-done.23
  109.6 0.9 copy-done.25
  110.5 2.7 %all-to-all-start.2 = ((bf16[32,48,128]{2,1,0:T(8,128)(2,1)}), bf16[32,48,128]{2,1,0:T(8,128)(2,1)S(1)}, u32[]{:S(2)}, u32[]{:S(2)}) async-start(bf16[32,48,128]{2,1,0:T(8,128)(2,1)} %get-tuple-element.47), calls=%async_computation.2 | async-start | bytes 786432 | tf_op jit(solution)/shard_map/all_to_all | solution.py:647
  113.8 5.2 %collective-permute-start.5 = (bf16[12,64,384]{2,1,0:T(8,128)(2,1)S(1)}, bf16[12,64,384]{2,1,0:T(8,128)(2,1)}, u32[]{:S(2)}, u32[]{:S(2)}) collective-permute-start(bf16[12,64,384]{2,1,0:T(8,128)(2,1)S(1)} %get-tuple-element.42.old_top.top), channel_id=1, source_target_pairs={{1,0},{2,1},{3,2},{4,3},{5,4},{6,5},{7,6},{8,7},{9,8},{10,9},{11,1... | collective-permute-start | bytes 1769480 | tf_op jit(solution)/shard_map/ppermute | solution.py:643
  119.0 13.7 %all-to-all-done.2.recv = bf16[32,48,128]{2,1,0:T(8,128)(2,1)S(1)} async-done(((bf16[32,48,128]{2,1,0:T(8,128)(2,1)}), bf16[32,48,128]{2,1,0:T(8,128)(2,1)S(1)}, u32[]{:S(2)}, u32[]{:S(2)}) %all-to-all-start.2) | async-done | bytes 393248 | tf_op jit(solution)/shard_map/all_to_all | solution.py:647
  132.7 2.8 %all-to-all-start.3 = ((bf16[32,96,128]{2,1,0:T(8,128)(2,1)}), bf16[32,96,128]{2,1,0:T(8,128)(2,1)S(1)}, u32[]{:S(2)}, u32[]{:S(2)}) async-start(bf16[32,96,128]{2,1,0:T(8,128)(2,1)} %get-tuple-element.49), calls=%async_computation.3 | async-start | bytes 1572864 | tf_op jit(solution)/shard_map/all_to_all | solution.py:647
  136.1 1.0 reshape.152
  137.1 0.8 broadcast_multiply_fusion
  137.9 1.1 copy-done.26
  139.1 11.3 %coarse.1 = (bf16[12,4,64,128]{3,2,1,0:T(8,128)(2,1)S(1)}, bf16[12,64,128]{2,1,0:T(8,128)(2,1)S(1)}, bf16[12,64,128]{2,1,0:T(8,128)(2,1)}, bf16[192,64]{1,0:T(8,128)(2,1)S(1)}, bf16[32,48,128]{2,1,0:T(8,128)(2,1)}) custom-call(s32[1]{0:T(128)} %bitcast.stripe_ref, s32[48,2]{1,0:T(8,128)S(1)} %copy.197.tab, bf16[12,4,64,128]{3,2,1,0:T(8,128)(2,1)S(1)} %copy-done.26, ...), custom_call_target="tpu_custom_call" | custom-call | flops 10000000000 | bytes 5284228 | tf_op jit(solution)/shard_map/coarse/pallas_call | solution.py:625
  150.3 0.9 copy-done.27
  151.2 0.6 copy-done.29
  151.9 4.1 %all-to-all-done.3.recv = bf16[32,96,128]{2,1,0:T(8,128)(2,1)S(1)} async-done(((bf16[32,96,128]{2,1,0:T(8,128)(2,1)}), bf16[32,96,128]{2,1,0:T(8,128)(2,1)S(1)}, u32[]{:S(2)}, u32[]{:S(2)}) %all-to-all-start.3) | async-done | bytes 786464 | tf_op jit(solution)/shard_map/all_to_all | solution.py:647
  156.0 3.5 %all-to-all-start.4 = ((bf16[32,48,128]{2,1,0:T(8,128)(2,1)}), bf16[32,48,128]{2,1,0:T(8,128)(2,1)S(1)}, u32[]{:S(2)}, u32[]{:S(2)}) async-start(bf16[32,48,128]{2,1,0:T(8,128)(2,1)} %get-tuple-element.55), calls=%async_computation.4 | async-start | bytes 786432 | tf_op jit(solution)/shard_map/all_to_all | solution.py:647
  159.5 1.1 slice_bitcast_fusion.1
  160.9 5.1 %collective-permute-start.7 = (bf16[12,64,128]{2,1,0:T(8,128)(2,1)S(1)}, bf16[12,64,128]{2,1,0:T(8,128)(2,1)}, u32[]{:S(2)}, u32[]{:S(2)}) collective-permute-start(bf16[12,64,128]{2,1,0:T(8,128)(2,1)S(1)} %get-tuple-element.52.low_top), channel_id=1, source_target_pairs={{1,0},{2,1},{3,2},{4,3},{5,4},{6,5},{7,6},{8,7},{9,8},{10,9},{11,1... | collective-permute-start | bytes 589832 | tf_op jit(solution)/shard_map/ppermute | solution.py:643
  166.1 2.1 copy.211
  168.2 1.9 copy.209
  170.1 1.9 slice.65
  172.0 0.7 stack.45
  172.7 0.7 stack.46
  173.4 1.3 reshape.153.weight
  174.8 1.1 mul.112.head
  175.9 0.8 pad_maximum_fusion.3.side_weight
  176.8 1.1 copy-done.5
  177.9 1.1 copy-done.7
  179.0 1.0 copy-done.18
  179.9 1.9 copy-done.24
  181.8 1.1 copy-done.28
  183.0 0.8 copy-done.30
  183.8 21.4 %decode.1 = (bf16[8,12,8,256]{3,2,1,0:T(8,128)(2,1)}, bf16[32,24,256]{2,1,0:T(8,128)(2,1)}) custom-call(s32[1]{0:T(128)} %bitcast.stripe_ref, s32[48,2]{1,0:T(8,128)S(1)} %copy.197.tab, bf16[12,8,64,256]{3,2,1,0:T(8,128)(2,1)S(1)} %copy-done.24, bf16[12,64,384]{2,1,0:T(8,128)(2,1)S(1)} %copy-done.5, bf16[12,64,384]{2,1,0:T(8,128)(2,1)S(1)} %copy-done.7, ...), custom_call_target="tpu_custom_call" | custom-call | flops 3623878656 | bytes 11178884 | tf_op jit(solution)/shard_map/decode/pallas_call | solution.py:625
  205.1 2.7 %all-to-all-start.5 = ((bf16[32,24,256]{2,1,0:T(8,128)(2,1)}), bf16[32,24,256]{2,1,0:T(8,128)(2,1)S(1)}, u32[]{:S(2)}, u32[]{:S(2)}) async-start(bf16[32,24,256]{2,1,0:T(8,128)(2,1)} %get-tuple-element.56), calls=%async_computation.5 | async-start | bytes 786432 | tf_op jit(solution)/shard_map/all_to_all | solution.py:799
  209.1 0.7 broadcast_in_dim.6
  209.8 0.9 copy.205
  211.1 10.0 %all-to-all-done.5.recv = bf16[32,24,256]{2,1,0:T(8,128)(2,1)S(1)} async-done(((bf16[32,24,256]{2,1,0:T(8,128)(2,1)}), bf16[32,24,256]{2,1,0:T(8,128)(2,1)S(1)}, u32[]{:S(2)}, u32[]{:S(2)}) %all-to-all-start.5) | async-done | bytes 393248 | tf_op jit(solution)/shard_map/all_to_all | solution.py:799
  221.2 10.1 %ocean.1 = (f32[32,8,256]{2,1,0:T(8,128)S(1)}, bf16[32,8,256]{2,1,0:T(8,128)(2,1)}) custom-call(bf16[32,24,256]{2,1,0:T(8,128)(2,1)S(1)} %all-to-all-done.5.recv, f32[32,16,256]{2,1,0:T(8,128)S(1)} %pad_bitcast_fusion.state, bf16[384,112]{1,0:T(8,128)(2,1)S(1)} %concatenate.8.into, f32[384,128]{1,0:T(8,128)S(1)} %broadcast_in_dim.8.out_weight), custom_call_target="tpu_custom_call" | custom-call | flops 50331648 | bytes 1593344 | tf_op jit(solution)/shard_map/ocean/pallas_call | solution.py:625
  231.3 2.6 %all-to-all-start.6 = ((bf16[32,8,256]{2,1,0:T(8,128)(2,1)}), bf16[32,8,256]{2,1,0:T(8,128)(2,1)S(1)}, u32[]{:S(2)}, u32[]{:S(2)}) async-start(bf16[32,8,256]{2,1,0:T(8,128)(2,1)} %get-tuple-element.57), calls=%async_computation.6 | async-start | bytes 262144 | tf_op jit(solution)/shard_map/all_to_all | solution.py:830
  234.0 1.1 copy.206
  235.1 7.0 %all-to-all-done.6.back = bf16[32,8,256]{2,1,0:T(8,128)(2,1)S(1)} async-done(((bf16[32,8,256]{2,1,0:T(8,128)(2,1)}), bf16[32,8,256]{2,1,0:T(8,128)(2,1)S(1)}, u32[]{:S(2)}, u32[]{:S(2)}) %all-to-all-start.6) | async-done | bytes 131104 | tf_op jit(solution)/shard_map/all_to_all | solution.py:830
  242.1 1.6 surface.1
  (126 shorter events, 5.3 us)
Async XLA Ops:
  1.4 1.4 copy-start
  2.8 0.9 copy-start.2
  10.6 23.1 %all-to-all-start = ((bf16[32,48,128]{2,1,0:T(8,128)(2,1)}), bf16[32,48,128]{2,1,0:T(8,128)(2,1)S(1)}, u32[]{:S(2)}, u32[]{:S(2)}) async-start(bf16[32,48,128]{2,1,0:T(8,128)(2,1)} %get-tuple-element.35), calls=%async_computation | async-start | bytes 786432 | tf_op jit(solution)/shard_map/all_to_all | solution.py:647
  17.4 15.0 %collective-permute-start = (bf16[12,32,256]{2,1,0:T(8,128)(2,1)S(1)}, bf16[12,32,256]{2,1,0:T(8,128)(2,1)S(1)}, u32[]{:S(2)}, u32[]{:S(2)}) collective-permute-start(bf16[12,32,256]{2,1,0:T(8,128)(2,1)S(1)} %get-tuple-element.33.old_bot), channel_id=1, source_target_pairs={{0,1},{1,2},{2,3},{3,4},{4,5},{5,6},{6,7},{7,8},{8,9},{9,10},{10,1... | collective-permute-start | bytes 589832 | tf_op jit(solution)/shard_map/ppermute | solution.py:642
  17.7 15.4 %collective-permute-start.1 = (bf16[12,32,256]{2,1,0:T(8,128)(2,1)S(1)}, bf16[12,32,256]{2,1,0:T(8,128)(2,1)S(1)}, u32[]{:S(2)}, u32[]{:S(2)}) collective-permute-start(bf16[12,32,256]{2,1,0:T(8,128)(2,1)S(1)} %get-tuple-element.32.old_top), channel_id=1, source_target_pairs={{1,0},{2,1},{3,2},{4,3},{5,4},{6,5},{7,6},{8,7},{9,8},{10,9},{11,1... | collective-permute-start | bytes 589832 | tf_op jit(solution)/shard_map/ppermute | solution.py:643
  32.4 0.7 copy-start.14
  33.1 0.7 copy-start.16
  33.8 0.9 copy-start.15
  34.7 0.9 copy-start.17
  35.6 43.4 %copy-start.20 = (bf16[256,128]{1,0:T(8,128)(2,1)S(1)}, bf16[256,128]{1,0:T(8,128)(2,1)}, u32[]{:S(2)}) copy-start(bf16[256,128]{1,0:T(8,128)(2,1)} %constant.27.clone.refs_0_) | copy-start | bytes 196612
  50.2 1.6 copy-start.21
  51.8 27.2 %copy-start.8 = (bf16[12,64,256]{2,1,0:T(8,128)(2,1)}, bf16[12,64,256]{2,1,0:T(8,128)(2,1)S(1)}, u32[]{:S(2)}) copy-start(bf16[12,64,256]{2,1,0:T(8,128)(2,1)S(1)} %get-tuple-element.37.old_top) | copy-start | bytes 1179652
  51.8 27.2 %copy-start.10 = (bf16[12,64,256]{2,1,0:T(8,128)(2,1)}, bf16[12,64,256]{2,1,0:T(8,128)(2,1)S(1)}, u32[]{:S(2)}) copy-start(bf16[12,64,256]{2,1,0:T(8,128)(2,1)S(1)} %get-tuple-element.38.old_bot) | copy-start | bytes 1179652
  51.8 27.2 %all-to-all-start.1 = ((bf16[32,96,128]{2,1,0:T(8,128)(2,1)}), bf16[32,96,128]{2,1,0:T(8,128)(2,1)S(1)}, u32[]{:S(2)}, u32[]{:S(2)}) async-start(bf16[32,96,128]{2,1,0:T(8,128)(2,1)} %get-tuple-element.40), calls=%async_computation.1 | async-start | bytes 1572864 | tf_op jit(solution)/shard_map/all_to_all | solution.py:647
  54.4 23.7 %collective-permute-start.2 = (bf16[12,64,256]{2,1,0:T(8,128)(2,1)S(1)}, bf16[12,64,256]{2,1,0:T(8,128)(2,1)S(1)}, u32[]{:S(2)}, u32[]{:S(2)}) collective-permute-start(bf16[12,64,256]{2,1,0:T(8,128)(2,1)S(1)} %get-tuple-element.38.old_bot), channel_id=1, source_target_pairs={{0,1},{1,2},{2,3},{3,4},{4,5},{5,6},{6,7},{7,8},{8,9},{9,10},{10,1... | collective-permute-start | bytes 1179656 | tf_op jit(solution)/shard_map/ppermute | solution.py:642
  54.6 23.5 %collective-permute-start.3 = (bf16[12,64,256]{2,1,0:T(8,128)(2,1)S(1)}, bf16[12,64,256]{2,1,0:T(8,128)(2,1)S(1)}, u32[]{:S(2)}, u32[]{:S(2)}) collective-permute-start(bf16[12,64,256]{2,1,0:T(8,128)(2,1)S(1)} %get-tuple-element.37.old_top), channel_id=1, source_target_pairs={{1,0},{2,1},{3,2},{4,3},{5,4},{6,5},{7,6},{8,7},{9,8},{10,9},{11,1... | collective-permute-start | bytes 1179656 | tf_op jit(solution)/shard_map/ppermute | solution.py:643
  78.1 0.8 copy-start.12
  79.0 1.0 copy-start.9
  80.0 1.0 copy-start.11
  81.0 1.0 copy-start.13
  82.0 1.9 copy-start.22
  83.9 29.3 %copy-start.33 = (bf16[3,64,192]{2,1,0:T(8,128)(2,1)S(1)}, bf16[3,64,192]{2,1,0:T(8,128)(2,1)}, u32[]{:S(2)}) copy-start(bf16[3,64,192]{2,1,0:T(8,128)(2,1)} %param.25) | copy-start | bytes 221188
  83.9 29.5 %copy-start.34 = (pred[96,96]{1,0:T(32,128)(4,1)S(1)}, pred[96,96]{1,0:T(32,128)(4,1)}, u32[]{:S(2)}) copy-start(pred[96,96]{1,0:T(32,128)(4,1)} %constant.29.clone) | copy-start | bytes 27652
  83.9 29.5 %copy-start.37 = (s32[96,1]{0,1:T(1,128)S(1)}, s32[96,1]{0,1:T(1,128)}, u32[]{:S(2)}) copy-start(s32[96,1]{0,1:T(1,128)} %param.20) | copy-start | bytes 1156
  107.9 1.6 copy-start.23
  109.6 0.9 copy-start.25
  110.5 27.5 %copy-start.4 = (bf16[12,64,384]{2,1,0:T(8,128)(2,1)}, bf16[12,64,384]{2,1,0:T(8,128)(2,1)S(1)}, u32[]{:S(2)}) copy-start(bf16[12,64,384]{2,1,0:T(8,128)(2,1)S(1)} %get-tuple-element.42.old_top.top) | copy-start | bytes 1769476
  110.5 27.5 %copy-start.6 = (bf16[12,64,384]{2,1,0:T(8,128)(2,1)}, bf16[12,64,384]{2,1,0:T(8,128)(2,1)S(1)}, u32[]{:S(2)}) copy-start(bf16[12,64,384]{2,1,0:T(8,128)(2,1)S(1)} %get-tuple-element.43.old_bot.bot) | copy-start | bytes 1769476
  110.5 25.7 %copy-start.32 = (bf16[3,64,384]{2,1,0:T(8,128)(2,1)S(1)}, bf16[3,64,384]{2,1,0:T(8,128)(2,1)}, u32[]{:S(2)}) copy-start(bf16[3,64,384]{2,1,0:T(8,128)(2,1)} %param.26) | copy-start | bytes 442372
  110.5 26.6 %copy-start.36 = (f32[64,6]{0,1:T(8,128)S(1)}, f32[64,6]{0,1:T(8,128)}, u32[]{:S(2)}) copy-start(f32[64,6]{0,1:T(8,128)} %param.28) | copy-start | bytes 4612
  110.5 26.7 %copy-start.35 = (bf16[12,64]{1,0:T(8,128)(2,1)S(1)}, bf16[12,64]{1,0:T(8,128)(2,1)}, u32[]{:S(2)}) copy-start(bf16[12,64]{1,0:T(8,128)(2,1)} %param.27) | copy-start | bytes 4612
  110.5 22.3 %all-to-all-start.2 = ((bf16[32,48,128]{2,1,0:T(8,128)(2,1)}), bf16[32,48,128]{2,1,0:T(8,128)(2,1)S(1)}, u32[]{:S(2)}, u32[]{:S(2)}) async-start(bf16[32,48,128]{2,1,0:T(8,128)(2,1)} %get-tuple-element.47), calls=%async_computation.2 | async-start | bytes 786432 | tf_op jit(solution)/shard_map/all_to_all | solution.py:647
  113.6 45.9 %copy-start.38 = (s32[96]{0:T(128)}, s32[96]{0:T(128)S(1)}, u32[]{:S(2)}) copy-start(s32[96]{0:T(128)S(1)} %convert_reduce_fusion) | copy-start | bytes 1156
  113.6 24.3 %collective-permute-start.4 = (bf16[12,64,384]{2,1,0:T(8,128)(2,1)S(1)}, bf16[12,64,384]{2,1,0:T(8,128)(2,1)}, u32[]{:S(2)}, u32[]{:S(2)}) collective-permute-start(bf16[12,64,384]{2,1,0:T(8,128)(2,1)S(1)} %get-tuple-element.43.old_bot.bot), channel_id=1, source_target_pairs={{0,1},{1,2},{2,3},{3,4},{4,5},{5,6},{6,7},{7,8},{8,9},{9,10},{10,1... | collective-permute-start | bytes 1769480 | tf_op jit(solution)/shard_map/ppermute | solution.py:642
  113.8 24.1 %collective-permute-start.5 = (bf16[12,64,384]{2,1,0:T(8,128)(2,1)S(1)}, bf16[12,64,384]{2,1,0:T(8,128)(2,1)}, u32[]{:S(2)}, u32[]{:S(2)}) collective-permute-start(bf16[12,64,384]{2,1,0:T(8,128)(2,1)S(1)} %get-tuple-element.42.old_top.top), channel_id=1, source_target_pairs={{1,0},{2,1},{3,2},{4,3},{5,4},{6,5},{7,6},{8,7},{9,8},{10,9},{11,1... | collective-permute-start | bytes 1769480 | tf_op jit(solution)/shard_map/ppermute | solution.py:643
  132.7 23.2 %all-to-all-start.3 = ((bf16[32,96,128]{2,1,0:T(8,128)(2,1)}), bf16[32,96,128]{2,1,0:T(8,128)(2,1)S(1)}, u32[]{:S(2)}, u32[]{:S(2)}) async-start(bf16[32,96,128]{2,1,0:T(8,128)(2,1)} %get-tuple-element.49), calls=%async_computation.3 | async-start | bytes 1572864 | tf_op jit(solution)/shard_map/all_to_all | solution.py:647
  137.9 1.1 copy-start.26
  150.3 0.9 copy-start.27
  151.2 0.6 copy-start.29
  151.8 24.9 %copy-start.1 = (bf16[32,12,8,256]{3,2,1,0:T(8,128)(2,1)S(1)}, bf16[32,12,8,256]{3,2,1,0:T(8,128)(2,1)}, u32[]{:S(2)}) copy-start(bf16[32,12,8,256]{3,2,1,0:T(8,128)(2,1)} %atmos.3) | copy-start | bytes 4718596
  151.9 25.0 %copy-start.3 = (s32[12,8,256]{2,1,0:T(8,128)S(1)}, s32[12,8,256]{2,1,0:T(8,128)}, u32[]{:S(2)}) copy-start(s32[12,8,256]{2,1,0:T(8,128)} %land.3) | copy-start | bytes 294916
  151.9 25.0 %copy-start.19 = (bf16[128,256]{1,0:T(8,128)(2,1)S(1)}, bf16[128,256]{1,0:T(8,128)(2,1)}, u32[]{:S(2)}) copy-start(bf16[128,256]{1,0:T(8,128)(2,1)} %constant.28.clone.spread) | copy-start | bytes 196612
  156.0 20.8 %all-to-all-start.4 = ((bf16[32,48,128]{2,1,0:T(8,128)(2,1)}), bf16[32,48,128]{2,1,0:T(8,128)(2,1)S(1)}, u32[]{:S(2)}, u32[]{:S(2)}) async-start(bf16[32,48,128]{2,1,0:T(8,128)(2,1)} %get-tuple-element.55), calls=%async_computation.4 | async-start | bytes 786432 | tf_op jit(solution)/shard_map/all_to_all | solution.py:647
  160.6 16.1 %collective-permute-start.6 = (bf16[12,64,128]{2,1,0:T(8,128)(2,1)}, bf16[12,64,128]{2,1,0:T(8,128)(2,1)}, u32[]{:S(2)}, u32[]{:S(2)}) collective-permute-start(bf16[12,64,128]{2,1,0:T(8,128)(2,1)} %get-tuple-element.53.low_bot), channel_id=1, source_target_pairs={{0,1},{1,2},{2,3},{3,4},{4,5},{5,6},{6,7},{7,8},{8,9},{9,10},{10,1... | collective-permute-start | bytes 589832 | tf_op jit(solution)/shard_map/ppermute | solution.py:642
  160.9 15.9 %collective-permute-start.7 = (bf16[12,64,128]{2,1,0:T(8,128)(2,1)S(1)}, bf16[12,64,128]{2,1,0:T(8,128)(2,1)}, u32[]{:S(2)}, u32[]{:S(2)}) collective-permute-start(bf16[12,64,128]{2,1,0:T(8,128)(2,1)S(1)} %get-tuple-element.52.low_top), channel_id=1, source_target_pairs={{1,0},{2,1},{3,2},{4,3},{5,4},{6,5},{7,6},{8,7},{9,8},{10,9},{11,1... | collective-permute-start | bytes 589832 | tf_op jit(solution)/shard_map/ppermute | solution.py:643
  176.8 1.1 copy-start.5
  177.9 1.1 copy-start.7
  179.0 1.0 copy-start.18
  179.9 1.9 copy-start.24
  181.8 1.1 copy-start.28
  183.0 0.8 copy-start.30
  205.1 5.9 %copy-start.31 = (f32[32,2,6,256]{3,2,1,0:T(8,128)S(1)}, f32[32,2,6,256]{3,2,1,0:T(8,128)}, u32[]{:S(2)}) copy-start(f32[32,2,6,256]{3,2,1,0:T(8,128)} %copy.209) | copy-start | bytes 1179652
  205.1 28.7 %copy-start.39 = (s32[96]{0:T(128)S(1)}, s32[96]{0:T(128)}, u32[]{:S(2)}) copy-start(s32[96]{0:T(128)} %copy-done.38) | copy-start | bytes 1156
  205.1 15.9 %all-to-all-start.5 = ((bf16[32,24,256]{2,1,0:T(8,128)(2,1)}), bf16[32,24,256]{2,1,0:T(8,128)(2,1)S(1)}, u32[]{:S(2)}, u32[]{:S(2)}) async-start(bf16[32,24,256]{2,1,0:T(8,128)(2,1)} %get-tuple-element.56), calls=%async_computation.5 | async-start | bytes 786432 | tf_op jit(solution)/shard_map/all_to_all | solution.py:799
  231.3 10.8 %all-to-all-start.6 = ((bf16[32,8,256]{2,1,0:T(8,128)(2,1)}), bf16[32,8,256]{2,1,0:T(8,128)(2,1)S(1)}, u32[]{:S(2)}, u32[]{:S(2)}) async-start(bf16[32,8,256]{2,1,0:T(8,128)(2,1)} %get-tuple-element.57), calls=%async_computation.6 | async-start | bytes 262144 | tf_op jit(solution)/shard_map/all_to_all | solution.py:830

commit v4 on v3

--- a/solution.py
+++ b/solution.py
@@ -630,7 +630,7 @@
         out_specs=[(out_specs or {}).get(n, whole) for n in range(len(outs))],
         scratch_shapes=scratch,
         input_output_aliases=aliases or {},
-        compiler_params=pltpu.CompilerParams(vmem_limit_bytes=30 * 1024 * 1024),
+        compiler_params=pltpu.CompilerParams(vmem_limit_bytes=56 * 1024 * 1024),
         cost_estimate=pl.CostEstimate(flops=int(flops), bytes_accessed=int(moved), transcendentals=0),
         name=name,
     )(*ins)

time: 245 us -> 237 us (0.967)
  local copies, waits for them, and re-layouts: 45.6 us -> 20.7 us
  Pallas kernels: 89.9 us -> 103 us
  waiting for transfers between devices: 59.6 us -> 62.5 us
    unnamed x87 -> x53, local copies, waits for them, and re-layouts: 31.8 us -> 7.81 us
    pallas_call x7, Pallas kernels: 89.9 us -> 103 us  [call(): pl.pallas_call(kernel, out_shape=outs, **grid, in_specs=in_specs, out_spe...]
    ppermute x4, waiting for transfers between devices: 24.7 us -> 28.4 us  [swap_rows(): up = lax.ppermute(bot, 'tile', ring)]
    reshape x2, local copies, waits for them, and re-layouts: 3.07 us -> 0.58 us  [on_one_group(): split = conv_decode.reshape(taps, width, taps, 2, width)]
  transfers between devices with their start and end apart: 15 -> 15, of which waited for: 7 -> 10; matrix products, arithmetic and copies ran while one was open for 9% -> 7% of each run, Pallas kernels for 5% -> 6%
where the time goes in v4:
time: 237 us; the launch traced here: 235 us
  Pallas kernels  103 us (43%)
  waiting for transfers between devices  62.5 us (26%)
  starting transfers between devices  45.2 us (19%)
  local copies, waits for them, and re-layouts  20.7 us (9%)
  other arithmetic  2.52 us (1%)
    pallas_call x7, Pallas kernels, call(): pl.pallas_call(kernel, out_shape=outs, **grid, in_specs=in_specs, out_spe...  103 us
    ppermute x4, waiting for transfers between devices, swap_rows(): up = lax.ppermute(bot, 'tile', ring)  28.4 us
    ppermute x4, starting transfers between devices, swap_rows(): return (up, lax.ppermute(top, 'tile', [(j, i) for i, j in ring]))  20.6 us
    all_to_all x5, waiting for transfers between devices, swap_chunks(): lax.all_to_all(chunks, 'tile', split_axis=0, concat_axis=0, tiled=True)  18.5 us
    all_to_all x5, starting transfers between devices, swap_chunks(): lax.all_to_all(chunks, 'tile', split_axis=0, concat_axis=0, tiled=True)  18.5 us
    all_to_all x1, waiting for transfers between devices, on_one_group(): lax.all_to_all(outgoing, 'tile', split_axis=0, concat_axis=0, tiled=True)  10.2 us
    unnamed x53, local copies, waits for them, and re-layouts  7.81 us
    all_to_all x1, waiting for transfers between devices, on_one_group(): lax.all_to_all(back, 'tile', split_axis=0, concat_axis=0, tiled=True)  5.43 us
  transfers between devices with their start and end apart: 15, of which 10 were waited for; matrix products, arithmetic and copies ran while one was open for 7% of the time, Pallas kernels for 6%

profile of v4, /device:TPU:0, one launch (start us, length us, event | category | flops | bytes accessed | tf_op | source)
XLA Modules:
  0.0 234.8 jit_solution(14481121802623298332)
XLA Ops:
  0.6 1.4 copy.197.tab
  2.0 10.6 %prep.1 = (bf16[12,8,32,256]{3,2,1,0:T(8,128)(2,1)}, bf16[12,32,256]{2,1,0:T(8,128)(2,1)}, bf16[12,32,256]{2,1,0:T(8,128)(2,1)}, bf16[192,32]{1,0:T(8,128)(2,1)}, bf16[32,48,128]{2,1,0:T(8,128)(2,1)}) custom-call(s32[1]{0:T(128)} %bitcast.stripe_ref, s32[48,2]{1,0:T(8,128)} %copy.197.tab, bf16[32,12,8,256]{3,2,1,0:T(8,128)(2,1)} %atmos.3, ...), custom_call_target="tpu_custom_call" | custom-call | flops 402653184 | bytes 4075908 | tf_op jit(solution)/shard_map/prep/pallas_call | solution.py:625
  12.6 6.7 %all-to-all-start = ((bf16[32,48,128]{2,1,0:T(8,128)(2,1)}), bf16[32,48,128]{2,1,0:T(8,128)(2,1)S(1)}, u32[]{:S(2)}, u32[]{:S(2)}) async-start(bf16[32,48,128]{2,1,0:T(8,128)(2,1)} %get-tuple-element.35), calls=%async_computation | async-start | bytes 786432 | tf_op jit(solution)/shard_map/all_to_all | solution.py:647
  19.3 0.3 collective-permute-start
  19.6 5.1 %collective-permute-start.1 = (bf16[12,32,256]{2,1,0:T(8,128)(2,1)}, bf16[12,32,256]{2,1,0:T(8,128)(2,1)S(1)}, u32[]{:S(2)}, u32[]{:S(2)}) collective-permute-start(bf16[12,32,256]{2,1,0:T(8,128)(2,1)} %get-tuple-element.32.old_top), channel_id=1, source_target_pairs={{1,0},{2,1},{3,2},{4,3},{5,4},{6,5},{7,6},{8,7},{9,8},{10,9},{11,1... | collective-permute-start | bytes 589832 | tf_op jit(solution)/shard_map/ppermute | solution.py:643
  24.7 0.9 copy.177
  25.9 0.7 copy.183.side_weight
  26.8 0.7 copy.182.weight
  27.5 6.8 %collective-permute-done.up = bf16[12,32,256]{2,1,0:T(8,128)(2,1)S(1)} collective-permute-done((bf16[12,32,256]{2,1,0:T(8,128)(2,1)}, bf16[12,32,256]{2,1,0:T(8,128)(2,1)S(1)}, u32[]{:S(2)}, u32[]{:S(2)}) %collective-permute-start) | collective-permute-done | bytes 196640 | tf_op jit(solution)/shard_map/ppermute | solution.py:642
  34.3 0.3 all-to-all-done.recv
  34.6 0.4 copy-done.21
  35.1 0.3 copy-done.7
  35.4 16.7 %conv_in.1 = (bf16[12,8,64,256]{3,2,1,0:T(8,128)(2,1)}, bf16[12,64,256]{2,1,0:T(8,128)(2,1)}, bf16[12,64,256]{2,1,0:T(8,128)(2,1)}, bf16[192,64]{1,0:T(8,128)(2,1)}, bf16[32,96,128]{2,1,0:T(8,128)(2,1)}) custom-call(s32[1]{0:T(128)} %bitcast.stripe_ref, s32[48,2]{1,0:T(8,128)} %copy.197.tab, bf16[12,8,32,256]{3,2,1,0:T(8,128)(2,1)} %get-tuple-element.31.x, ...), custom_call_target="tpu_custom_call" | custom-call | flops 905969664 | bytes 7569796 | tf_op jit(solution)/shard_map/conv_in/pallas_call | solution.py:625
  52.1 2.6 %all-to-all-start.1 = ((bf16[32,96,128]{2,1,0:T(8,128)(2,1)}), bf16[32,96,128]{2,1,0:T(8,128)(2,1)S(1)}, u32[]{:S(2)}, u32[]{:S(2)}) async-start(bf16[32,96,128]{2,1,0:T(8,128)(2,1)} %get-tuple-element.40), calls=%async_computation.1 | async-start | bytes 1572864 | tf_op jit(solution)/shard_map/all_to_all | solution.py:647
  54.7 0.2 collective-permute-start.2
  54.9 5.2 %collective-permute-start.3 = (bf16[12,64,256]{2,1,0:T(8,128)(2,1)}, bf16[12,64,256]{2,1,0:T(8,128)(2,1)S(1)}, u32[]{:S(2)}, u32[]{:S(2)}) collective-permute-start(bf16[12,64,256]{2,1,0:T(8,128)(2,1)} %get-tuple-element.37.old_top), channel_id=1, source_target_pairs={{1,0},{2,1},{3,2},{4,3},{5,4},{6,5},{7,6},{8,7},{9,8},{10,9},{11,1... | collective-permute-start | bytes 1179656 | tf_op jit(solution)/shard_map/ppermute | solution.py:643
  60.1 0.2 copy.184
  60.5 0.2 copy.185
  60.7 0.8 reshape.149.weight
  61.5 0.7 pad_maximum_fusion.1.side_weight
  62.2 16.3 %collective-permute-done.2.up = bf16[12,64,256]{2,1,0:T(8,128)(2,1)S(1)} collective-permute-done((bf16[12,64,256]{2,1,0:T(8,128)(2,1)}, bf16[12,64,256]{2,1,0:T(8,128)(2,1)S(1)}, u32[]{:S(2)}, u32[]{:S(2)}) %collective-permute-start.2) | collective-permute-done | bytes 393248 | tf_op jit(solution)/shard_map/ppermute | solution.py:642
  78.4 0.9 all-to-all-done.1.recv
  79.3 1.0 copy-done.3
  80.3 25.4 %encode.1 = (bf16[12,8,64,256]{3,2,1,0:T(8,128)(2,1)}, bf16[12,4,64,128]{3,2,1,0:T(8,128)(2,1)}, bf16[12,64,384]{2,1,0:T(8,128)(2,1)}, bf16[12,64,384]{2,1,0:T(8...) custom-call(s32[1]{0:T(128)} %bitcast.stripe_ref, ...), custom_call_target="tpu_custom_call" | custom-call | flops 1811939328 | bytes 12059012 | tf_op jit(solution)/shard_map/encode/pallas_call | solution.py:625
  105.8 2.7 %all-to-all-start.2 = ((bf16[32,48,128]{2,1,0:T(8,128)(2,1)}), bf16[32,48,128]{2,1,0:T(8,128)(2,1)S(1)}, u32[]{:S(2)}, u32[]{:S(2)}) async-start(bf16[32,48,128]{2,1,0:T(8,128)(2,1)} %get-tuple-element.47), calls=%async_computation.2 | async-start | bytes 786432 | tf_op jit(solution)/shard_map/all_to_all | solution.py:647
  108.5 0.2 copy.189
  108.7 0.2 convert_reduce_fusion
  108.9 0.2 collective-permute-start.4
  109.1 5.2 %collective-permute-start.5 = (bf16[12,64,384]{2,1,0:T(8,128)(2,1)}, bf16[12,64,384]{2,1,0:T(8,128)(2,1)}, u32[]{:S(2)}, u32[]{:S(2)}) collective-permute-start(bf16[12,64,384]{2,1,0:T(8,128)(2,1)} %get-tuple-element.42.old_top.top), channel_id=1, source_target_pairs={{1,0},{2,1},{3,2},{4,3},{5,4},{6,5},{7,6},{8,7},{9,8},{10,9},{11,1... | collective-permute-start | bytes 1769480 | tf_op jit(solution)/shard_map/ppermute | solution.py:643
  114.3 13.7 %all-to-all-done.2.recv = bf16[32,48,128]{2,1,0:T(8,128)(2,1)S(1)} async-done(((bf16[32,48,128]{2,1,0:T(8,128)(2,1)}), bf16[32,48,128]{2,1,0:T(8,128)(2,1)S(1)}, u32[]{:S(2)}, u32[]{:S(2)}) %all-to-all-start.2) | async-done | bytes 393248 | tf_op jit(solution)/shard_map/all_to_all | solution.py:647
  128.0 2.8 %all-to-all-start.3 = ((bf16[32,96,128]{2,1,0:T(8,128)(2,1)}), bf16[32,96,128]{2,1,0:T(8,128)(2,1)S(1)}, u32[]{:S(2)}, u32[]{:S(2)}) async-start(bf16[32,96,128]{2,1,0:T(8,128)(2,1)} %get-tuple-element.49), calls=%async_computation.3 | async-start | bytes 1572864 | tf_op jit(solution)/shard_map/all_to_all | solution.py:647
  131.1 0.2 copy.190
  131.3 0.8 reshape.151.weight
  132.1 0.2 reshape.152
  132.2 0.7 pad_maximum_fusion.2.side_weight
  133.0 0.8 copy-done.16
  133.8 14.1 %coarse.1 = (bf16[12,4,64,128]{3,2,1,0:T(8,128)(2,1)}, bf16[12,64,128]{2,1,0:T(8,128)(2,1)}, bf16[12,64,128]{2,1,0:T(8,128)(2,1)}, bf16[192,64]{1,0:T(8,128)(2,1)}, bf16[32,48,128]{2,1,0:T(8,128)(2,1)}) custom-call(s32[1]{0:T(128)} %bitcast.stripe_ref, s32[48,2]{1,0:T(8,128)} %copy.197.tab, bf16[12,4,64,128]{3,2,1,0:T(8,128)(2,1)} %get-tuple-element.45.x, ...), custom_call_target="tpu_custom_call" | custom-call | flops 10000000000 | bytes 5284228 | tf_op jit(solution)/shard_map/coarse/pallas_call | solution.py:625
  147.9 3.4 %all-to-all-done.3.recv = bf16[32,96,128]{2,1,0:T(8,128)(2,1)S(1)} async-done(((bf16[32,96,128]{2,1,0:T(8,128)(2,1)}), bf16[32,96,128]{2,1,0:T(8,128)(2,1)S(1)}, u32[]{:S(2)}, u32[]{:S(2)}) %all-to-all-start.3) | async-done | bytes 786464 | tf_op jit(solution)/shard_map/all_to_all | solution.py:647
  151.3 3.5 %all-to-all-start.4 = ((bf16[32,48,128]{2,1,0:T(8,128)(2,1)}), bf16[32,48,128]{2,1,0:T(8,128)(2,1)S(1)}, u32[]{:S(2)}, u32[]{:S(2)}) async-start(bf16[32,48,128]{2,1,0:T(8,128)(2,1)} %get-tuple-element.55), calls=%async_computation.4 | async-start | bytes 786432 | tf_op jit(solution)/shard_map/all_to_all | solution.py:647
  155.0 0.3 collective-permute-start.6
  155.3 5.1 %collective-permute-start.7 = (bf16[12,64,128]{2,1,0:T(8,128)(2,1)}, bf16[12,64,128]{2,1,0:T(8,128)(2,1)S(1)}, u32[]{:S(2)}, u32[]{:S(2)}) collective-permute-start(bf16[12,64,128]{2,1,0:T(8,128)(2,1)} %get-tuple-element.52.low_top), channel_id=1, source_target_pairs={{1,0},{2,1},{3,2},{4,3},{5,4},{6,5},{7,6},{8,7},{9,8},{10,9},{11,1... | collective-permute-start | bytes 589832 | tf_op jit(solution)/shard_map/ppermute | solution.py:643
  160.4 0.4 copy.211
  161.3 1.0 reshape.153.weight
  162.3 0.7 add.47.col_key
  163.0 0.8 mul.112.head
  163.8 0.7 pad_maximum_fusion.3.side_weight
  164.5 5.3 %collective-permute-done.6.yup = bf16[12,64,128]{2,1,0:T(8,128)(2,1)S(1)} collective-permute-done((bf16[12,64,128]{2,1,0:T(8,128)(2,1)}, bf16[12,64,128]{2,1,0:T(8,128)(2,1)S(1)}, u32[]{:S(2)}, u32[]{:S(2)}) %collective-permute-start.6) | collective-permute-done | bytes 196640 | tf_op jit(solution)/shard_map/ppermute | solution.py:642
  169.8 0.3 all-to-all-done.4.yrecv
  170.1 0.4 copy-done.19
  170.6 0.3 copy-done.5
  170.9 22.9 %decode.1 = (bf16[8,12,8,256]{3,2,1,0:T(8,128)(2,1)}, bf16[32,24,256]{2,1,0:T(8,128)(2,1)}) custom-call(s32[1]{0:T(128)} %bitcast.stripe_ref, s32[48,2]{1,0:T(8,128)} %copy.197.tab, bf16[12,8,64,256]{3,2,1,0:T(8,128)(2,1)} %get-tuple-element.41.x, bf16[12,64,384]{2,1,0:T(8,128)(2,1)} %get-tuple-element.42.old_top.top, ...), custom_call_target="tpu_custom_call" | custom-call | flops 3623878656 | bytes 11178884 | tf_op jit(solution)/shard_map/decode/pallas_call | solution.py:625
  193.8 2.6 %all-to-all-start.5 = ((bf16[32,24,256]{2,1,0:T(8,128)(2,1)}), bf16[32,24,256]{2,1,0:T(8,128)(2,1)S(1)}, u32[]{:S(2)}, u32[]{:S(2)}) async-start(bf16[32,24,256]{2,1,0:T(8,128)(2,1)} %get-tuple-element.56), calls=%async_computation.5 | async-start | bytes 786432 | tf_op jit(solution)/shard_map/all_to_all | solution.py:799
  197.7 0.8 concatenate.8.into
  198.6 0.8 pad_bitcast_fusion.state
  199.4 10.2 %all-to-all-done.5.recv = bf16[32,24,256]{2,1,0:T(8,128)(2,1)S(1)} async-done(((bf16[32,24,256]{2,1,0:T(8,128)(2,1)}), bf16[32,24,256]{2,1,0:T(8,128)(2,1)S(1)}, u32[]{:S(2)}, u32[]{:S(2)}) %all-to-all-start.5) | async-done | bytes 393248 | tf_op jit(solution)/shard_map/all_to_all | solution.py:799
  209.6 0.8 broadcast_in_dim.8.out_weight
  210.4 11.2 %ocean.1 = (f32[32,8,256]{2,1,0:T(8,128)}, bf16[32,8,256]{2,1,0:T(8,128)(2,1)}) custom-call(bf16[32,24,256]{2,1,0:T(8,128)(2,1)} %copy-done, f32[32,16,256]{2,1,0:T(8,128)} %pad_bitcast_fusion.state, bf16[384,112]{1,0:T(8,128)(2,1)} %concatenate.8.into, f32[384,128]{1,0:T(8,128)} %broadcast_in_dim.8.out_weight), custom_call_target="tpu_custom_call" | custom-call | flops 50331648 | bytes 1593344 | tf_op jit(solution)/shard_map/ocean/pallas_call | solution.py:625
  221.5 2.6 %all-to-all-start.6 = ((bf16[32,8,256]{2,1,0:T(8,128)(2,1)}), bf16[32,8,256]{2,1,0:T(8,128)(2,1)S(1)}, u32[]{:S(2)}, u32[]{:S(2)}) async-start(bf16[32,8,256]{2,1,0:T(8,128)(2,1)} %get-tuple-element.57), calls=%async_computation.6 | async-start | bytes 262144 | tf_op jit(solution)/shard_map/all_to_all | solution.py:830
  224.1 0.7 copy.204.key
  224.8 1.0 stack.48
  225.9 1.1 copy.206
  226.9 5.4 %all-to-all-done.6.back = bf16[32,8,256]{2,1,0:T(8,128)(2,1)S(1)} async-done(((bf16[32,8,256]{2,1,0:T(8,128)(2,1)}), bf16[32,8,256]{2,1,0:T(8,128)(2,1)S(1)}, u32[]{:S(2)}, u32[]{:S(2)}) %all-to-all-start.6) | async-done | bytes 131104 | tf_op jit(solution)/shard_map/all_to_all | solution.py:830
  232.3 0.7 copy-done.4
  233.0 1.8 surface.1
  (92 shorter events, 3.1 us)
Async XLA Ops:
  12.6 22.0 %all-to-all-start = ((bf16[32,48,128]{2,1,0:T(8,128)(2,1)}), bf16[32,48,128]{2,1,0:T(8,128)(2,1)S(1)}, u32[]{:S(2)}, u32[]{:S(2)}) async-start(bf16[32,48,128]{2,1,0:T(8,128)(2,1)} %get-tuple-element.35), calls=%async_computation | async-start | bytes 786432 | tf_op jit(solution)/shard_map/all_to_all | solution.py:647
  19.3 40.8 %copy-start.9 = (bf16[3,64,192]{2,1,0:T(8,128)(2,1)S(1)}, bf16[3,64,192]{2,1,0:T(8,128)(2,1)}, u32[]{:S(2)}) copy-start(bf16[3,64,192]{2,1,0:T(8,128)(2,1)} %param.24) | copy-start | bytes 221188
  19.3 15.0 %collective-permute-start = (bf16[12,32,256]{2,1,0:T(8,128)(2,1)}, bf16[12,32,256]{2,1,0:T(8,128)(2,1)S(1)}, u32[]{:S(2)}, u32[]{:S(2)}) collective-permute-start(bf16[12,32,256]{2,1,0:T(8,128)(2,1)} %get-tuple-element.33.old_bot), channel_id=1, source_target_pairs={{0,1},{1,2},{2,3},{3,4},{4,5},{5,6},{6,7},{7,8},{8,9},{9,10},{10,1... | collective-permute-start | bytes 589832 | tf_op jit(solution)/shard_map/ppermute | solution.py:642
  19.6 14.7 %collective-permute-start.1 = (bf16[12,32,256]{2,1,0:T(8,128)(2,1)}, bf16[12,32,256]{2,1,0:T(8,128)(2,1)S(1)}, u32[]{:S(2)}, u32[]{:S(2)}) collective-permute-start(bf16[12,32,256]{2,1,0:T(8,128)(2,1)} %get-tuple-element.32.old_top), channel_id=1, source_target_pairs={{1,0},{2,1},{3,2},{4,3},{5,4},{6,5},{7,6},{8,7},{9,8},{10,9},{11,1... | collective-permute-start | bytes 589832 | tf_op jit(solution)/shard_map/ppermute | solution.py:643
  34.3 0.7 copy-start.21
  34.3 0.7 copy-start.22
  34.6 0.7 copy-start.7
  52.1 27.2 %all-to-all-start.1 = ((bf16[32,96,128]{2,1,0:T(8,128)(2,1)}), bf16[32,96,128]{2,1,0:T(8,128)(2,1)S(1)}, u32[]{:S(2)}, u32[]{:S(2)}) async-start(bf16[32,96,128]{2,1,0:T(8,128)(2,1)} %get-tuple-element.40), calls=%async_computation.1 | async-start | bytes 1572864 | tf_op jit(solution)/shard_map/all_to_all | solution.py:647
  54.7 23.7 %collective-permute-start.2 = (bf16[12,64,256]{2,1,0:T(8,128)(2,1)}, bf16[12,64,256]{2,1,0:T(8,128)(2,1)S(1)}, u32[]{:S(2)}, u32[]{:S(2)}) collective-permute-start(bf16[12,64,256]{2,1,0:T(8,128)(2,1)} %get-tuple-element.38.old_bot), channel_id=1, source_target_pairs={{0,1},{1,2},{2,3},{3,4},{4,5},{5,6},{6,7},{7,8},{8,9},{9,10},{10,1... | collective-permute-start | bytes 1179656 | tf_op jit(solution)/shard_map/ppermute | solution.py:642
  54.9 23.5 %collective-permute-start.3 = (bf16[12,64,256]{2,1,0:T(8,128)(2,1)}, bf16[12,64,256]{2,1,0:T(8,128)(2,1)S(1)}, u32[]{:S(2)}, u32[]{:S(2)}) collective-permute-start(bf16[12,64,256]{2,1,0:T(8,128)(2,1)} %get-tuple-element.37.old_top), channel_id=1, source_target_pairs={{1,0},{2,1},{3,2},{4,3},{5,4},{6,5},{7,6},{8,7},{9,8},{10,9},{11,1... | collective-permute-start | bytes 1179656 | tf_op jit(solution)/shard_map/ppermute | solution.py:643
  78.4 0.9 copy-start.17
  78.4 0.9 copy-start.18
  79.3 1.0 copy-start.3
  80.3 28.2 %copy-start.10 = (bf16[3,64,192]{2,1,0:T(8,128)(2,1)S(1)}, bf16[3,64,192]{2,1,0:T(8,128)(2,1)}, u32[]{:S(2)}) copy-start(bf16[3,64,192]{2,1,0:T(8,128)(2,1)} %param.25) | copy-start | bytes 221188
  80.3 28.4 %copy-start.11 = (pred[96,96]{1,0:T(32,128)(4,1)S(1)}, pred[96,96]{1,0:T(32,128)(4,1)}, u32[]{:S(2)}) copy-start(pred[96,96]{1,0:T(32,128)(4,1)} %constant.29.clone) | copy-start | bytes 27652
  80.3 28.4 %copy-start.14 = (s32[96,1]{0,1:T(1,128)S(1)}, s32[96,1]{0,1:T(1,128)}, u32[]{:S(2)}) copy-start(s32[96,1]{0,1:T(1,128)} %param.20) | copy-start | bytes 1156
  105.7 26.3 %copy-start.8 = (bf16[3,64,384]{2,1,0:T(8,128)(2,1)S(1)}, bf16[3,64,384]{2,1,0:T(8,128)(2,1)}, u32[]{:S(2)}) copy-start(bf16[3,64,384]{2,1,0:T(8,128)(2,1)} %param.26) | copy-start | bytes 442372
  105.8 27.1 %copy-start.13 = (f32[64,6]{0,1:T(8,128)S(1)}, f32[64,6]{0,1:T(8,128)}, u32[]{:S(2)}) copy-start(f32[64,6]{0,1:T(8,128)} %param.28) | copy-start | bytes 4612
  105.8 27.1 %copy-start.12 = (bf16[12,64]{1,0:T(8,128)(2,1)S(1)}, bf16[12,64]{1,0:T(8,128)(2,1)}, u32[]{:S(2)}) copy-start(bf16[12,64]{1,0:T(8,128)(2,1)} %param.27) | copy-start | bytes 4612
  105.8 22.3 %all-to-all-start.2 = ((bf16[32,48,128]{2,1,0:T(8,128)(2,1)}), bf16[32,48,128]{2,1,0:T(8,128)(2,1)S(1)}, u32[]{:S(2)}, u32[]{:S(2)}) async-start(bf16[32,48,128]{2,1,0:T(8,128)(2,1)} %get-tuple-element.47), calls=%async_computation.2 | async-start | bytes 786432 | tf_op jit(solution)/shard_map/all_to_all | solution.py:647
  108.9 24.1 %collective-permute-start.4 = (bf16[12,64,384]{2,1,0:T(8,128)(2,1)}, bf16[12,64,384]{2,1,0:T(8,128)(2,1)S(1)}, u32[]{:S(2)}, u32[]{:S(2)}) collective-permute-start(bf16[12,64,384]{2,1,0:T(8,128)(2,1)} %get-tuple-element.43.old_bot.bot), channel_id=1, source_target_pairs={{0,1},{1,2},{2,3},{3,4},{4,5},{5,6},{6,7},{7,8},{8,9},{9,10},{10,1... | collective-permute-start | bytes 1769480 | tf_op jit(solution)/shard_map/ppermute | solution.py:642
  109.1 23.9 %collective-permute-start.5 = (bf16[12,64,384]{2,1,0:T(8,128)(2,1)}, bf16[12,64,384]{2,1,0:T(8,128)(2,1)}, u32[]{:S(2)}, u32[]{:S(2)}) collective-permute-start(bf16[12,64,384]{2,1,0:T(8,128)(2,1)} %get-tuple-element.42.old_top.top), channel_id=1, source_target_pairs={{1,0},{2,1},{3,2},{4,3},{5,4},{6,5},{7,6},{8,7},{9,8},{10,9},{11,1... | collective-permute-start | bytes 1769480 | tf_op jit(solution)/shard_map/ppermute | solution.py:643
  128.0 5.0 %copy-start.6 = (bf16[32,48,128]{2,1,0:T(8,128)(2,1)}, bf16[32,48,128]{2,1,0:T(8,128)(2,1)S(1)}, u32[]{:S(2)}) copy-start(bf16[32,48,128]{2,1,0:T(8,128)(2,1)S(1)} %all-to-all-done.2.recv) | copy-start | bytes 1179652
  128.0 23.2 %all-to-all-start.3 = ((bf16[32,96,128]{2,1,0:T(8,128)(2,1)}), bf16[32,96,128]{2,1,0:T(8,128)(2,1)S(1)}, u32[]{:S(2)}, u32[]{:S(2)}) async-start(bf16[32,96,128]{2,1,0:T(8,128)(2,1)} %get-tuple-element.49), calls=%async_computation.3 | async-start | bytes 1572864 | tf_op jit(solution)/shard_map/all_to_all | solution.py:647
  133.0 0.8 copy-start.16
  133.8 27.1 %copy-start.1 = (f32[1,1,192,2,256]{4,3,2,1,0:T(2,128)S(1)}, f32[1,1,192,2,256]{4,3,2,1,0:T(2,128)}, u32[]{:S(2)}) copy-start(f32[1,1,192,2,256]{4,3,2,1,0:T(2,128)} %param.22) | copy-start | bytes 1179652
  151.3 18.8 %copy-start.2 = (bf16[32,96,128]{2,1,0:T(8,128)(2,1)}, bf16[32,96,128]{2,1,0:T(8,128)(2,1)S(1)}, u32[]{:S(2)}) copy-start(bf16[32,96,128]{2,1,0:T(8,128)(2,1)S(1)} %all-to-all-done.3.recv) | copy-start | bytes 2359300
  151.3 18.8 %all-to-all-start.4 = ((bf16[32,48,128]{2,1,0:T(8,128)(2,1)}), bf16[32,48,128]{2,1,0:T(8,128)(2,1)S(1)}, u32[]{:S(2)}, u32[]{:S(2)}) async-start(bf16[32,48,128]{2,1,0:T(8,128)(2,1)} %get-tuple-element.55), calls=%async_computation.4 | async-start | bytes 786432 | tf_op jit(solution)/shard_map/all_to_all | solution.py:647
  155.0 14.8 %collective-permute-start.6 = (bf16[12,64,128]{2,1,0:T(8,128)(2,1)}, bf16[12,64,128]{2,1,0:T(8,128)(2,1)S(1)}, u32[]{:S(2)}, u32[]{:S(2)}) collective-permute-start(bf16[12,64,128]{2,1,0:T(8,128)(2,1)} %get-tuple-element.53.low_bot), channel_id=1, source_target_pairs={{0,1},{1,2},{2,3},{3,4},{4,5},{5,6},{6,7},{7,8},{8,9},{9,10},{10,1... | collective-permute-start | bytes 589832 | tf_op jit(solution)/shard_map/ppermute | solution.py:642
  155.3 14.5 %collective-permute-start.7 = (bf16[12,64,128]{2,1,0:T(8,128)(2,1)}, bf16[12,64,128]{2,1,0:T(8,128)(2,1)S(1)}, u32[]{:S(2)}, u32[]{:S(2)}) collective-permute-start(bf16[12,64,128]{2,1,0:T(8,128)(2,1)} %get-tuple-element.52.low_top), channel_id=1, source_target_pairs={{1,0},{2,1},{3,2},{4,3},{5,4},{6,5},{7,6},{8,7},{9,8},{10,9},{11,1... | collective-permute-start | bytes 589832 | tf_op jit(solution)/shard_map/ppermute | solution.py:643
  169.8 0.7 copy-start.19
  169.8 0.7 copy-start.20
  170.1 0.7 copy-start.5
  170.9 26.7 %copy-start.15 = (f32[64]{0:T(128)S(1)}, f32[64]{0:T(128)}, u32[]{:S(2)}) copy-start(f32[64]{0:T(128)} %param.29) | copy-start | bytes 772
  193.8 15.8 %all-to-all-start.5 = ((bf16[32,24,256]{2,1,0:T(8,128)(2,1)}), bf16[32,24,256]{2,1,0:T(8,128)(2,1)S(1)}, u32[]{:S(2)}, u32[]{:S(2)}) async-start(bf16[32,24,256]{2,1,0:T(8,128)(2,1)} %get-tuple-element.56), calls=%async_computation.5 | async-start | bytes 786432 | tf_op jit(solution)/shard_map/all_to_all | solution.py:799
  209.6 0.8 copy-start
  221.5 10.8 %all-to-all-start.6 = ((bf16[32,8,256]{2,1,0:T(8,128)(2,1)}), bf16[32,8,256]{2,1,0:T(8,128)(2,1)S(1)}, u32[]{:S(2)}, u32[]{:S(2)}) async-start(bf16[32,8,256]{2,1,0:T(8,128)(2,1)} %get-tuple-element.57), calls=%async_computation.6 | async-start | bytes 262144 | tf_op jit(solution)/shard_map/all_to_all | solution.py:830
  232.3 0.7 copy-start.4

commit v5 on v4

--- a/solution.py
+++ b/solution.py
@@ -471,34 +471,40 @@
     return smooth(z[out_ch : 2 * out_ch] + left + right).astype(BF)
 
 
-def row_stack(x, above, below, f, rows):
-    lines = [above[f]] + [x[0, r] for r in range(rows)] + [below[f]]
+def row_stack(x, above, below, k, f, rows):
+    lines = [above[f]] + [x[k, r] for r in range(rows)] + [below[f]]
     return lambda r: lines[r : r + 3]
 
 
 def prep_kernel(fld, stripe_ref, tab, atmos, perm, x_out, top, bot, ec_out, send_out, *sends):
-    stripe, f = stripe_ref[0], pl.program_id(0)
-
-    @pl.when(f == 0)
+    stripe, step = stripe_ref[0], pl.program_id(0)
+    batch = x_out.shape[0]
+
+    @pl.when(step == 0)
     def _():
         sends[3][...] = column_picker(fld)
 
-    block = atmos[...].astype(F32).reshape(fld.chans * fld.rows, fld.side).astype(BF)
-    moved = mm(perm[...], block).astype(BF)
-    lines = [moved[r * fld.chans : (r + 1) * fld.chans] for r in range(fld.rows)]
-    for r in range(fld.rows):
-        x_out[0, r] = lines[r]
-    top[f] = lines[0]
-    bot[f] = lines[-1]
-    keep_columns(sends[3][...], lines, f, sends[0])
-
-    @pl.when(f == fld.faces - 1)
+    def one_face(k, carry):
+        f = step * batch + k
+        block = atmos[:, k].astype(F32).reshape(fld.chans * fld.rows, fld.side).astype(BF)
+        moved = mm(perm[...], block).astype(BF)
+        lines = [moved[r * fld.chans : (r + 1) * fld.chans] for r in range(fld.rows)]
+        for r in range(fld.rows):
+            x_out[k, r] = lines[r]
+        top[f] = lines[0]
+        bot[f] = lines[-1]
+        keep_columns(sends[3][...], lines, f, sends[0])
+        return carry
+
+    lax.fori_loop(0, batch, one_face, 0)
+
+    @pl.when(step == fld.faces // batch - 1)
     def _():
         pack_sends(fld, stripe, tab, top, bot, 0, ec_out, send_out, *sends)
 
 
 def level_kernel(fld, out_fld, low, off, stripe_ref, tab, x, old_top, old_bot, up, dn, ec, recv, weight, side_weight, *refs):
-    stripe, f = stripe_ref[0], pl.program_id(0)
+    stripe, step = stripe_ref[0], pl.program_id(0)
     if low is None:
         outs, sends, halos = refs[:5], refs[5:9], refs[9:]
         x_out, top, bot, ec_out, send_out = outs
@@ -506,10 +512,11 @@
         pool, outs, sends, low_sends, halos = refs[0], refs[1:9], refs[9:13], refs[13:17], refs[17:]
         x_out, y_out, top, bot, ec_out, send_out, low_ec, low_send = outs
     *halos, ends_ref = halos
+    batch = x_out.shape[0]
     _, cols, above, below = halos[:4]
     side = fld.side
 
-    @pl.when(f == 0)
+    @pl.when(step == 0)
     def _():
         gather_halos(fld, stripe, tab, old_top, old_bot, up, dn, off, ec, recv, *halos)
         terms = column_terms(side_weight, [cols[0].astype(BF), cols[1].astype(BF)], out_fld.chans)
@@ -518,26 +525,31 @@
         if low is not None:
             low_sends[3][...] = column_picker(low)
 
-    lines = row_stack(x, above, below, f, fld.rows)
-    ends = face_terms([ends_ref[0], ends_ref[1]], f)
-    made, pooled = [], []
-    for r in range(fld.rows):
-        cells = conv_row(weight[...], jnp.concatenate(lines(r), axis=0), ends, r, out_fld.chans)
-        x_out[0, r] = cells
-        made.append(cells)
-        if low is not None and r % 2 == 1:
-            mean = (mm(made[r - 1], pool[...]) + mm(cells, pool[...])).astype(BF)
-            y_out[0, r // 2] = mean
-            pooled.append(mean)
-    top[f, :, :side] = made[0]
-    bot[f, :, :side] = made[-1]
-    keep_columns(sends[3][...], made, f, sends[0])
-    if low is not None:
-        top[f, :, side:] = pooled[0]
-        bot[f, :, side:] = pooled[-1]
-        keep_columns(low_sends[3][...], pooled, f, low_sends[0])
-
-    @pl.when(f == fld.faces - 1)
+    def one_face(k, carry):
+        f = step * batch + k
+        lines = row_stack(x, above, below, k, f, fld.rows)
+        ends = face_terms([ends_ref[0], ends_ref[1]], f)
+        made, pooled = [], []
+        for r in range(fld.rows):
+            cells = conv_row(weight[...], jnp.concatenate(lines(r), axis=0), ends, r, out_fld.chans)
+            x_out[k, r] = cells
+            made.append(cells)
+            if low is not None and r % 2 == 1:
+                mean = (mm(made[r - 1], pool[...]) + mm(cells, pool[...])).astype(BF)
+                y_out[k, r // 2] = mean
+                pooled.append(mean)
+        top[f, :, :side] = made[0]
+        bot[f, :, :side] = made[-1]
+        keep_columns(sends[3][...], made, f, sends[0])
+        if low is not None:
+            top[f, :, side:] = pooled[0]
+            bot[f, :, side:] = pooled[-1]
+            keep_columns(low_sends[3][...], pooled, f, low_sends[0])
+        return carry
+
+    lax.fori_loop(0, batch, one_face, 0)
+
+    @pl.when(step == fld.faces // batch - 1)
     def _():
         if low is not None:
             pack_sends(low, stripe, tab, top, bot, side, low_ec, low_send, *low_sends)
@@ -546,11 +558,12 @@
 
 def decode_kernel(fld, low, out_ch, vars_out, stripe_ref, tab, x, top, bot, up, dn, ec, recv, y, low_top, low_bot, yup, ydn, yec, yrecv, weight, side_weight, spread, head, atmos, land, row_key, col_key, pred_out, flux_out, *refs):
     halos, low_halos, flux, ends_ref = refs[:7], refs[7:14], refs[14], refs[15]
-    stripe, f = stripe_ref[0], pl.program_id(0)
+    stripe, step = stripe_ref[0], pl.program_id(0)
     _, cols, above, below = halos[:4]
     _, low_cols, low_above, low_below = low_halos[:4]
-
-    @pl.when(f == 0)
+    batch = x.shape[0]
+
+    @pl.when(step == 0)
     def _():
         gather_halos(low, stripe, tab, low_top, low_bot, yup, ydn, 0, yec, yrecv, *low_halos)
         gather_halos(fld, stripe, tab, top, bot, up, dn, 0, ec, recv, *halos)
@@ -563,21 +576,26 @@
             joined.append(jnp.concatenate([cols[s], wide], axis=1).astype(BF))
         ends_ref[0], ends_ref[1] = column_terms(side_weight, joined, out_ch)
 
-    lines = row_stack(x, above, below, f, fld.rows)
-    ends = face_terms([ends_ref[0], ends_ref[1]], f)
-    low_lines = [low_above[f]] + [y[0, r] for r in range(low.rows)] + [low_below[f]]
-    wide = [mm(cells, spread[...]).astype(BF) for cells in low_lines]
-    made = []
-    for r in range(fld.rows):
-        picked = [wide[(r + a + 1) // 2] for a in range(3)]
-        made.append(
-            conv_row(weight[...], jnp.concatenate(lines(r) + picked, axis=0), ends, r, out_ch)
-        )
-    result = mm(head[...], jnp.concatenate(made, axis=0)).reshape(-1, fld.rows, fld.side)
-    pred_out[:, 0] = (atmos[:, 0].astype(F32) + result[:vars_out]).astype(BF)
-    flux[:, f] = jnp.where((land[0] == 1)[None], result[vars_out:], 0.0)
-
-    @pl.when(f == fld.faces - 1)
+    def one_face(k, carry):
+        f = step * batch + k
+        lines = row_stack(x, above, below, k, f, fld.rows)
+        ends = face_terms([ends_ref[0], ends_ref[1]], f)
+        low_lines = [low_above[f]] + [y[k, r] for r in range(low.rows)] + [low_below[f]]
+        wide = [mm(cells, spread[...]).astype(BF) for cells in low_lines]
+        made = []
+        for r in range(fld.rows):
+            picked = [wide[(r + a + 1) // 2] for a in range(3)]
+            made.append(
+                conv_row(weight[...], jnp.concatenate(lines(r) + picked, axis=0), ends, r, out_ch)
+            )
+        result = mm(head[...], jnp.concatenate(made, axis=0)).reshape(-1, fld.rows, fld.side)
+        pred_out[:, k] = (atmos[:, k].astype(F32) + result[:vars_out]).astype(BF)
+        flux[:, f] = jnp.where((land[k] == 1)[None], result[vars_out:], 0.0)
+        return carry
+
+    lax.fori_loop(0, batch, one_face, 0)
+
+    @pl.when(step == fld.faces // batch - 1)
     def _():
         chosen = (row_key[...] == col_key[...]).astype(F32).astype(BF)
         tiles = flux[...].reshape(-1, fld.side).astype(BF)
@@ -686,10 +704,12 @@
     perm, pool = jnp.asarray(perm, BF), jnp.asarray(0.25 * spread.T, BF)
     spread = jnp.asarray(spread, BF)
 
-    def one(shape, dim=0):
-        block = tuple(1 if n == dim else size for n, size in enumerate(shape))
+    def some(batch, shape, dim=0):
+        block = tuple(batch if n == dim else size for n, size in enumerate(shape))
         return pl.BlockSpec(block, lambda i: tuple(i if n == dim else 0 for n in range(len(shape))))
 
+    few, many = (3 if faces % 3 == 0 else 1), faces
+    half = many // 2 if many % 2 == 0 else many
     ends = [pltpu.VMEM((2, width, GROUP * GROUP), F32)]
     x0, top, bot, ec, send = call(
         functools.partial(prep_kernel, entry),
@@ -698,9 +718,9 @@
         entry.send_scratch(),
         2 * cells * in_ch * in_ch * rows,
         smem=2,
-        steps=faces,
-        specs={2: one(atmos_state.shape, 1)},
-        out_specs={0: one(entry.main().shape)},
+        steps=faces // half,
+        specs={2: some(half, atmos_state.shape, 1)},
+        out_specs={0: some(half, entry.main().shape)},
         name="prep",
     )
     got = swap_chunks(send)
@@ -712,9 +732,9 @@
         full.send_scratch() + entry.halo_scratch() + ends,
         2 * cells * 9 * in_ch * width,
         smem=2,
-        steps=faces,
-        specs={2: one(x0.shape)},
-        out_specs={0: one(full.main().shape)},
+        steps=faces // few,
+        specs={2: some(few, x0.shape)},
+        out_specs={0: some(few, full.main().shape)},
         name="conv_in",
     )
     got = swap_chunks(send)
@@ -726,9 +746,9 @@
         full.send_scratch() + low.send_scratch() + full.halo_scratch() + ends,
         2 * cells * 9 * width * width,
         smem=2,
-        steps=faces,
-        specs={2: one(x1.shape)},
-        out_specs={0: one(full.main().shape), 1: one(low.main().shape)},
+        steps=faces // few,
+        specs={2: some(few, x1.shape)},
+        out_specs={0: some(few, full.main().shape), 1: some(few, low.main().shape)},
         name="encode",
     )
     low_got = swap_chunks(low_send)
@@ -740,9 +760,9 @@
         low.send_scratch() + low.halo_scratch() + ends,
         10e9,
         smem=2,
-        steps=faces,
-        specs={2: one(y0.shape)},
-        out_specs={0: one(low.main().shape)},
+        steps=faces // many,
+        specs={2: some(many, y0.shape)},
+        out_specs={0: some(many, low.main().shape)},
         name="coarse",
     )
     low_send, got = lax.optimization_barrier((low_send, swap_chunks(send)))
@@ -786,14 +806,14 @@
         + ends,
         2 * cells * 18 * width * width,
         smem=2,
-        steps=faces,
+        steps=faces // few,
         specs={
-            2: one(x2.shape),
-            9: one(y1.shape),
-            20: pl.BlockSpec((OUT_VARS, 1, rows, side), lambda i: (0, i, 0, 0)),
-            21: one(land_sea.shape),
+            2: some(few, x2.shape),
+            9: some(few, y1.shape),
+            20: pl.BlockSpec((OUT_VARS, few, rows, side), lambda i: (0, i, 0, 0)),
+            21: some(few, land_sea.shape),
         },
-        out_specs={0: one((OUT_VARS, faces, rows, side), 1)},
+        out_specs={0: some(few, (OUT_VARS, faces, rows, side), 1)},
         name="decode",
     )
     arrived = lax.all_to_all(outgoing, "tile", split_axis=0, concat_axis=0, tiled=True)

time: 237 us -> 231 us (0.975)
  Pallas kernels: 103 us -> 96.2 us
    pallas_call x7, Pallas kernels: 103 us -> 96.2 us  [call(): pl.pallas_call(kernel, out_shape=outs, **grid, in_specs=in_specs, out_spe...]
  transfers between devices with their start and end apart: 15 -> 15, of which waited for: 10 -> 10; matrix products, arithmetic and copies ran while one was open for 7% -> 7% of each run, Pallas kernels for 6% -> 5%
where the time goes in v5:
time: 231 us; the launch traced here: 230 us
  Pallas kernels  96.2 us (42%)
  waiting for transfers between devices  64.5 us (28%)
  starting transfers between devices  45 us (19%)
  local copies, waits for them, and re-layouts  20.7 us (9%)
  other arithmetic  2.52 us (1%)
    pallas_call x7, Pallas kernels, call(): pl.pallas_call(kernel, out_shape=outs, **grid, in_specs=in_specs, out_spe...  96.2 us
    ppermute x4, waiting for transfers between devices, swap_rows(): up = lax.ppermute(bot, 'tile', ring)  28.4 us
    ppermute x4, starting transfers between devices, swap_rows(): return (up, lax.ppermute(top, 'tile', [(j, i) for i, j in ring]))  20.6 us
    all_to_all x5, waiting for transfers between devices, swap_chunks(): lax.all_to_all(chunks, 'tile', split_axis=0, concat_axis=0, tiled=True)  20.5 us
    all_to_all x5, starting transfers between devices, swap_chunks(): lax.all_to_all(chunks, 'tile', split_axis=0, concat_axis=0, tiled=True)  18.3 us
    all_to_all x1, waiting for transfers between devices, on_one_group(): lax.all_to_all(outgoing, 'tile', split_axis=0, concat_axis=0, tiled=True)  10.2 us
    unnamed x53, local copies, waits for them, and re-layouts  7.81 us
    all_to_all x1, waiting for transfers between devices, on_one_group(): lax.all_to_all(back, 'tile', split_axis=0, concat_axis=0, tiled=True)  5.43 us
  transfers between devices with their start and end apart: 15, of which 10 were waited for; matrix products, arithmetic and copies ran while one was open for 7% of the time, Pallas kernels for 5%

profile of v5, /device:TPU:0, one launch (start us, length us, event | category | flops | bytes accessed | tf_op | source)
XLA Modules:
  0.0 230.1 jit_solution(7455829184946954640)
XLA Ops:
  0.6 1.4 copy.197.tab
  2.0 7.3 %prep.1 = (bf16[12,8,32,256]{3,2,1,0:T(8,128)(2,1)}, bf16[12,32,256]{2,1,0:T(8,128)(2,1)}, bf16[12,32,256]{2,1,0:T(8,128)(2,1)}, bf16[192,32]{1,0:T(8,128)(2,1)}, bf16[32,48,128]{2,1,0:T(8,128)(2,1)}) custom-call(s32[1]{0:T(128)} %bitcast.stripe_ref, s32[48,2]{1,0:T(8,128)} %copy.197.tab, bf16[32,12,8,256]{3,2,1,0:T(8,128)(2,1)} %atmos.3, ...), custom_call_target="tpu_custom_call" | custom-call | flops 402653184 | bytes 4075908 | tf_op jit(solution)/shard_map/prep/pallas_call | solution.py:643
  9.3 6.7 %all-to-all-start = ((bf16[32,48,128]{2,1,0:T(8,128)(2,1)}), bf16[32,48,128]{2,1,0:T(8,128)(2,1)S(1)}, u32[]{:S(2)}, u32[]{:S(2)}) async-start(bf16[32,48,128]{2,1,0:T(8,128)(2,1)} %get-tuple-element.35), calls=%async_computation | async-start | bytes 786432 | tf_op jit(solution)/shard_map/all_to_all | solution.py:665
  16.1 0.3 collective-permute-start
  16.4 5.1 %collective-permute-start.1 = (bf16[12,32,256]{2,1,0:T(8,128)(2,1)}, bf16[12,32,256]{2,1,0:T(8,128)(2,1)S(1)}, u32[]{:S(2)}, u32[]{:S(2)}) collective-permute-start(bf16[12,32,256]{2,1,0:T(8,128)(2,1)} %get-tuple-element.32.old_top), channel_id=1, source_target_pairs={{1,0},{2,1},{3,2},{4,3},{5,4},{6,5},{7,6},{8,7},{9,8},{10,9},{11,1... | collective-permute-start | bytes 589832 | tf_op jit(solution)/shard_map/ppermute | solution.py:661
  21.5 0.9 copy.177
  22.6 0.7 copy.183.side_weight
  23.6 0.7 copy.182.weight
  24.3 6.8 %collective-permute-done.up = bf16[12,32,256]{2,1,0:T(8,128)(2,1)S(1)} collective-permute-done((bf16[12,32,256]{2,1,0:T(8,128)(2,1)}, bf16[12,32,256]{2,1,0:T(8,128)(2,1)S(1)}, u32[]{:S(2)}, u32[]{:S(2)}) %collective-permute-start) | collective-permute-done | bytes 196640 | tf_op jit(solution)/shard_map/ppermute | solution.py:660
  31.1 0.3 all-to-all-done.recv
  31.3 0.4 copy-done.21
  31.8 0.3 copy-done.7
  32.1 15.6 %conv_in.1 = (bf16[12,8,64,256]{3,2,1,0:T(8,128)(2,1)}, bf16[12,64,256]{2,1,0:T(8,128)(2,1)}, bf16[12,64,256]{2,1,0:T(8,128)(2,1)}, bf16[192,64]{1,0:T(8,128)(2,1)}, bf16[32,96,128]{2,1,0:T(8,128)(2,1)}) custom-call(s32[1]{0:T(128)} %bitcast.stripe_ref, s32[48,2]{1,0:T(8,128)} %copy.197.tab, bf16[12,8,32,256]{3,2,1,0:T(8,128)(2,1)} %get-tuple-element.31.x, ...), custom_call_target="tpu_custom_call" | custom-call | flops 905969664 | bytes 7569796 | tf_op jit(solution)/shard_map/conv_in/pallas_call | solution.py:643
  47.7 2.6 %all-to-all-start.1 = ((bf16[32,96,128]{2,1,0:T(8,128)(2,1)}), bf16[32,96,128]{2,1,0:T(8,128)(2,1)S(1)}, u32[]{:S(2)}, u32[]{:S(2)}) async-start(bf16[32,96,128]{2,1,0:T(8,128)(2,1)} %get-tuple-element.40), calls=%async_computation.1 | async-start | bytes 1572864 | tf_op jit(solution)/shard_map/all_to_all | solution.py:665
  50.3 0.2 collective-permute-start.2
  50.5 5.2 %collective-permute-start.3 = (bf16[12,64,256]{2,1,0:T(8,128)(2,1)}, bf16[12,64,256]{2,1,0:T(8,128)(2,1)S(1)}, u32[]{:S(2)}, u32[]{:S(2)}) collective-permute-start(bf16[12,64,256]{2,1,0:T(8,128)(2,1)} %get-tuple-element.37.old_top), channel_id=1, source_target_pairs={{1,0},{2,1},{3,2},{4,3},{5,4},{6,5},{7,6},{8,7},{9,8},{10,9},{11,1... | collective-permute-start | bytes 1179656 | tf_op jit(solution)/shard_map/ppermute | solution.py:661
  55.7 0.2 copy.184
  56.1 0.2 copy.185
  56.3 0.8 reshape.149.weight
  57.1 0.7 pad_maximum_fusion.1.side_weight
  57.7 16.3 %collective-permute-done.2.up = bf16[12,64,256]{2,1,0:T(8,128)(2,1)S(1)} collective-permute-done((bf16[12,64,256]{2,1,0:T(8,128)(2,1)}, bf16[12,64,256]{2,1,0:T(8,128)(2,1)S(1)}, u32[]{:S(2)}, u32[]{:S(2)}) %collective-permute-start.2) | collective-permute-done | bytes 393248 | tf_op jit(solution)/shard_map/ppermute | solution.py:660
  74.0 0.9 all-to-all-done.1.recv
  74.9 1.0 copy-done.3
  75.9 25.6 %encode.1 = (bf16[12,8,64,256]{3,2,1,0:T(8,128)(2,1)}, bf16[12,4,64,128]{3,2,1,0:T(8,128)(2,1)}, bf16[12,64,384]{2,1,0:T(8,128)(2,1)}, bf16[12,64,384]{2,1,0:T(8...) custom-call(s32[1]{0:T(128)} %bitcast.stripe_ref, ...), custom_call_target="tpu_custom_call" | custom-call | flops 1811939328 | bytes 12059012 | tf_op jit(solution)/shard_map/encode/pallas_call | solution.py:643
  101.6 2.7 %all-to-all-start.2 = ((bf16[32,48,128]{2,1,0:T(8,128)(2,1)}), bf16[32,48,128]{2,1,0:T(8,128)(2,1)S(1)}, u32[]{:S(2)}, u32[]{:S(2)}) async-start(bf16[32,48,128]{2,1,0:T(8,128)(2,1)} %get-tuple-element.47), calls=%async_computation.2 | async-start | bytes 786432 | tf_op jit(solution)/shard_map/all_to_all | solution.py:665
  104.3 0.2 copy.189
  104.5 0.2 convert_reduce_fusion
  104.7 0.2 collective-permute-start.4
  104.9 5.2 %collective-permute-start.5 = (bf16[12,64,384]{2,1,0:T(8,128)(2,1)}, bf16[12,64,384]{2,1,0:T(8,128)(2,1)}, u32[]{:S(2)}, u32[]{:S(2)}) collective-permute-start(bf16[12,64,384]{2,1,0:T(8,128)(2,1)} %get-tuple-element.42.old_top.top), channel_id=1, source_target_pairs={{1,0},{2,1},{3,2},{4,3},{5,4},{6,5},{7,6},{8,7},{9,8},{10,9},{11,1... | collective-permute-start | bytes 1769480 | tf_op jit(solution)/shard_map/ppermute | solution.py:661
  110.1 13.7 %all-to-all-done.2.recv = bf16[32,48,128]{2,1,0:T(8,128)(2,1)S(1)} async-done(((bf16[32,48,128]{2,1,0:T(8,128)(2,1)}), bf16[32,48,128]{2,1,0:T(8,128)(2,1)S(1)}, u32[]{:S(2)}, u32[]{:S(2)}) %all-to-all-start.2) | async-done | bytes 393248 | tf_op jit(solution)/shard_map/all_to_all | solution.py:665
  123.8 2.6 %all-to-all-start.3 = ((bf16[32,96,128]{2,1,0:T(8,128)(2,1)}), bf16[32,96,128]{2,1,0:T(8,128)(2,1)S(1)}, u32[]{:S(2)}, u32[]{:S(2)}) async-start(bf16[32,96,128]{2,1,0:T(8,128)(2,1)} %get-tuple-element.49), calls=%async_computation.3 | async-start | bytes 1572864 | tf_op jit(solution)/shard_map/all_to_all | solution.py:665
  126.7 0.2 copy.190
  126.8 0.8 reshape.151.weight
  127.6 0.2 reshape.152
  127.8 0.7 pad_maximum_fusion.2.side_weight
  128.6 0.8 copy-done.16
  129.4 12.3 %coarse.1 = (bf16[12,4,64,128]{3,2,1,0:T(8,128)(2,1)}, bf16[12,64,128]{2,1,0:T(8,128)(2,1)}, bf16[12,64,128]{2,1,0:T(8,128)(2,1)}, bf16[192,64]{1,0:T(8,128)(2,1)}, bf16[32,48,128]{2,1,0:T(8,128)(2,1)}) custom-call(s32[1]{0:T(128)} %bitcast.stripe_ref, s32[48,2]{1,0:T(8,128)} %copy.197.tab, bf16[12,4,64,128]{3,2,1,0:T(8,128)(2,1)} %get-tuple-element.45.x, ...), custom_call_target="tpu_custom_call" | custom-call | flops 10000000000 | bytes 5284228 | tf_op jit(solution)/shard_map/coarse/pallas_call | solution.py:643
  141.7 5.3 %all-to-all-done.3.recv = bf16[32,96,128]{2,1,0:T(8,128)(2,1)S(1)} async-done(((bf16[32,96,128]{2,1,0:T(8,128)(2,1)}), bf16[32,96,128]{2,1,0:T(8,128)(2,1)S(1)}, u32[]{:S(2)}, u32[]{:S(2)}) %all-to-all-start.3) | async-done | bytes 786464 | tf_op jit(solution)/shard_map/all_to_all | solution.py:665
  147.0 3.5 %all-to-all-start.4 = ((bf16[32,48,128]{2,1,0:T(8,128)(2,1)}), bf16[32,48,128]{2,1,0:T(8,128)(2,1)S(1)}, u32[]{:S(2)}, u32[]{:S(2)}) async-start(bf16[32,48,128]{2,1,0:T(8,128)(2,1)} %get-tuple-element.55), calls=%async_computation.4 | async-start | bytes 786432 | tf_op jit(solution)/shard_map/all_to_all | solution.py:665
  150.7 0.3 collective-permute-start.6
  151.1 5.1 %collective-permute-start.7 = (bf16[12,64,128]{2,1,0:T(8,128)(2,1)}, bf16[12,64,128]{2,1,0:T(8,128)(2,1)S(1)}, u32[]{:S(2)}, u32[]{:S(2)}) collective-permute-start(bf16[12,64,128]{2,1,0:T(8,128)(2,1)} %get-tuple-element.52.low_top), channel_id=1, source_target_pairs={{1,0},{2,1},{3,2},{4,3},{5,4},{6,5},{7,6},{8,7},{9,8},{10,9},{11,1... | collective-permute-start | bytes 589832 | tf_op jit(solution)/shard_map/ppermute | solution.py:661
  156.2 0.4 copy.211
  157.1 1.0 reshape.153.weight
  158.1 0.7 add.47.col_key
  158.8 0.8 mul.112.head
  159.6 0.7 pad_maximum_fusion.3.side_weight
  160.3 5.3 %collective-permute-done.6.yup = bf16[12,64,128]{2,1,0:T(8,128)(2,1)S(1)} collective-permute-done((bf16[12,64,128]{2,1,0:T(8,128)(2,1)}, bf16[12,64,128]{2,1,0:T(8,128)(2,1)S(1)}, u32[]{:S(2)}, u32[]{:S(2)}) %collective-permute-start.6) | collective-permute-done | bytes 196640 | tf_op jit(solution)/shard_map/ppermute | solution.py:660
  165.6 0.3 all-to-all-done.4.yrecv
  165.9 0.4 copy-done.19
  166.3 0.3 copy-done.5
  166.6 22.4 %decode.1 = (bf16[8,12,8,256]{3,2,1,0:T(8,128)(2,1)}, bf16[32,24,256]{2,1,0:T(8,128)(2,1)}) custom-call(s32[1]{0:T(128)} %bitcast.stripe_ref, s32[48,2]{1,0:T(8,128)} %copy.197.tab, bf16[12,8,64,256]{3,2,1,0:T(8,128)(2,1)} %get-tuple-element.41.x, bf16[12,64,384]{2,1,0:T(8,128)(2,1)} %get-tuple-element.42.old_top.top, ...), custom_call_target="tpu_custom_call" | custom-call | flops 3623878656 | bytes 11178884 | tf_op jit(solution)/shard_map/decode/pallas_call | solution.py:643
  189.0 2.6 %all-to-all-start.5 = ((bf16[32,24,256]{2,1,0:T(8,128)(2,1)}), bf16[32,24,256]{2,1,0:T(8,128)(2,1)S(1)}, u32[]{:S(2)}, u32[]{:S(2)}) async-start(bf16[32,24,256]{2,1,0:T(8,128)(2,1)} %get-tuple-element.56), calls=%async_computation.5 | async-start | bytes 786432 | tf_op jit(solution)/shard_map/all_to_all | solution.py:819
  192.9 0.8 concatenate.8.into
  193.8 0.8 pad_bitcast_fusion.state
  194.6 10.2 %all-to-all-done.5.recv = bf16[32,24,256]{2,1,0:T(8,128)(2,1)S(1)} async-done(((bf16[32,24,256]{2,1,0:T(8,128)(2,1)}), bf16[32,24,256]{2,1,0:T(8,128)(2,1)S(1)}, u32[]{:S(2)}, u32[]{:S(2)}) %all-to-all-start.5) | async-done | bytes 393248 | tf_op jit(solution)/shard_map/all_to_all | solution.py:819
  204.8 0.8 broadcast_in_dim.8.out_weight
  205.6 11.2 %ocean.1 = (f32[32,8,256]{2,1,0:T(8,128)}, bf16[32,8,256]{2,1,0:T(8,128)(2,1)}) custom-call(bf16[32,24,256]{2,1,0:T(8,128)(2,1)} %copy-done, f32[32,16,256]{2,1,0:T(8,128)} %pad_bitcast_fusion.state, bf16[384,112]{1,0:T(8,128)(2,1)} %concatenate.8.into, f32[384,128]{1,0:T(8,128)} %broadcast_in_dim.8.out_weight), custom_call_target="tpu_custom_call" | custom-call | flops 50331648 | bytes 1593344 | tf_op jit(solution)/shard_map/ocean/pallas_call | solution.py:643
  216.8 2.6 %all-to-all-start.6 = ((bf16[32,8,256]{2,1,0:T(8,128)(2,1)}), bf16[32,8,256]{2,1,0:T(8,128)(2,1)S(1)}, u32[]{:S(2)}, u32[]{:S(2)}) async-start(bf16[32,8,256]{2,1,0:T(8,128)(2,1)} %get-tuple-element.57), calls=%async_computation.6 | async-start | bytes 262144 | tf_op jit(solution)/shard_map/all_to_all | solution.py:850
  219.4 0.7 copy.204.key
  220.1 1.0 stack.48
  221.1 1.1 copy.206
  222.2 5.4 %all-to-all-done.6.back = bf16[32,8,256]{2,1,0:T(8,128)(2,1)S(1)} async-done(((bf16[32,8,256]{2,1,0:T(8,128)(2,1)}), bf16[32,8,256]{2,1,0:T(8,128)(2,1)S(1)}, u32[]{:S(2)}, u32[]{:S(2)}) %all-to-all-start.6) | async-done | bytes 131104 | tf_op jit(solution)/shard_map/all_to_all | solution.py:850
  227.6 0.7 copy-done.4
  228.3 1.8 surface.1
  (92 shorter events, 3.1 us)
Async XLA Ops:
  9.3 22.0 %all-to-all-start = ((bf16[32,48,128]{2,1,0:T(8,128)(2,1)}), bf16[32,48,128]{2,1,0:T(8,128)(2,1)S(1)}, u32[]{:S(2)}, u32[]{:S(2)}) async-start(bf16[32,48,128]{2,1,0:T(8,128)(2,1)} %get-tuple-element.35), calls=%async_computation | async-start | bytes 786432 | tf_op jit(solution)/shard_map/all_to_all | solution.py:665
  16.1 39.6 %copy-start.9 = (bf16[3,64,192]{2,1,0:T(8,128)(2,1)S(1)}, bf16[3,64,192]{2,1,0:T(8,128)(2,1)}, u32[]{:S(2)}) copy-start(bf16[3,64,192]{2,1,0:T(8,128)(2,1)} %param.24) | copy-start | bytes 221188
  16.1 15.0 %collective-permute-start = (bf16[12,32,256]{2,1,0:T(8,128)(2,1)}, bf16[12,32,256]{2,1,0:T(8,128)(2,1)S(1)}, u32[]{:S(2)}, u32[]{:S(2)}) collective-permute-start(bf16[12,32,256]{2,1,0:T(8,128)(2,1)} %get-tuple-element.33.old_bot), channel_id=1, source_target_pairs={{0,1},{1,2},{2,3},{3,4},{4,5},{5,6},{6,7},{7,8},{8,9},{9,10},{10,1... | collective-permute-start | bytes 589832 | tf_op jit(solution)/shard_map/ppermute | solution.py:660
  16.4 14.7 %collective-permute-start.1 = (bf16[12,32,256]{2,1,0:T(8,128)(2,1)}, bf16[12,32,256]{2,1,0:T(8,128)(2,1)S(1)}, u32[]{:S(2)}, u32[]{:S(2)}) collective-permute-start(bf16[12,32,256]{2,1,0:T(8,128)(2,1)} %get-tuple-element.32.old_top), channel_id=1, source_target_pairs={{1,0},{2,1},{3,2},{4,3},{5,4},{6,5},{7,6},{8,7},{9,8},{10,9},{11,1... | collective-permute-start | bytes 589832 | tf_op jit(solution)/shard_map/ppermute | solution.py:661
  31.1 0.7 copy-start.21
  31.1 0.7 copy-start.22
  31.3 0.7 copy-start.7
  47.7 27.2 %all-to-all-start.1 = ((bf16[32,96,128]{2,1,0:T(8,128)(2,1)}), bf16[32,96,128]{2,1,0:T(8,128)(2,1)S(1)}, u32[]{:S(2)}, u32[]{:S(2)}) async-start(bf16[32,96,128]{2,1,0:T(8,128)(2,1)} %get-tuple-element.40), calls=%async_computation.1 | async-start | bytes 1572864 | tf_op jit(solution)/shard_map/all_to_all | solution.py:665
  50.3 23.7 %collective-permute-start.2 = (bf16[12,64,256]{2,1,0:T(8,128)(2,1)}, bf16[12,64,256]{2,1,0:T(8,128)(2,1)S(1)}, u32[]{:S(2)}, u32[]{:S(2)}) collective-permute-start(bf16[12,64,256]{2,1,0:T(8,128)(2,1)} %get-tuple-element.38.old_bot), channel_id=1, source_target_pairs={{0,1},{1,2},{2,3},{3,4},{4,5},{5,6},{6,7},{7,8},{8,9},{9,10},{10,1... | collective-permute-start | bytes 1179656 | tf_op jit(solution)/shard_map/ppermute | solution.py:660
  50.5 23.5 %collective-permute-start.3 = (bf16[12,64,256]{2,1,0:T(8,128)(2,1)}, bf16[12,64,256]{2,1,0:T(8,128)(2,1)S(1)}, u32[]{:S(2)}, u32[]{:S(2)}) collective-permute-start(bf16[12,64,256]{2,1,0:T(8,128)(2,1)} %get-tuple-element.37.old_top), channel_id=1, source_target_pairs={{1,0},{2,1},{3,2},{4,3},{5,4},{6,5},{7,6},{8,7},{9,8},{10,9},{11,1... | collective-permute-start | bytes 1179656 | tf_op jit(solution)/shard_map/ppermute | solution.py:661
  74.0 0.9 copy-start.17
  74.0 0.9 copy-start.18
  74.9 1.0 copy-start.3
  75.9 28.4 %copy-start.10 = (bf16[3,64,192]{2,1,0:T(8,128)(2,1)S(1)}, bf16[3,64,192]{2,1,0:T(8,128)(2,1)}, u32[]{:S(2)}) copy-start(bf16[3,64,192]{2,1,0:T(8,128)(2,1)} %param.25) | copy-start | bytes 221188
  75.9 28.6 %copy-start.11 = (pred[96,96]{1,0:T(32,128)(4,1)S(1)}, pred[96,96]{1,0:T(32,128)(4,1)}, u32[]{:S(2)}) copy-start(pred[96,96]{1,0:T(32,128)(4,1)} %constant.29.clone) | copy-start | bytes 27652
  75.9 28.6 %copy-start.14 = (s32[96,1]{0,1:T(1,128)S(1)}, s32[96,1]{0,1:T(1,128)}, u32[]{:S(2)}) copy-start(s32[96,1]{0,1:T(1,128)} %param.20) | copy-start | bytes 1156
  101.5 26.1 %copy-start.8 = (bf16[3,64,384]{2,1,0:T(8,128)(2,1)S(1)}, bf16[3,64,384]{2,1,0:T(8,128)(2,1)}, u32[]{:S(2)}) copy-start(bf16[3,64,384]{2,1,0:T(8,128)(2,1)} %param.26) | copy-start | bytes 442372
  101.5 27.0 %copy-start.13 = (f32[64,6]{0,1:T(8,128)S(1)}, f32[64,6]{0,1:T(8,128)}, u32[]{:S(2)}) copy-start(f32[64,6]{0,1:T(8,128)} %param.28) | copy-start | bytes 4612
  101.5 26.9 %copy-start.12 = (bf16[12,64]{1,0:T(8,128)(2,1)S(1)}, bf16[12,64]{1,0:T(8,128)(2,1)}, u32[]{:S(2)}) copy-start(bf16[12,64]{1,0:T(8,128)(2,1)} %param.27) | copy-start | bytes 4612
  101.6 22.3 %all-to-all-start.2 = ((bf16[32,48,128]{2,1,0:T(8,128)(2,1)}), bf16[32,48,128]{2,1,0:T(8,128)(2,1)S(1)}, u32[]{:S(2)}, u32[]{:S(2)}) async-start(bf16[32,48,128]{2,1,0:T(8,128)(2,1)} %get-tuple-element.47), calls=%async_computation.2 | async-start | bytes 786432 | tf_op jit(solution)/shard_map/all_to_all | solution.py:665
  104.7 23.9 %collective-permute-start.4 = (bf16[12,64,384]{2,1,0:T(8,128)(2,1)}, bf16[12,64,384]{2,1,0:T(8,128)(2,1)S(1)}, u32[]{:S(2)}, u32[]{:S(2)}) collective-permute-start(bf16[12,64,384]{2,1,0:T(8,128)(2,1)} %get-tuple-element.43.old_bot.bot), channel_id=1, source_target_pairs={{0,1},{1,2},{2,3},{3,4},{4,5},{5,6},{6,7},{7,8},{8,9},{9,10},{10,1... | collective-permute-start | bytes 1769480 | tf_op jit(solution)/shard_map/ppermute | solution.py:660
  104.9 23.7 %collective-permute-start.5 = (bf16[12,64,384]{2,1,0:T(8,128)(2,1)}, bf16[12,64,384]{2,1,0:T(8,128)(2,1)}, u32[]{:S(2)}, u32[]{:S(2)}) collective-permute-start(bf16[12,64,384]{2,1,0:T(8,128)(2,1)} %get-tuple-element.42.old_top.top), channel_id=1, source_target_pairs={{1,0},{2,1},{3,2},{4,3},{5,4},{6,5},{7,6},{8,7},{9,8},{10,9},{11,1... | collective-permute-start | bytes 1769480 | tf_op jit(solution)/shard_map/ppermute | solution.py:661
  123.8 4.8 %copy-start.6 = (bf16[32,48,128]{2,1,0:T(8,128)(2,1)}, bf16[32,48,128]{2,1,0:T(8,128)(2,1)S(1)}, u32[]{:S(2)}) copy-start(bf16[32,48,128]{2,1,0:T(8,128)(2,1)S(1)} %all-to-all-done.2.recv) | copy-start | bytes 1179652
  123.8 23.2 %all-to-all-start.3 = ((bf16[32,96,128]{2,1,0:T(8,128)(2,1)}), bf16[32,96,128]{2,1,0:T(8,128)(2,1)S(1)}, u32[]{:S(2)}, u32[]{:S(2)}) async-start(bf16[32,96,128]{2,1,0:T(8,128)(2,1)} %get-tuple-element.49), calls=%async_computation.3 | async-start | bytes 1572864 | tf_op jit(solution)/shard_map/all_to_all | solution.py:665
  128.6 0.8 copy-start.16
  129.4 27.3 %copy-start.1 = (f32[1,1,192,2,256]{4,3,2,1,0:T(2,128)S(1)}, f32[1,1,192,2,256]{4,3,2,1,0:T(2,128)}, u32[]{:S(2)}) copy-start(f32[1,1,192,2,256]{4,3,2,1,0:T(2,128)} %param.22) | copy-start | bytes 1179652
  147.0 18.8 %copy-start.2 = (bf16[32,96,128]{2,1,0:T(8,128)(2,1)}, bf16[32,96,128]{2,1,0:T(8,128)(2,1)S(1)}, u32[]{:S(2)}) copy-start(bf16[32,96,128]{2,1,0:T(8,128)(2,1)S(1)} %all-to-all-done.3.recv) | copy-start | bytes 2359300
  147.0 18.8 %all-to-all-start.4 = ((bf16[32,48,128]{2,1,0:T(8,128)(2,1)}), bf16[32,48,128]{2,1,0:T(8,128)(2,1)S(1)}, u32[]{:S(2)}, u32[]{:S(2)}) async-start(bf16[32,48,128]{2,1,0:T(8,128)(2,1)} %get-tuple-element.55), calls=%async_computation.4 | async-start | bytes 786432 | tf_op jit(solution)/shard_map/all_to_all | solution.py:665
  150.7 14.8 %collective-permute-start.6 = (bf16[12,64,128]{2,1,0:T(8,128)(2,1)}, bf16[12,64,128]{2,1,0:T(8,128)(2,1)S(1)}, u32[]{:S(2)}, u32[]{:S(2)}) collective-permute-start(bf16[12,64,128]{2,1,0:T(8,128)(2,1)} %get-tuple-element.53.low_bot), channel_id=1, source_target_pairs={{0,1},{1,2},{2,3},{3,4},{4,5},{5,6},{6,7},{7,8},{8,9},{9,10},{10,1... | collective-permute-start | bytes 589832 | tf_op jit(solution)/shard_map/ppermute | solution.py:660
  151.1 14.5 %collective-permute-start.7 = (bf16[12,64,128]{2,1,0:T(8,128)(2,1)}, bf16[12,64,128]{2,1,0:T(8,128)(2,1)S(1)}, u32[]{:S(2)}, u32[]{:S(2)}) collective-permute-start(bf16[12,64,128]{2,1,0:T(8,128)(2,1)} %get-tuple-element.52.low_top), channel_id=1, source_target_pairs={{1,0},{2,1},{3,2},{4,3},{5,4},{6,5},{7,6},{8,7},{9,8},{10,9},{11,1... | collective-permute-start | bytes 589832 | tf_op jit(solution)/shard_map/ppermute | solution.py:661
  165.6 0.7 copy-start.19
  165.6 0.7 copy-start.20
  165.9 0.7 copy-start.5
  166.6 26.2 %copy-start.15 = (f32[64]{0:T(128)S(1)}, f32[64]{0:T(128)}, u32[]{:S(2)}) copy-start(f32[64]{0:T(128)} %param.29) | copy-start | bytes 772
  189.0 15.8 %all-to-all-start.5 = ((bf16[32,24,256]{2,1,0:T(8,128)(2,1)}), bf16[32,24,256]{2,1,0:T(8,128)(2,1)S(1)}, u32[]{:S(2)}, u32[]{:S(2)}) async-start(bf16[32,24,256]{2,1,0:T(8,128)(2,1)} %get-tuple-element.56), calls=%async_computation.5 | async-start | bytes 786432 | tf_op jit(solution)/shard_map/all_to_all | solution.py:819
  204.8 0.8 copy-start
  216.8 10.8 %all-to-all-start.6 = ((bf16[32,8,256]{2,1,0:T(8,128)(2,1)}), bf16[32,8,256]{2,1,0:T(8,128)(2,1)S(1)}, u32[]{:S(2)}, u32[]{:S(2)}) async-start(bf16[32,8,256]{2,1,0:T(8,128)(2,1)} %get-tuple-element.57), calls=%async_computation.6 | async-start | bytes 262144 | tf_op jit(solution)/shard_map/all_to_all | solution.py:850
  227.6 0.7 copy-start.4

commit v6 on v5

--- a/solution.py
+++ b/solution.py
@@ -240,6 +240,7 @@
             pltpu.VMEM((self.tiles, self.chunk, LANES), F32),
             pltpu.VMEM((self.side + 8, LANES), F32),
             pltpu.VMEM((16, self.rows * self.side), BF),
+            pltpu.VMEM((2, self.side, self.side), BF),
         ]
 
     def halo_scratch(self):
@@ -251,12 +252,15 @@
             pltpu.VMEM((2, self.faces, self.chans, self.side), BF),
             pltpu.VMEM((self.tiles, self.chunk, LANES), F32),
             pltpu.VMEM((2, self.faces, 8, self.chans), F32),
+            pltpu.VMEM((2, self.side, self.side), BF),
         ]
 
 
-def flip_matrix(size, flag):
+def fill_flips(flips):
+    size = flips.shape[1]
     row, col = iota((size, size), 0), iota((size, size), 1)
-    return (row == jnp.where(flag == 1, size - 1 - col, col)).astype(F32).astype(BF)
+    flips[0] = (row == col).astype(F32).astype(BF)
+    flips[1] = (row + col == size - 1).astype(F32).astype(BF)
 
 
 def end_picker(side):
@@ -277,7 +281,7 @@
     cols[1, f] = picked[8:]
 
 
-def pack_sends(fld, stripe, tab, top, bot, off, ec_out, send_out, cols, stage, strip, picker):
+def pack_sends(fld, stripe, tab, top, bot, off, ec_out, send_out, cols, stage, strip, picker, flips):
     last, rows, chans, groups, per = fld.tiles - 1, fld.rows, fld.chans, fld.groups, fld.per
     held = cols[...]
     ec_out[...] = held.reshape(2 * fld.faces * 8, chans).astype(BF)
@@ -303,13 +307,14 @@
     @pl.when((stripe == 0) | (stripe == last))
     def _():
         q = jnp.where(stripe == 0, 0, 1)
+        fill_flips(flips)
         for i in range(groups):
             turned = []
             for h in range(i * per, (i + 1) * per):
                 upper = top[h, :, off : off + fld.side].astype(F32)
                 lower = bot[h, :, off : off + fld.side].astype(F32)
                 cells = jnp.where(q == 0, upper, lower).astype(BF)
-                turned.append(mm_nt(flip_matrix(fld.side, tab[4 * h + q, 1]), cells))
+                turned.append(mm_nt(flips[tab[4 * h + q, 1]], cells))
             strip[0:8] = jnp.zeros((8, LANES), F32)
             strip[fld.side : fld.side + 8] = jnp.zeros((8, LANES), F32)
             strip[1 : fld.side + 1, :] = jnp.concatenate(turned, axis=1)
@@ -332,7 +337,7 @@
     send_out[...] = stage[...].astype(BF)
 
 
-def gather_halos(fld, stripe, tab, top, bot, up, dn, off, ec, recv, cand, cols, above, below, pair, got, mirror):
+def gather_halos(fld, stripe, tab, top, bot, up, dn, off, ec, recv, cand, cols, above, below, pair, got, mirror, flips):
     faces, rows, chans, side, tiles = fld.faces, fld.rows, fld.chans, fld.side, fld.tiles
     last = tiles - 1
     groups = fld.groups
@@ -377,6 +382,7 @@
     @pl.when(at_edge)
     def _():
         q = jnp.where(stripe == 0, 0, 1)
+        fill_flips(flips)
         for h in range(faces):
             pair[0, h] = jnp.where(q == 0, top[h, :, here].astype(F32), below[h].astype(F32)).astype(BF)
             pair[1, h] = jnp.where(q == 0, above[h].astype(F32), bot[h, :, here].astype(F32)).astype(BF)
@@ -410,7 +416,7 @@
                 near = pair[jnp.minimum(kind, 1), h].astype(F32)
                 far = lined[j * chans : (j + 1) * chans]
                 cells = jnp.where(kind < 2, near, far).astype(BF)
-                placed = mm(cells, flip_matrix(side, tab[4 * g + q, 1])).astype(BF)
+                placed = mm(cells, flips[tab[4 * g + q, 1]]).astype(BF)
 
                 @pl.when(q == 0)
                 def _():
@@ -506,10 +512,10 @@
 def level_kernel(fld, out_fld, low, off, stripe_ref, tab, x, old_top, old_bot, up, dn, ec, recv, weight, side_weight, *refs):
     stripe, step = stripe_ref[0], pl.program_id(0)
     if low is None:
-        outs, sends, halos = refs[:5], refs[5:9], refs[9:]
+        outs, sends, halos = refs[:5], refs[5:10], refs[10:]
         x_out, top, bot, ec_out, send_out = outs
     else:
-        pool, outs, sends, low_sends, halos = refs[0], refs[1:9], refs[9:13], refs[13:17], refs[17:]
+        pool, outs, sends, low_sends, halos = refs[0], refs[1:9], refs[9:14], refs[14:19], refs[19:]
         x_out, y_out, top, bot, ec_out, send_out, low_ec, low_send = outs
     *halos, ends_ref = halos
     batch = x_out.shape[0]
@@ -557,7 +563,7 @@
 
 
 def decode_kernel(fld, low, out_ch, vars_out, stripe_ref, tab, x, top, bot, up, dn, ec, recv, y, low_top, low_bot, yup, ydn, yec, yrecv, weight, side_weight, spread, head, atmos, land, row_key, col_key, pred_out, flux_out, *refs):
-    halos, low_halos, flux, ends_ref = refs[:7], refs[7:14], refs[14], refs[15]
+    halos, low_halos, flux, ends_ref = refs[:8], refs[8:16], refs[16], refs[17]
     stripe, step = stripe_ref[0], pl.program_id(0)
     _, cols, above, below = halos[:4]
     _, low_cols, low_above, low_below = low_halos[:4]
@@ -605,24 +611,33 @@
 def ocean_kernel(cap, recv, state, into, out_weight, sea_out, back_out):
     tiles, _, side = recv.shape
 
-    def one_source(t, carry):
+    hidden = into.shape[0] // cap
+    unit = 2 if tiles % 2 == 0 else 1
+
+    def one_source(t):
         flux = recv[t].astype(F32)
         pad = (-flux.shape[0]) % 16
         flux = jnp.concatenate([flux, jnp.zeros((pad, side), F32)], axis=0).astype(BF)
         held = state[t]
         high = held.astype(BF)
         low = (held - high.astype(F32)).astype(BF)
-        hidden = smooth(mm(into[...], jnp.concatenate([flux, flux, high, high, low], axis=0)))
-        width = out_weight[...]
-        wide = jnp.concatenate([width] * (side // LANES), axis=1)
-        drift = (hidden * wide).reshape(cap, -1, side).sum(axis=1)
-        drift = jnp.concatenate([drift, jnp.zeros((8 - cap, side), F32)], axis=0)
-        sea = held[:8] + drift
-        sea_out[t] = sea
-        back_out[t] = sea.astype(BF)
+        stacked = jnp.concatenate([flux, flux, high, high, low], axis=0)
+        width = jnp.concatenate([out_weight[...]] * (side // LANES), axis=1)
+        drift = []
+        for k in range(cap):
+            grown = smooth(mm(into[k * hidden : (k + 1) * hidden, :], stacked)) * width
+            drift.append(grown.sum(axis=0, keepdims=True))
+        drift.append(jnp.zeros((8 - cap, side), F32))
+        return held[:8] + jnp.concatenate(drift, axis=0)
+
+    def some_sources(n, carry):
+        made = [one_source(n * unit + u) for u in range(unit)]
+        for u, sea in enumerate(made):
+            sea_out[n * unit + u] = sea
+            back_out[n * unit + u] = sea.astype(BF)
         return carry
 
-    lax.fori_loop(0, tiles, one_source, 0)
+    lax.fori_loop(0, tiles // unit, some_sources, 0)
 
 
 def surface_kernel(back, key, land, pred, out):
@@ -838,7 +853,7 @@
     into = jnp.concatenate(
         [flux_part(high), flux_part(rest), state_part(high), state_part(rest), state_part(high)], axis=1
     )
-    out_weight = jnp.broadcast_to(ocean_out[None, :, None], (cap, hidden, LANES)).reshape(-1, LANES)
+    out_weight = jnp.broadcast_to(ocean_out[:, None], (hidden, LANES))
     sea, back = call(
         functools.partial(ocean_kernel, cap),
         [jax.ShapeDtypeStruct((tiles, 8, side), F32), jax.ShapeDtypeStruct((tiles, 8, side), BF)],

time: 231 us -> 229 us (level)
  no operation moved by 1% of the time
where the time goes in v6:
time: 229 us; the launch traced here: 228 us
  Pallas kernels  94.1 us (41%)
  waiting for transfers between devices  64.6 us (28%)
  starting transfers between devices  45 us (20%)
  local copies, waits for them, and re-layouts  20.6 us (9%)
  other arithmetic  2.52 us (1%)
    pallas_call x7, Pallas kernels, call(): pl.pallas_call(kernel, out_shape=outs, **grid, in_specs=in_specs, out_spe...  94.1 us
    ppermute x4, waiting for transfers between devices, swap_rows(): up = lax.ppermute(bot, 'tile', ring)  28.4 us
    ppermute x4, starting transfers between devices, swap_rows(): return (up, lax.ppermute(top, 'tile', [(j, i) for i, j in ring]))  20.6 us
    all_to_all x5, waiting for transfers between devices, swap_chunks(): lax.all_to_all(chunks, 'tile', split_axis=0, concat_axis=0, tiled=True)  20.5 us
    all_to_all x5, starting transfers between devices, swap_chunks(): lax.all_to_all(chunks, 'tile', split_axis=0, concat_axis=0, tiled=True)  18.3 us
    all_to_all x1, waiting for transfers between devices, on_one_group(): lax.all_to_all(outgoing, 'tile', split_axis=0, concat_axis=0, tiled=True)  10.3 us
    unnamed x53, local copies, waits for them, and re-layouts  7.82 us
    all_to_all x1, waiting for transfers between devices, on_one_group(): lax.all_to_all(back, 'tile', split_axis=0, concat_axis=0, tiled=True)  5.43 us
  transfers between devices with their start and end apart: 15, of which 10 were waited for; matrix products, arithmetic and copies ran while one was open for 7% of the time, Pallas kernels for 5%

profile of v6, /device:TPU:0, one launch (start us, length us, event | category | flops | bytes accessed | tf_op | source)
XLA Modules:
  0.0 227.9 jit_solution(7670258873836082791)
XLA Ops:
  0.6 1.4 copy.197.tab
  2.0 7.4 %prep.1 = (bf16[12,8,32,256]{3,2,1,0:T(8,128)(2,1)}, bf16[12,32,256]{2,1,0:T(8,128)(2,1)}, bf16[12,32,256]{2,1,0:T(8,128)(2,1)}, bf16[192,32]{1,0:T(8,128)(2,1)}, bf16[32,48,128]{2,1,0:T(8,128)(2,1)}) custom-call(s32[1]{0:T(128)} %bitcast.stripe_ref, s32[48,2]{1,0:T(8,128)} %copy.197.tab, bf16[32,12,8,256]{3,2,1,0:T(8,128)(2,1)} %atmos.3, ...), custom_call_target="tpu_custom_call" | custom-call | flops 402653184 | bytes 4075908 | tf_op jit(solution)/shard_map/prep/pallas_call | solution.py:658
  9.3 6.7 %all-to-all-start = ((bf16[32,48,128]{2,1,0:T(8,128)(2,1)}), bf16[32,48,128]{2,1,0:T(8,128)(2,1)S(1)}, u32[]{:S(2)}, u32[]{:S(2)}) async-start(bf16[32,48,128]{2,1,0:T(8,128)(2,1)} %get-tuple-element.35), calls=%async_computation | async-start | bytes 786432 | tf_op jit(solution)/shard_map/all_to_all | solution.py:680
  16.1 0.3 collective-permute-start
  16.4 5.1 %collective-permute-start.1 = (bf16[12,32,256]{2,1,0:T(8,128)(2,1)}, bf16[12,32,256]{2,1,0:T(8,128)(2,1)S(1)}, u32[]{:S(2)}, u32[]{:S(2)}) collective-permute-start(bf16[12,32,256]{2,1,0:T(8,128)(2,1)} %get-tuple-element.32.old_top), channel_id=1, source_target_pairs={{1,0},{2,1},{3,2},{4,3},{5,4},{6,5},{7,6},{8,7},{9,8},{10,9},{11,1... | collective-permute-start | bytes 589832 | tf_op jit(solution)/shard_map/ppermute | solution.py:676
  21.5 0.9 copy.177
  22.7 0.7 copy.183.side_weight
  23.6 0.7 copy.182.weight
  24.3 6.8 %collective-permute-done.up = bf16[12,32,256]{2,1,0:T(8,128)(2,1)S(1)} collective-permute-done((bf16[12,32,256]{2,1,0:T(8,128)(2,1)}, bf16[12,32,256]{2,1,0:T(8,128)(2,1)S(1)}, u32[]{:S(2)}, u32[]{:S(2)}) %collective-permute-start) | collective-permute-done | bytes 196640 | tf_op jit(solution)/shard_map/ppermute | solution.py:675
  31.1 0.3 all-to-all-done.recv
  31.4 0.4 copy-done.21
  31.8 0.3 copy-done.7
  32.1 15.6 %conv_in.1 = (bf16[12,8,64,256]{3,2,1,0:T(8,128)(2,1)}, bf16[12,64,256]{2,1,0:T(8,128)(2,1)}, bf16[12,64,256]{2,1,0:T(8,128)(2,1)}, bf16[192,64]{1,0:T(8,128)(2,1)}, bf16[32,96,128]{2,1,0:T(8,128)(2,1)}) custom-call(s32[1]{0:T(128)} %bitcast.stripe_ref, s32[48,2]{1,0:T(8,128)} %copy.197.tab, bf16[12,8,32,256]{3,2,1,0:T(8,128)(2,1)} %get-tuple-element.31.x, ...), custom_call_target="tpu_custom_call" | custom-call | flops 905969664 | bytes 7569796 | tf_op jit(solution)/shard_map/conv_in/pallas_call | solution.py:658
  47.7 2.6 %all-to-all-start.1 = ((bf16[32,96,128]{2,1,0:T(8,128)(2,1)}), bf16[32,96,128]{2,1,0:T(8,128)(2,1)S(1)}, u32[]{:S(2)}, u32[]{:S(2)}) async-start(bf16[32,96,128]{2,1,0:T(8,128)(2,1)} %get-tuple-element.40), calls=%async_computation.1 | async-start | bytes 1572864 | tf_op jit(solution)/shard_map/all_to_all | solution.py:680
  50.4 0.2 collective-permute-start.2
  50.5 5.2 %collective-permute-start.3 = (bf16[12,64,256]{2,1,0:T(8,128)(2,1)}, bf16[12,64,256]{2,1,0:T(8,128)(2,1)S(1)}, u32[]{:S(2)}, u32[]{:S(2)}) collective-permute-start(bf16[12,64,256]{2,1,0:T(8,128)(2,1)} %get-tuple-element.37.old_top), channel_id=1, source_target_pairs={{1,0},{2,1},{3,2},{4,3},{5,4},{6,5},{7,6},{8,7},{9,8},{10,9},{11,1... | collective-permute-start | bytes 1179656 | tf_op jit(solution)/shard_map/ppermute | solution.py:676
  55.8 0.2 copy.184
  56.2 0.2 copy.185
  56.3 0.8 reshape.147.weight
  57.1 0.7 pad_maximum_fusion.1.side_weight
  57.8 16.3 %collective-permute-done.2.up = bf16[12,64,256]{2,1,0:T(8,128)(2,1)S(1)} collective-permute-done((bf16[12,64,256]{2,1,0:T(8,128)(2,1)}, bf16[12,64,256]{2,1,0:T(8,128)(2,1)S(1)}, u32[]{:S(2)}, u32[]{:S(2)}) %collective-permute-start.2) | collective-permute-done | bytes 393248 | tf_op jit(solution)/shard_map/ppermute | solution.py:675
  74.1 0.9 all-to-all-done.1.recv
  75.0 1.0 copy-done.3
  75.9 25.7 %encode.1 = (bf16[12,8,64,256]{3,2,1,0:T(8,128)(2,1)}, bf16[12,4,64,128]{3,2,1,0:T(8,128)(2,1)}, bf16[12,64,384]{2,1,0:T(8,128)(2,1)}, bf16[12,64,384]{2,1,0:T(8...) custom-call(s32[1]{0:T(128)} %bitcast.stripe_ref, ...), custom_call_target="tpu_custom_call" | custom-call | flops 1811939328 | bytes 12059012 | tf_op jit(solution)/shard_map/encode/pallas_call | solution.py:658
  101.7 2.7 %all-to-all-start.2 = ((bf16[32,48,128]{2,1,0:T(8,128)(2,1)}), bf16[32,48,128]{2,1,0:T(8,128)(2,1)S(1)}, u32[]{:S(2)}, u32[]{:S(2)}) async-start(bf16[32,48,128]{2,1,0:T(8,128)(2,1)} %get-tuple-element.47), calls=%async_computation.2 | async-start | bytes 786432 | tf_op jit(solution)/shard_map/all_to_all | solution.py:680
  104.5 0.2 copy.189
  104.7 0.2 convert_reduce_fusion
  104.8 0.2 collective-permute-start.4
  105.0 5.2 %collective-permute-start.5 = (bf16[12,64,384]{2,1,0:T(8,128)(2,1)}, bf16[12,64,384]{2,1,0:T(8,128)(2,1)}, u32[]{:S(2)}, u32[]{:S(2)}) collective-permute-start(bf16[12,64,384]{2,1,0:T(8,128)(2,1)} %get-tuple-element.42.old_top.top), channel_id=1, source_target_pairs={{1,0},{2,1},{3,2},{4,3},{5,4},{6,5},{7,6},{8,7},{9,8},{10,9},{11,1... | collective-permute-start | bytes 1769480 | tf_op jit(solution)/shard_map/ppermute | solution.py:676
  110.2 13.7 %all-to-all-done.2.recv = bf16[32,48,128]{2,1,0:T(8,128)(2,1)S(1)} async-done(((bf16[32,48,128]{2,1,0:T(8,128)(2,1)}), bf16[32,48,128]{2,1,0:T(8,128)(2,1)S(1)}, u32[]{:S(2)}, u32[]{:S(2)}) %all-to-all-start.2) | async-done | bytes 393248 | tf_op jit(solution)/shard_map/all_to_all | solution.py:680
  124.0 2.6 %all-to-all-start.3 = ((bf16[32,96,128]{2,1,0:T(8,128)(2,1)}), bf16[32,96,128]{2,1,0:T(8,128)(2,1)S(1)}, u32[]{:S(2)}, u32[]{:S(2)}) async-start(bf16[32,96,128]{2,1,0:T(8,128)(2,1)} %get-tuple-element.49), calls=%async_computation.3 | async-start | bytes 1572864 | tf_op jit(solution)/shard_map/all_to_all | solution.py:680
  126.8 0.2 copy.190
  127.0 0.8 reshape.149.weight
  127.8 0.2 reshape.150
  128.0 0.7 pad_maximum_fusion.2.side_weight
  128.8 0.8 copy-done.16
  129.6 12.3 %coarse.1 = (bf16[12,4,64,128]{3,2,1,0:T(8,128)(2,1)}, bf16[12,64,128]{2,1,0:T(8,128)(2,1)}, bf16[12,64,128]{2,1,0:T(8,128)(2,1)}, bf16[192,64]{1,0:T(8,128)(2,1)}, bf16[32,48,128]{2,1,0:T(8,128)(2,1)}) custom-call(s32[1]{0:T(128)} %bitcast.stripe_ref, s32[48,2]{1,0:T(8,128)} %copy.197.tab, bf16[12,4,64,128]{3,2,1,0:T(8,128)(2,1)} %get-tuple-element.45.x, ...), custom_call_target="tpu_custom_call" | custom-call | flops 10000000000 | bytes 5284228 | tf_op jit(solution)/shard_map/coarse/pallas_call | solution.py:658
  141.8 5.3 %all-to-all-done.3.recv = bf16[32,96,128]{2,1,0:T(8,128)(2,1)S(1)} async-done(((bf16[32,96,128]{2,1,0:T(8,128)(2,1)}), bf16[32,96,128]{2,1,0:T(8,128)(2,1)S(1)}, u32[]{:S(2)}, u32[]{:S(2)}) %all-to-all-start.3) | async-done | bytes 786464 | tf_op jit(solution)/shard_map/all_to_all | solution.py:680
  147.2 3.5 %all-to-all-start.4 = ((bf16[32,48,128]{2,1,0:T(8,128)(2,1)}), bf16[32,48,128]{2,1,0:T(8,128)(2,1)S(1)}, u32[]{:S(2)}, u32[]{:S(2)}) async-start(bf16[32,48,128]{2,1,0:T(8,128)(2,1)} %get-tuple-element.55), calls=%async_computation.4 | async-start | bytes 786432 | tf_op jit(solution)/shard_map/all_to_all | solution.py:680
  150.9 0.3 collective-permute-start.6
  151.2 5.1 %collective-permute-start.7 = (bf16[12,64,128]{2,1,0:T(8,128)(2,1)}, bf16[12,64,128]{2,1,0:T(8,128)(2,1)S(1)}, u32[]{:S(2)}, u32[]{:S(2)}) collective-permute-start(bf16[12,64,128]{2,1,0:T(8,128)(2,1)} %get-tuple-element.52.low_top), channel_id=1, source_target_pairs={{1,0},{2,1},{3,2},{4,3},{5,4},{6,5},{7,6},{8,7},{9,8},{10,9},{11,1... | collective-permute-start | bytes 589832 | tf_op jit(solution)/shard_map/ppermute | solution.py:676
  156.4 0.4 copy.211
  157.3 1.0 reshape.151.weight
  158.3 0.7 add.47.col_key
  158.9 0.8 mul.112.head
  159.7 0.7 pad_maximum_fusion.3.side_weight
  160.4 5.3 %collective-permute-done.6.yup = bf16[12,64,128]{2,1,0:T(8,128)(2,1)S(1)} collective-permute-done((bf16[12,64,128]{2,1,0:T(8,128)(2,1)}, bf16[12,64,128]{2,1,0:T(8,128)(2,1)S(1)}, u32[]{:S(2)}, u32[]{:S(2)}) %collective-permute-start.6) | collective-permute-done | bytes 196640 | tf_op jit(solution)/shard_map/ppermute | solution.py:675
  165.7 0.3 all-to-all-done.4.yrecv
  166.0 0.4 copy-done.19
  166.5 0.3 copy-done.5
  166.8 22.4 %decode.1 = (bf16[8,12,8,256]{3,2,1,0:T(8,128)(2,1)}, bf16[32,24,256]{2,1,0:T(8,128)(2,1)}) custom-call(s32[1]{0:T(128)} %bitcast.stripe_ref, s32[48,2]{1,0:T(8,128)} %copy.197.tab, bf16[12,8,64,256]{3,2,1,0:T(8,128)(2,1)} %get-tuple-element.41.x, bf16[12,64,384]{2,1,0:T(8,128)(2,1)} %get-tuple-element.42.old_top.top, ...), custom_call_target="tpu_custom_call" | custom-call | flops 3623878656 | bytes 11178884 | tf_op jit(solution)/shard_map/decode/pallas_call | solution.py:658
  189.2 2.6 %all-to-all-start.5 = ((bf16[32,24,256]{2,1,0:T(8,128)(2,1)}), bf16[32,24,256]{2,1,0:T(8,128)(2,1)S(1)}, u32[]{:S(2)}, u32[]{:S(2)}) async-start(bf16[32,24,256]{2,1,0:T(8,128)(2,1)} %get-tuple-element.56), calls=%async_computation.5 | async-start | bytes 786432 | tf_op jit(solution)/shard_map/all_to_all | solution.py:834
  193.0 0.8 concatenate.8.into
  193.9 0.8 pad_bitcast_fusion.state
  194.7 10.3 %all-to-all-done.5.recv = bf16[32,24,256]{2,1,0:T(8,128)(2,1)S(1)} async-done(((bf16[32,24,256]{2,1,0:T(8,128)(2,1)}), bf16[32,24,256]{2,1,0:T(8,128)(2,1)S(1)}, u32[]{:S(2)}, u32[]{:S(2)}) %all-to-all-start.5) | async-done | bytes 393248 | tf_op jit(solution)/shard_map/all_to_all | solution.py:834
  205.0 0.7 broadcast_in_dim.2.out_weight
  205.7 8.9 %ocean.1 = (f32[32,8,256]{2,1,0:T(8,128)}, bf16[32,8,256]{2,1,0:T(8,128)(2,1)}) custom-call(bf16[32,24,256]{2,1,0:T(8,128)(2,1)} %copy-done, f32[32,16,256]{2,1,0:T(8,128)} %pad_bitcast_fusion.state, bf16[384,112]{1,0:T(8,128)(2,1)} %concatenate.8.into, f32[64,128]{1,0:T(8,128)} %broadcast_in_dim.2.out_weight), custom_call_target="tpu_custom_call" | custom-call | flops 50331648 | bytes 1429504 | tf_op jit(solution)/shard_map/ocean/pallas_call | solution.py:658
  214.7 2.6 %all-to-all-start.6 = ((bf16[32,8,256]{2,1,0:T(8,128)(2,1)}), bf16[32,8,256]{2,1,0:T(8,128)(2,1)S(1)}, u32[]{:S(2)}, u32[]{:S(2)}) async-start(bf16[32,8,256]{2,1,0:T(8,128)(2,1)} %get-tuple-element.57), calls=%async_computation.6 | async-start | bytes 262144 | tf_op jit(solution)/shard_map/all_to_all | solution.py:865
  217.2 0.7 copy.204.key
  218.0 1.0 stack.48
  219.0 1.1 copy.206
  220.0 5.4 %all-to-all-done.6.back = bf16[32,8,256]{2,1,0:T(8,128)(2,1)S(1)} async-done(((bf16[32,8,256]{2,1,0:T(8,128)(2,1)}), bf16[32,8,256]{2,1,0:T(8,128)(2,1)S(1)}, u32[]{:S(2)}, u32[]{:S(2)}) %all-to-all-start.6) | async-done | bytes 131104 | tf_op jit(solution)/shard_map/all_to_all | solution.py:865
  225.5 0.7 copy-done.4
  226.1 1.8 surface.1
  (90 shorter events, 3.0 us)
Async XLA Ops:
  9.3 22.0 %all-to-all-start = ((bf16[32,48,128]{2,1,0:T(8,128)(2,1)}), bf16[32,48,128]{2,1,0:T(8,128)(2,1)S(1)}, u32[]{:S(2)}, u32[]{:S(2)}) async-start(bf16[32,48,128]{2,1,0:T(8,128)(2,1)} %get-tuple-element.35), calls=%async_computation | async-start | bytes 786432 | tf_op jit(solution)/shard_map/all_to_all | solution.py:680
  16.1 39.7 %copy-start.9 = (bf16[3,64,192]{2,1,0:T(8,128)(2,1)S(1)}, bf16[3,64,192]{2,1,0:T(8,128)(2,1)}, u32[]{:S(2)}) copy-start(bf16[3,64,192]{2,1,0:T(8,128)(2,1)} %param.24) | copy-start | bytes 221188
  16.1 15.0 %collective-permute-start = (bf16[12,32,256]{2,1,0:T(8,128)(2,1)}, bf16[12,32,256]{2,1,0:T(8,128)(2,1)S(1)}, u32[]{:S(2)}, u32[]{:S(2)}) collective-permute-start(bf16[12,32,256]{2,1,0:T(8,128)(2,1)} %get-tuple-element.33.old_bot), channel_id=1, source_target_pairs={{0,1},{1,2},{2,3},{3,4},{4,5},{5,6},{6,7},{7,8},{8,9},{9,10},{10,1... | collective-permute-start | bytes 589832 | tf_op jit(solution)/shard_map/ppermute | solution.py:675
  16.4 14.7 %collective-permute-start.1 = (bf16[12,32,256]{2,1,0:T(8,128)(2,1)}, bf16[12,32,256]{2,1,0:T(8,128)(2,1)S(1)}, u32[]{:S(2)}, u32[]{:S(2)}) collective-permute-start(bf16[12,32,256]{2,1,0:T(8,128)(2,1)} %get-tuple-element.32.old_top), channel_id=1, source_target_pairs={{1,0},{2,1},{3,2},{4,3},{5,4},{6,5},{7,6},{8,7},{9,8},{10,9},{11,1... | collective-permute-start | bytes 589832 | tf_op jit(solution)/shard_map/ppermute | solution.py:676
  31.1 0.7 copy-start.21
  31.1 0.7 copy-start.22
  31.4 0.7 copy-start.7
  47.7 27.2 %all-to-all-start.1 = ((bf16[32,96,128]{2,1,0:T(8,128)(2,1)}), bf16[32,96,128]{2,1,0:T(8,128)(2,1)S(1)}, u32[]{:S(2)}, u32[]{:S(2)}) async-start(bf16[32,96,128]{2,1,0:T(8,128)(2,1)} %get-tuple-element.40), calls=%async_computation.1 | async-start | bytes 1572864 | tf_op jit(solution)/shard_map/all_to_all | solution.py:680
  50.4 23.7 %collective-permute-start.2 = (bf16[12,64,256]{2,1,0:T(8,128)(2,1)}, bf16[12,64,256]{2,1,0:T(8,128)(2,1)S(1)}, u32[]{:S(2)}, u32[]{:S(2)}) collective-permute-start(bf16[12,64,256]{2,1,0:T(8,128)(2,1)} %get-tuple-element.38.old_bot), channel_id=1, source_target_pairs={{0,1},{1,2},{2,3},{3,4},{4,5},{5,6},{6,7},{7,8},{8,9},{9,10},{10,1... | collective-permute-start | bytes 1179656 | tf_op jit(solution)/shard_map/ppermute | solution.py:675
  50.5 23.5 %collective-permute-start.3 = (bf16[12,64,256]{2,1,0:T(8,128)(2,1)}, bf16[12,64,256]{2,1,0:T(8,128)(2,1)S(1)}, u32[]{:S(2)}, u32[]{:S(2)}) collective-permute-start(bf16[12,64,256]{2,1,0:T(8,128)(2,1)} %get-tuple-element.37.old_top), channel_id=1, source_target_pairs={{1,0},{2,1},{3,2},{4,3},{5,4},{6,5},{7,6},{8,7},{9,8},{10,9},{11,1... | collective-permute-start | bytes 1179656 | tf_op jit(solution)/shard_map/ppermute | solution.py:676
  74.0 0.9 copy-start.17
  74.1 0.9 copy-start.18
  75.0 1.0 copy-start.3
  75.9 28.5 %copy-start.10 = (bf16[3,64,192]{2,1,0:T(8,128)(2,1)S(1)}, bf16[3,64,192]{2,1,0:T(8,128)(2,1)}, u32[]{:S(2)}) copy-start(bf16[3,64,192]{2,1,0:T(8,128)(2,1)} %param.25) | copy-start | bytes 221188
  75.9 28.7 %copy-start.11 = (pred[96,96]{1,0:T(32,128)(4,1)S(1)}, pred[96,96]{1,0:T(32,128)(4,1)}, u32[]{:S(2)}) copy-start(pred[96,96]{1,0:T(32,128)(4,1)} %constant.29.clone) | copy-start | bytes 27652
  75.9 28.7 %copy-start.14 = (s32[96,1]{0,1:T(1,128)S(1)}, s32[96,1]{0,1:T(1,128)}, u32[]{:S(2)}) copy-start(s32[96,1]{0,1:T(1,128)} %param.20) | copy-start | bytes 1156
  101.7 26.1 %copy-start.8 = (bf16[3,64,384]{2,1,0:T(8,128)(2,1)S(1)}, bf16[3,64,384]{2,1,0:T(8,128)(2,1)}, u32[]{:S(2)}) copy-start(bf16[3,64,384]{2,1,0:T(8,128)(2,1)} %param.26) | copy-start | bytes 442372
  101.7 27.0 %copy-start.13 = (f32[64,6]{0,1:T(8,128)S(1)}, f32[64,6]{0,1:T(8,128)}, u32[]{:S(2)}) copy-start(f32[64,6]{0,1:T(8,128)} %param.28) | copy-start | bytes 4612
  101.7 26.9 %copy-start.12 = (bf16[12,64]{1,0:T(8,128)(2,1)S(1)}, bf16[12,64]{1,0:T(8,128)(2,1)}, u32[]{:S(2)}) copy-start(bf16[12,64]{1,0:T(8,128)(2,1)} %param.27) | copy-start | bytes 4612
  101.7 22.3 %all-to-all-start.2 = ((bf16[32,48,128]{2,1,0:T(8,128)(2,1)}), bf16[32,48,128]{2,1,0:T(8,128)(2,1)S(1)}, u32[]{:S(2)}, u32[]{:S(2)}) async-start(bf16[32,48,128]{2,1,0:T(8,128)(2,1)} %get-tuple-element.47), calls=%async_computation.2 | async-start | bytes 786432 | tf_op jit(solution)/shard_map/all_to_all | solution.py:680
  104.8 23.9 %collective-permute-start.4 = (bf16[12,64,384]{2,1,0:T(8,128)(2,1)}, bf16[12,64,384]{2,1,0:T(8,128)(2,1)S(1)}, u32[]{:S(2)}, u32[]{:S(2)}) collective-permute-start(bf16[12,64,384]{2,1,0:T(8,128)(2,1)} %get-tuple-element.43.old_bot.bot), channel_id=1, source_target_pairs={{0,1},{1,2},{2,3},{3,4},{4,5},{5,6},{6,7},{7,8},{8,9},{9,10},{10,1... | collective-permute-start | bytes 1769480 | tf_op jit(solution)/shard_map/ppermute | solution.py:675
  105.0 23.7 %collective-permute-start.5 = (bf16[12,64,384]{2,1,0:T(8,128)(2,1)}, bf16[12,64,384]{2,1,0:T(8,128)(2,1)}, u32[]{:S(2)}, u32[]{:S(2)}) collective-permute-start(bf16[12,64,384]{2,1,0:T(8,128)(2,1)} %get-tuple-element.42.old_top.top), channel_id=1, source_target_pairs={{1,0},{2,1},{3,2},{4,3},{5,4},{6,5},{7,6},{8,7},{9,8},{10,9},{11,1... | collective-permute-start | bytes 1769480 | tf_op jit(solution)/shard_map/ppermute | solution.py:676
  124.0 4.8 %copy-start.6 = (bf16[32,48,128]{2,1,0:T(8,128)(2,1)}, bf16[32,48,128]{2,1,0:T(8,128)(2,1)S(1)}, u32[]{:S(2)}) copy-start(bf16[32,48,128]{2,1,0:T(8,128)(2,1)S(1)} %all-to-all-done.2.recv) | copy-start | bytes 1179652
  124.0 23.2 %all-to-all-start.3 = ((bf16[32,96,128]{2,1,0:T(8,128)(2,1)}), bf16[32,96,128]{2,1,0:T(8,128)(2,1)S(1)}, u32[]{:S(2)}, u32[]{:S(2)}) async-start(bf16[32,96,128]{2,1,0:T(8,128)(2,1)} %get-tuple-element.49), calls=%async_computation.3 | async-start | bytes 1572864 | tf_op jit(solution)/shard_map/all_to_all | solution.py:680
  128.7 0.8 copy-start.16
  129.6 27.3 %copy-start.1 = (f32[1,1,192,2,256]{4,3,2,1,0:T(2,128)S(1)}, f32[1,1,192,2,256]{4,3,2,1,0:T(2,128)}, u32[]{:S(2)}) copy-start(f32[1,1,192,2,256]{4,3,2,1,0:T(2,128)} %param.22) | copy-start | bytes 1179652
  147.2 18.8 %copy-start.2 = (bf16[32,96,128]{2,1,0:T(8,128)(2,1)}, bf16[32,96,128]{2,1,0:T(8,128)(2,1)S(1)}, u32[]{:S(2)}) copy-start(bf16[32,96,128]{2,1,0:T(8,128)(2,1)S(1)} %all-to-all-done.3.recv) | copy-start | bytes 2359300
  147.2 18.8 %all-to-all-start.4 = ((bf16[32,48,128]{2,1,0:T(8,128)(2,1)}), bf16[32,48,128]{2,1,0:T(8,128)(2,1)S(1)}, u32[]{:S(2)}, u32[]{:S(2)}) async-start(bf16[32,48,128]{2,1,0:T(8,128)(2,1)} %get-tuple-element.55), calls=%async_computation.4 | async-start | bytes 786432 | tf_op jit(solution)/shard_map/all_to_all | solution.py:680
  150.9 14.8 %collective-permute-start.6 = (bf16[12,64,128]{2,1,0:T(8,128)(2,1)}, bf16[12,64,128]{2,1,0:T(8,128)(2,1)S(1)}, u32[]{:S(2)}, u32[]{:S(2)}) collective-permute-start(bf16[12,64,128]{2,1,0:T(8,128)(2,1)} %get-tuple-element.53.low_bot), channel_id=1, source_target_pairs={{0,1},{1,2},{2,3},{3,4},{4,5},{5,6},{6,7},{7,8},{8,9},{9,10},{10,1... | collective-permute-start | bytes 589832 | tf_op jit(solution)/shard_map/ppermute | solution.py:675
  151.2 14.5 %collective-permute-start.7 = (bf16[12,64,128]{2,1,0:T(8,128)(2,1)}, bf16[12,64,128]{2,1,0:T(8,128)(2,1)S(1)}, u32[]{:S(2)}, u32[]{:S(2)}) collective-permute-start(bf16[12,64,128]{2,1,0:T(8,128)(2,1)} %get-tuple-element.52.low_top), channel_id=1, source_target_pairs={{1,0},{2,1},{3,2},{4,3},{5,4},{6,5},{7,6},{8,7},{9,8},{10,9},{11,1... | collective-permute-start | bytes 589832 | tf_op jit(solution)/shard_map/ppermute | solution.py:676
  165.7 0.7 copy-start.19
  165.7 0.7 copy-start.20
  166.0 0.7 copy-start.5
  189.2 15.8 %copy-start.15 = (f32[64]{0:T(128)S(1)}, f32[64]{0:T(128)}, u32[]{:S(2)}) copy-start(f32[64]{0:T(128)} %param.29) | copy-start | bytes 772
  189.2 15.8 %all-to-all-start.5 = ((bf16[32,24,256]{2,1,0:T(8,128)(2,1)}), bf16[32,24,256]{2,1,0:T(8,128)(2,1)S(1)}, u32[]{:S(2)}, u32[]{:S(2)}) async-start(bf16[32,24,256]{2,1,0:T(8,128)(2,1)} %get-tuple-element.56), calls=%async_computation.5 | async-start | bytes 786432 | tf_op jit(solution)/shard_map/all_to_all | solution.py:834
  205.0 0.7 copy-start
  214.7 10.8 %all-to-all-start.6 = ((bf16[32,8,256]{2,1,0:T(8,128)(2,1)}), bf16[32,8,256]{2,1,0:T(8,128)(2,1)S(1)}, u32[]{:S(2)}, u32[]{:S(2)}) async-start(bf16[32,8,256]{2,1,0:T(8,128)(2,1)} %get-tuple-element.57), calls=%async_computation.6 | async-start | bytes 262144 | tf_op jit(solution)/shard_map/all_to_all | solution.py:865
  225.5 0.7 copy-start.4

commit v7 on v6

--- a/solution.py
+++ b/solution.py
@@ -239,7 +239,7 @@
             pltpu.VMEM((2, self.faces, 8, self.chans), F32),
             pltpu.VMEM((self.tiles, self.chunk, LANES), F32),
             pltpu.VMEM((self.side + 8, LANES), F32),
-            pltpu.VMEM((16, self.rows * self.side), BF),
+            pltpu.VMEM((16, self.rows * LANES), BF),
             pltpu.VMEM((2, self.side, self.side), BF),
         ]
 
@@ -269,10 +269,16 @@
 
 
 def column_picker(fld):
-    length = fld.rows * fld.side
+    length = fld.rows * LANES
     row, col = iota((16, length), 0), iota((16, length), 1)
-    want = (row & 7) * fld.side + (row >> 3) * (fld.side - 1)
-    return (col == want).astype(F32).astype(BF)
+    return (col == (row & 7) * LANES + (row >> 3) * (LANES - 1)).astype(F32).astype(BF)
+
+
+def near_ends(cells):
+    if cells.shape[1] > LANES:
+        lane = iota((cells.shape[0], LANES), 1)
+        cells = jnp.where(lane < LANES // 2, cells[:, :LANES], cells[:, cells.shape[1] - LANES :])
+    return cells.astype(BF)
 
 
 def keep_columns(picker, face_rows, f, cols):
@@ -353,8 +359,8 @@
     here = slice(off, off + side)
     above[...] = up[:, :, here]
     below[...] = dn[:, :, here]
-    over = mm_nt(end_picker(side), above[...].reshape(faces * chans, side))
-    under = mm_nt(end_picker(side), below[...].reshape(faces * chans, side))
+    over = mm_nt(end_picker(LANES), near_ends(above[...].reshape(faces * chans, side).astype(F32)))
+    under = mm_nt(end_picker(LANES), near_ends(below[...].reshape(faces * chans, side).astype(F32)))
     heads = [got[q * last, : fld.extra, :] for q in range(2)]
     before = got[jnp.minimum(last + 1 - stripe, last), fld.extra : fld.extra + 2 * groups, :]
     after = got[jnp.maximum(last - 1 - stripe, 0), fld.extra : fld.extra + 2 * groups, :]
@@ -474,7 +480,7 @@
         right = jnp.concatenate([right[:, : side - LANES], tail], axis=1)
     else:
         left, right = head, tail
-    return smooth(z[out_ch : 2 * out_ch] + left + right).astype(BF)
+    return smooth(z[out_ch : 2 * out_ch] + left + right)
 
 
 def row_stack(x, above, below, k, f, rows):
@@ -493,13 +499,13 @@
     def one_face(k, carry):
         f = step * batch + k
         block = atmos[:, k].astype(F32).reshape(fld.chans * fld.rows, fld.side).astype(BF)
-        moved = mm(perm[...], block).astype(BF)
+        moved = mm(perm[...], block)
         lines = [moved[r * fld.chans : (r + 1) * fld.chans] for r in range(fld.rows)]
         for r in range(fld.rows):
-            x_out[k, r] = lines[r]
-        top[f] = lines[0]
-        bot[f] = lines[-1]
-        keep_columns(sends[3][...], lines, f, sends[0])
+            x_out[k, r] = lines[r].astype(BF)
+        top[f] = lines[0].astype(BF)
+        bot[f] = lines[-1].astype(BF)
+        keep_columns(sends[3][...], [near_ends(cells) for cells in lines], f, sends[0])
         return carry
 
     lax.fori_loop(0, batch, one_face, 0)
@@ -535,9 +541,11 @@
         f = step * batch + k
         lines = row_stack(x, above, below, k, f, fld.rows)
         ends = face_terms([ends_ref[0], ends_ref[1]], f)
-        made, pooled = [], []
+        made, pooled, near = [], [], []
         for r in range(fld.rows):
             cells = conv_row(weight[...], jnp.concatenate(lines(r), axis=0), ends, r, out_fld.chans)
+            near.append(near_ends(cells))
+            cells = cells.astype(BF)
             x_out[k, r] = cells
             made.append(cells)
             if low is not None and r % 2 == 1:
@@ -546,7 +554,7 @@
                 pooled.append(mean)
         top[f, :, :side] = made[0]
         bot[f, :, :side] = made[-1]
-        keep_columns(sends[3][...], made, f, sends[0])
+        keep_columns(sends[3][...], near, f, sends[0])
         if low is not None:
             top[f, :, side:] = pooled[0]
             bot[f, :, side:] = pooled[-1]
@@ -592,7 +600,7 @@
         for r in range(fld.rows):
             picked = [wide[(r + a + 1) // 2] for a in range(3)]
             made.append(
-                conv_row(weight[...], jnp.concatenate(lines(r) + picked, axis=0), ends, r, out_ch)
+                conv_row(weight[...], jnp.concatenate(lines(r) + picked, axis=0), ends, r, out_ch).astype(BF)
             )
         result = mm(head[...], jnp.concatenate(made, axis=0)).reshape(-1, fld.rows, fld.side)
         pred_out[:, k] = (atmos[:, k].astype(F32) + result[:vars_out]).astype(BF)

time: 229 us -> 229 us (level)
  no operation moved by 1% of the time
where the time goes in v7:
time: 229 us; the launch traced here: 228 us
  Pallas kernels  94.2 us (41%)
  waiting for transfers between devices  64.6 us (28%)
  starting transfers between devices  45 us (20%)
  local copies, waits for them, and re-layouts  20.6 us (9%)
  other arithmetic  2.52 us (1%)
    pallas_call x7, Pallas kernels, call(): pl.pallas_call(kernel, out_shape=outs, **grid, in_specs=in_specs, out_spe...  94.2 us
    ppermute x4, waiting for transfers between devices, swap_rows(): up = lax.ppermute(bot, 'tile', ring)  28.4 us
    ppermute x4, starting transfers between devices, swap_rows(): return (up, lax.ppermute(top, 'tile', [(j, i) for i, j in ring]))  20.6 us
    all_to_all x5, waiting for transfers between devices, swap_chunks(): lax.all_to_all(chunks, 'tile', split_axis=0, concat_axis=0, tiled=True)  20.5 us
    all_to_all x5, starting transfers between devices, swap_chunks(): lax.all_to_all(chunks, 'tile', split_axis=0, concat_axis=0, tiled=True)  18.3 us
    all_to_all x1, waiting for transfers between devices, on_one_group(): lax.all_to_all(outgoing, 'tile', split_axis=0, concat_axis=0, tiled=True)  10.3 us
    unnamed x53, local copies, waits for them, and re-layouts  7.82 us
    all_to_all x1, waiting for transfers between devices, on_one_group(): lax.all_to_all(back, 'tile', split_axis=0, concat_axis=0, tiled=True)  5.43 us
  transfers between devices with their start and end apart: 15, of which 10 were waited for; matrix products, arithmetic and copies ran while one was open for 7% of the time, Pallas kernels for 5%

profile of v7, /device:TPU:0, one launch (start us, length us, event | category | flops | bytes accessed | tf_op | source)
XLA Modules:
  0.0 228.0 jit_solution(14419626932020225604)
XLA Ops:
  0.6 1.4 copy.197.tab
  2.0 7.3 %prep.1 = (bf16[12,8,32,256]{3,2,1,0:T(8,128)(2,1)}, bf16[12,32,256]{2,1,0:T(8,128)(2,1)}, bf16[12,32,256]{2,1,0:T(8,128)(2,1)}, bf16[192,32]{1,0:T(8,128)(2,1)}, bf16[32,48,128]{2,1,0:T(8,128)(2,1)}) custom-call(s32[1]{0:T(128)} %bitcast.stripe_ref, s32[48,2]{1,0:T(8,128)} %copy.197.tab, bf16[32,12,8,256]{3,2,1,0:T(8,128)(2,1)} %atmos.3, ...), custom_call_target="tpu_custom_call" | custom-call | flops 402653184 | bytes 4075908 | tf_op jit(solution)/shard_map/prep/pallas_call | solution.py:666
  9.3 6.7 %all-to-all-start = ((bf16[32,48,128]{2,1,0:T(8,128)(2,1)}), bf16[32,48,128]{2,1,0:T(8,128)(2,1)S(1)}, u32[]{:S(2)}, u32[]{:S(2)}) async-start(bf16[32,48,128]{2,1,0:T(8,128)(2,1)} %get-tuple-element.35), calls=%async_computation | async-start | bytes 786432 | tf_op jit(solution)/shard_map/all_to_all | solution.py:688
  16.1 0.3 collective-permute-start
  16.4 5.1 %collective-permute-start.1 = (bf16[12,32,256]{2,1,0:T(8,128)(2,1)}, bf16[12,32,256]{2,1,0:T(8,128)(2,1)S(1)}, u32[]{:S(2)}, u32[]{:S(2)}) collective-permute-start(bf16[12,32,256]{2,1,0:T(8,128)(2,1)} %get-tuple-element.32.old_top), channel_id=1, source_target_pairs={{1,0},{2,1},{3,2},{4,3},{5,4},{6,5},{7,6},{8,7},{9,8},{10,9},{11,1... | collective-permute-start | bytes 589832 | tf_op jit(solution)/shard_map/ppermute | solution.py:684
  21.5 0.9 copy.177
  22.7 0.7 copy.183.side_weight
  23.6 0.7 copy.182.weight
  24.3 6.8 %collective-permute-done.up = bf16[12,32,256]{2,1,0:T(8,128)(2,1)S(1)} collective-permute-done((bf16[12,32,256]{2,1,0:T(8,128)(2,1)}, bf16[12,32,256]{2,1,0:T(8,128)(2,1)S(1)}, u32[]{:S(2)}, u32[]{:S(2)}) %collective-permute-start) | collective-permute-done | bytes 196640 | tf_op jit(solution)/shard_map/ppermute | solution.py:683
  31.1 0.3 all-to-all-done.recv
  31.4 0.4 copy-done.21
  31.8 0.3 copy-done.7
  32.1 15.6 %conv_in.1 = (bf16[12,8,64,256]{3,2,1,0:T(8,128)(2,1)}, bf16[12,64,256]{2,1,0:T(8,128)(2,1)}, bf16[12,64,256]{2,1,0:T(8,128)(2,1)}, bf16[192,64]{1,0:T(8,128)(2,1)}, bf16[32,96,128]{2,1,0:T(8,128)(2,1)}) custom-call(s32[1]{0:T(128)} %bitcast.stripe_ref, s32[48,2]{1,0:T(8,128)} %copy.197.tab, bf16[12,8,32,256]{3,2,1,0:T(8,128)(2,1)} %get-tuple-element.31.x, ...), custom_call_target="tpu_custom_call" | custom-call | flops 905969664 | bytes 7569796 | tf_op jit(solution)/shard_map/conv_in/pallas_call | solution.py:666
  47.7 2.6 %all-to-all-start.1 = ((bf16[32,96,128]{2,1,0:T(8,128)(2,1)}), bf16[32,96,128]{2,1,0:T(8,128)(2,1)S(1)}, u32[]{:S(2)}, u32[]{:S(2)}) async-start(bf16[32,96,128]{2,1,0:T(8,128)(2,1)} %get-tuple-element.40), calls=%async_computation.1 | async-start | bytes 1572864 | tf_op jit(solution)/shard_map/all_to_all | solution.py:688
  50.3 0.2 collective-permute-start.2
  50.5 5.2 %collective-permute-start.3 = (bf16[12,64,256]{2,1,0:T(8,128)(2,1)}, bf16[12,64,256]{2,1,0:T(8,128)(2,1)S(1)}, u32[]{:S(2)}, u32[]{:S(2)}) collective-permute-start(bf16[12,64,256]{2,1,0:T(8,128)(2,1)} %get-tuple-element.37.old_top), channel_id=1, source_target_pairs={{1,0},{2,1},{3,2},{4,3},{5,4},{6,5},{7,6},{8,7},{9,8},{10,9},{11,1... | collective-permute-start | bytes 1179656 | tf_op jit(solution)/shard_map/ppermute | solution.py:684
  55.7 0.2 copy.184
  56.1 0.2 copy.185
  56.3 0.8 reshape.147.weight
  57.1 0.7 pad_maximum_fusion.1.side_weight
  57.8 16.3 %collective-permute-done.2.up = bf16[12,64,256]{2,1,0:T(8,128)(2,1)S(1)} collective-permute-done((bf16[12,64,256]{2,1,0:T(8,128)(2,1)}, bf16[12,64,256]{2,1,0:T(8,128)(2,1)S(1)}, u32[]{:S(2)}, u32[]{:S(2)}) %collective-permute-start.2) | collective-permute-done | bytes 393248 | tf_op jit(solution)/shard_map/ppermute | solution.py:683
  74.0 0.9 all-to-all-done.1.recv
  74.9 1.0 copy-done.3
  75.9 25.9 %encode.1 = (bf16[12,8,64,256]{3,2,1,0:T(8,128)(2,1)}, bf16[12,4,64,128]{3,2,1,0:T(8,128)(2,1)}, bf16[12,64,384]{2,1,0:T(8,128)(2,1)}, bf16[12,64,384]{2,1,0:T(8...) custom-call(s32[1]{0:T(128)} %bitcast.stripe_ref, ...), custom_call_target="tpu_custom_call" | custom-call | flops 1811939328 | bytes 12059012 | tf_op jit(solution)/shard_map/encode/pallas_call | solution.py:666
  101.9 2.7 %all-to-all-start.2 = ((bf16[32,48,128]{2,1,0:T(8,128)(2,1)}), bf16[32,48,128]{2,1,0:T(8,128)(2,1)S(1)}, u32[]{:S(2)}, u32[]{:S(2)}) async-start(bf16[32,48,128]{2,1,0:T(8,128)(2,1)} %get-tuple-element.47), calls=%async_computation.2 | async-start | bytes 786432 | tf_op jit(solution)/shard_map/all_to_all | solution.py:688
  104.6 0.2 copy.189
  104.8 0.2 convert_reduce_fusion
  105.0 0.2 collective-permute-start.4
  105.2 5.2 %collective-permute-start.5 = (bf16[12,64,384]{2,1,0:T(8,128)(2,1)}, bf16[12,64,384]{2,1,0:T(8,128)(2,1)}, u32[]{:S(2)}, u32[]{:S(2)}) collective-permute-start(bf16[12,64,384]{2,1,0:T(8,128)(2,1)} %get-tuple-element.42.old_top.top), channel_id=1, source_target_pairs={{1,0},{2,1},{3,2},{4,3},{5,4},{6,5},{7,6},{8,7},{9,8},{10,9},{11,1... | collective-permute-start | bytes 1769480 | tf_op jit(solution)/shard_map/ppermute | solution.py:684
  110.4 13.7 %all-to-all-done.2.recv = bf16[32,48,128]{2,1,0:T(8,128)(2,1)S(1)} async-done(((bf16[32,48,128]{2,1,0:T(8,128)(2,1)}), bf16[32,48,128]{2,1,0:T(8,128)(2,1)S(1)}, u32[]{:S(2)}, u32[]{:S(2)}) %all-to-all-start.2) | async-done | bytes 393248 | tf_op jit(solution)/shard_map/all_to_all | solution.py:688
  124.1 2.6 %all-to-all-start.3 = ((bf16[32,96,128]{2,1,0:T(8,128)(2,1)}), bf16[32,96,128]{2,1,0:T(8,128)(2,1)S(1)}, u32[]{:S(2)}, u32[]{:S(2)}) async-start(bf16[32,96,128]{2,1,0:T(8,128)(2,1)} %get-tuple-element.49), calls=%async_computation.3 | async-start | bytes 1572864 | tf_op jit(solution)/shard_map/all_to_all | solution.py:688
  127.0 0.2 copy.190
  127.2 0.8 reshape.149.weight
  128.0 0.2 reshape.150
  128.1 0.7 pad_maximum_fusion.2.side_weight
  128.9 0.8 copy-done.16
  129.7 12.3 %coarse.1 = (bf16[12,4,64,128]{3,2,1,0:T(8,128)(2,1)}, bf16[12,64,128]{2,1,0:T(8,128)(2,1)}, bf16[12,64,128]{2,1,0:T(8,128)(2,1)}, bf16[192,64]{1,0:T(8,128)(2,1)}, bf16[32,48,128]{2,1,0:T(8,128)(2,1)}) custom-call(s32[1]{0:T(128)} %bitcast.stripe_ref, s32[48,2]{1,0:T(8,128)} %copy.197.tab, bf16[12,4,64,128]{3,2,1,0:T(8,128)(2,1)} %get-tuple-element.45.x, ...), custom_call_target="tpu_custom_call" | custom-call | flops 10000000000 | bytes 5284228 | tf_op jit(solution)/shard_map/coarse/pallas_call | solution.py:666
  142.0 5.3 %all-to-all-done.3.recv = bf16[32,96,128]{2,1,0:T(8,128)(2,1)S(1)} async-done(((bf16[32,96,128]{2,1,0:T(8,128)(2,1)}), bf16[32,96,128]{2,1,0:T(8,128)(2,1)S(1)}, u32[]{:S(2)}, u32[]{:S(2)}) %all-to-all-start.3) | async-done | bytes 786464 | tf_op jit(solution)/shard_map/all_to_all | solution.py:688
  147.4 3.5 %all-to-all-start.4 = ((bf16[32,48,128]{2,1,0:T(8,128)(2,1)}), bf16[32,48,128]{2,1,0:T(8,128)(2,1)S(1)}, u32[]{:S(2)}, u32[]{:S(2)}) async-start(bf16[32,48,128]{2,1,0:T(8,128)(2,1)} %get-tuple-element.55), calls=%async_computation.4 | async-start | bytes 786432 | tf_op jit(solution)/shard_map/all_to_all | solution.py:688
  151.1 0.3 collective-permute-start.6
  151.4 5.1 %collective-permute-start.7 = (bf16[12,64,128]{2,1,0:T(8,128)(2,1)}, bf16[12,64,128]{2,1,0:T(8,128)(2,1)S(1)}, u32[]{:S(2)}, u32[]{:S(2)}) collective-permute-start(bf16[12,64,128]{2,1,0:T(8,128)(2,1)} %get-tuple-element.52.low_top), channel_id=1, source_target_pairs={{1,0},{2,1},{3,2},{4,3},{5,4},{6,5},{7,6},{8,7},{9,8},{10,9},{11,1... | collective-permute-start | bytes 589832 | tf_op jit(solution)/shard_map/ppermute | solution.py:684
  156.5 0.4 copy.211
  157.4 1.0 reshape.151.weight
  158.4 0.7 add.47.col_key
  159.1 0.8 mul.112.head
  159.9 0.7 pad_maximum_fusion.3.side_weight
  160.6 5.3 %collective-permute-done.6.yup = bf16[12,64,128]{2,1,0:T(8,128)(2,1)S(1)} collective-permute-done((bf16[12,64,128]{2,1,0:T(8,128)(2,1)}, bf16[12,64,128]{2,1,0:T(8,128)(2,1)S(1)}, u32[]{:S(2)}, u32[]{:S(2)}) %collective-permute-start.6) | collective-permute-done | bytes 196640 | tf_op jit(solution)/shard_map/ppermute | solution.py:683
  165.9 0.3 all-to-all-done.4.yrecv
  166.2 0.4 copy-done.19
  166.7 0.3 copy-done.5
  166.9 22.3 %decode.1 = (bf16[8,12,8,256]{3,2,1,0:T(8,128)(2,1)}, bf16[32,24,256]{2,1,0:T(8,128)(2,1)}) custom-call(s32[1]{0:T(128)} %bitcast.stripe_ref, s32[48,2]{1,0:T(8,128)} %copy.197.tab, bf16[12,8,64,256]{3,2,1,0:T(8,128)(2,1)} %get-tuple-element.41.x, bf16[12,64,384]{2,1,0:T(8,128)(2,1)} %get-tuple-element.42.old_top.top, ...), custom_call_target="tpu_custom_call" | custom-call | flops 3623878656 | bytes 11178884 | tf_op jit(solution)/shard_map/decode/pallas_call | solution.py:666
  189.3 2.6 %all-to-all-start.5 = ((bf16[32,24,256]{2,1,0:T(8,128)(2,1)}), bf16[32,24,256]{2,1,0:T(8,128)(2,1)S(1)}, u32[]{:S(2)}, u32[]{:S(2)}) async-start(bf16[32,24,256]{2,1,0:T(8,128)(2,1)} %get-tuple-element.56), calls=%async_computation.5 | async-start | bytes 786432 | tf_op jit(solution)/shard_map/all_to_all | solution.py:842
  193.1 0.8 concatenate.8.into
  194.0 0.8 pad_bitcast_fusion.state
  194.8 10.3 %all-to-all-done.5.recv = bf16[32,24,256]{2,1,0:T(8,128)(2,1)S(1)} async-done(((bf16[32,24,256]{2,1,0:T(8,128)(2,1)}), bf16[32,24,256]{2,1,0:T(8,128)(2,1)S(1)}, u32[]{:S(2)}, u32[]{:S(2)}) %all-to-all-start.5) | async-done | bytes 393248 | tf_op jit(solution)/shard_map/all_to_all | solution.py:842
  205.1 0.7 broadcast_in_dim.2.out_weight
  205.8 8.9 %ocean.1 = (f32[32,8,256]{2,1,0:T(8,128)}, bf16[32,8,256]{2,1,0:T(8,128)(2,1)}) custom-call(bf16[32,24,256]{2,1,0:T(8,128)(2,1)} %copy-done, f32[32,16,256]{2,1,0:T(8,128)} %pad_bitcast_fusion.state, bf16[384,112]{1,0:T(8,128)(2,1)} %concatenate.8.into, f32[64,128]{1,0:T(8,128)} %broadcast_in_dim.2.out_weight), custom_call_target="tpu_custom_call" | custom-call | flops 50331648 | bytes 1429504 | tf_op jit(solution)/shard_map/ocean/pallas_call | solution.py:666
  214.8 2.6 %all-to-all-start.6 = ((bf16[32,8,256]{2,1,0:T(8,128)(2,1)}), bf16[32,8,256]{2,1,0:T(8,128)(2,1)S(1)}, u32[]{:S(2)}, u32[]{:S(2)}) async-start(bf16[32,8,256]{2,1,0:T(8,128)(2,1)} %get-tuple-element.57), calls=%async_computation.6 | async-start | bytes 262144 | tf_op jit(solution)/shard_map/all_to_all | solution.py:873
  217.4 0.7 copy.204.key
  218.1 1.0 stack.48
  219.1 1.1 copy.206
  220.1 5.4 %all-to-all-done.6.back = bf16[32,8,256]{2,1,0:T(8,128)(2,1)S(1)} async-done(((bf16[32,8,256]{2,1,0:T(8,128)(2,1)}), bf16[32,8,256]{2,1,0:T(8,128)(2,1)S(1)}, u32[]{:S(2)}, u32[]{:S(2)}) %all-to-all-start.6) | async-done | bytes 131104 | tf_op jit(solution)/shard_map/all_to_all | solution.py:873
  225.6 0.7 copy-done.4
  226.2 1.8 surface.1
  (90 shorter events, 3.0 us)
Async XLA Ops:
  9.3 22.0 %all-to-all-start = ((bf16[32,48,128]{2,1,0:T(8,128)(2,1)}), bf16[32,48,128]{2,1,0:T(8,128)(2,1)S(1)}, u32[]{:S(2)}, u32[]{:S(2)}) async-start(bf16[32,48,128]{2,1,0:T(8,128)(2,1)} %get-tuple-element.35), calls=%async_computation | async-start | bytes 786432 | tf_op jit(solution)/shard_map/all_to_all | solution.py:688
  16.1 39.7 %copy-start.9 = (bf16[3,64,192]{2,1,0:T(8,128)(2,1)S(1)}, bf16[3,64,192]{2,1,0:T(8,128)(2,1)}, u32[]{:S(2)}) copy-start(bf16[3,64,192]{2,1,0:T(8,128)(2,1)} %param.24) | copy-start | bytes 221188
  16.1 15.0 %collective-permute-start = (bf16[12,32,256]{2,1,0:T(8,128)(2,1)}, bf16[12,32,256]{2,1,0:T(8,128)(2,1)S(1)}, u32[]{:S(2)}, u32[]{:S(2)}) collective-permute-start(bf16[12,32,256]{2,1,0:T(8,128)(2,1)} %get-tuple-element.33.old_bot), channel_id=1, source_target_pairs={{0,1},{1,2},{2,3},{3,4},{4,5},{5,6},{6,7},{7,8},{8,9},{9,10},{10,1... | collective-permute-start | bytes 589832 | tf_op jit(solution)/shard_map/ppermute | solution.py:683
  16.4 14.7 %collective-permute-start.1 = (bf16[12,32,256]{2,1,0:T(8,128)(2,1)}, bf16[12,32,256]{2,1,0:T(8,128)(2,1)S(1)}, u32[]{:S(2)}, u32[]{:S(2)}) collective-permute-start(bf16[12,32,256]{2,1,0:T(8,128)(2,1)} %get-tuple-element.32.old_top), channel_id=1, source_target_pairs={{1,0},{2,1},{3,2},{4,3},{5,4},{6,5},{7,6},{8,7},{9,8},{10,9},{11,1... | collective-permute-start | bytes 589832 | tf_op jit(solution)/shard_map/ppermute | solution.py:684
  31.1 0.7 copy-start.21
  31.1 0.7 copy-start.22
  31.4 0.7 copy-start.7
  47.7 27.2 %all-to-all-start.1 = ((bf16[32,96,128]{2,1,0:T(8,128)(2,1)}), bf16[32,96,128]{2,1,0:T(8,128)(2,1)S(1)}, u32[]{:S(2)}, u32[]{:S(2)}) async-start(bf16[32,96,128]{2,1,0:T(8,128)(2,1)} %get-tuple-element.40), calls=%async_computation.1 | async-start | bytes 1572864 | tf_op jit(solution)/shard_map/all_to_all | solution.py:688
  50.3 23.7 %collective-permute-start.2 = (bf16[12,64,256]{2,1,0:T(8,128)(2,1)}, bf16[12,64,256]{2,1,0:T(8,128)(2,1)S(1)}, u32[]{:S(2)}, u32[]{:S(2)}) collective-permute-start(bf16[12,64,256]{2,1,0:T(8,128)(2,1)} %get-tuple-element.38.old_bot), channel_id=1, source_target_pairs={{0,1},{1,2},{2,3},{3,4},{4,5},{5,6},{6,7},{7,8},{8,9},{9,10},{10,1... | collective-permute-start | bytes 1179656 | tf_op jit(solution)/shard_map/ppermute | solution.py:683
  50.5 23.5 %collective-permute-start.3 = (bf16[12,64,256]{2,1,0:T(8,128)(2,1)}, bf16[12,64,256]{2,1,0:T(8,128)(2,1)S(1)}, u32[]{:S(2)}, u32[]{:S(2)}) collective-permute-start(bf16[12,64,256]{2,1,0:T(8,128)(2,1)} %get-tuple-element.37.old_top), channel_id=1, source_target_pairs={{1,0},{2,1},{3,2},{4,3},{5,4},{6,5},{7,6},{8,7},{9,8},{10,9},{11,1... | collective-permute-start | bytes 1179656 | tf_op jit(solution)/shard_map/ppermute | solution.py:684
  74.0 0.9 copy-start.17
  74.0 0.9 copy-start.18
  74.9 1.0 copy-start.3
  75.9 28.7 %copy-start.10 = (bf16[3,64,192]{2,1,0:T(8,128)(2,1)S(1)}, bf16[3,64,192]{2,1,0:T(8,128)(2,1)}, u32[]{:S(2)}) copy-start(bf16[3,64,192]{2,1,0:T(8,128)(2,1)} %param.25) | copy-start | bytes 221188
  75.9 28.9 %copy-start.11 = (pred[96,96]{1,0:T(32,128)(4,1)S(1)}, pred[96,96]{1,0:T(32,128)(4,1)}, u32[]{:S(2)}) copy-start(pred[96,96]{1,0:T(32,128)(4,1)} %constant.29.clone) | copy-start | bytes 27652
  75.9 28.9 %copy-start.14 = (s32[96,1]{0,1:T(1,128)S(1)}, s32[96,1]{0,1:T(1,128)}, u32[]{:S(2)}) copy-start(s32[96,1]{0,1:T(1,128)} %param.20) | copy-start | bytes 1156
  101.8 26.1 %copy-start.8 = (bf16[3,64,384]{2,1,0:T(8,128)(2,1)S(1)}, bf16[3,64,384]{2,1,0:T(8,128)(2,1)}, u32[]{:S(2)}) copy-start(bf16[3,64,384]{2,1,0:T(8,128)(2,1)} %param.26) | copy-start | bytes 442372
  101.8 27.0 %copy-start.13 = (f32[64,6]{0,1:T(8,128)S(1)}, f32[64,6]{0,1:T(8,128)}, u32[]{:S(2)}) copy-start(f32[64,6]{0,1:T(8,128)} %param.28) | copy-start | bytes 4612
  101.9 26.9 %copy-start.12 = (bf16[12,64]{1,0:T(8,128)(2,1)S(1)}, bf16[12,64]{1,0:T(8,128)(2,1)}, u32[]{:S(2)}) copy-start(bf16[12,64]{1,0:T(8,128)(2,1)} %param.27) | copy-start | bytes 4612
  101.9 22.3 %all-to-all-start.2 = ((bf16[32,48,128]{2,1,0:T(8,128)(2,1)}), bf16[32,48,128]{2,1,0:T(8,128)(2,1)S(1)}, u32[]{:S(2)}, u32[]{:S(2)}) async-start(bf16[32,48,128]{2,1,0:T(8,128)(2,1)} %get-tuple-element.47), calls=%async_computation.2 | async-start | bytes 786432 | tf_op jit(solution)/shard_map/all_to_all | solution.py:688
  105.0 23.9 %collective-permute-start.4 = (bf16[12,64,384]{2,1,0:T(8,128)(2,1)}, bf16[12,64,384]{2,1,0:T(8,128)(2,1)S(1)}, u32[]{:S(2)}, u32[]{:S(2)}) collective-permute-start(bf16[12,64,384]{2,1,0:T(8,128)(2,1)} %get-tuple-element.43.old_bot.bot), channel_id=1, source_target_pairs={{0,1},{1,2},{2,3},{3,4},{4,5},{5,6},{6,7},{7,8},{8,9},{9,10},{10,1... | collective-permute-start | bytes 1769480 | tf_op jit(solution)/shard_map/ppermute | solution.py:683
  105.2 23.7 %collective-permute-start.5 = (bf16[12,64,384]{2,1,0:T(8,128)(2,1)}, bf16[12,64,384]{2,1,0:T(8,128)(2,1)}, u32[]{:S(2)}, u32[]{:S(2)}) collective-permute-start(bf16[12,64,384]{2,1,0:T(8,128)(2,1)} %get-tuple-element.42.old_top.top), channel_id=1, source_target_pairs={{1,0},{2,1},{3,2},{4,3},{5,4},{6,5},{7,6},{8,7},{9,8},{10,9},{11,1... | collective-permute-start | bytes 1769480 | tf_op jit(solution)/shard_map/ppermute | solution.py:684
  124.1 4.8 %copy-start.6 = (bf16[32,48,128]{2,1,0:T(8,128)(2,1)}, bf16[32,48,128]{2,1,0:T(8,128)(2,1)S(1)}, u32[]{:S(2)}) copy-start(bf16[32,48,128]{2,1,0:T(8,128)(2,1)S(1)} %all-to-all-done.2.recv) | copy-start | bytes 1179652
  124.1 23.2 %all-to-all-start.3 = ((bf16[32,96,128]{2,1,0:T(8,128)(2,1)}), bf16[32,96,128]{2,1,0:T(8,128)(2,1)S(1)}, u32[]{:S(2)}, u32[]{:S(2)}) async-start(bf16[32,96,128]{2,1,0:T(8,128)(2,1)} %get-tuple-element.49), calls=%async_computation.3 | async-start | bytes 1572864 | tf_op jit(solution)/shard_map/all_to_all | solution.py:688
  128.9 0.8 copy-start.16
  129.7 27.3 %copy-start.1 = (f32[1,1,192,2,256]{4,3,2,1,0:T(2,128)S(1)}, f32[1,1,192,2,256]{4,3,2,1,0:T(2,128)}, u32[]{:S(2)}) copy-start(f32[1,1,192,2,256]{4,3,2,1,0:T(2,128)} %param.22) | copy-start | bytes 1179652
  147.4 18.8 %copy-start.2 = (bf16[32,96,128]{2,1,0:T(8,128)(2,1)}, bf16[32,96,128]{2,1,0:T(8,128)(2,1)S(1)}, u32[]{:S(2)}) copy-start(bf16[32,96,128]{2,1,0:T(8,128)(2,1)S(1)} %all-to-all-done.3.recv) | copy-start | bytes 2359300
  147.4 18.8 %all-to-all-start.4 = ((bf16[32,48,128]{2,1,0:T(8,128)(2,1)}), bf16[32,48,128]{2,1,0:T(8,128)(2,1)S(1)}, u32[]{:S(2)}, u32[]{:S(2)}) async-start(bf16[32,48,128]{2,1,0:T(8,128)(2,1)} %get-tuple-element.55), calls=%async_computation.4 | async-start | bytes 786432 | tf_op jit(solution)/shard_map/all_to_all | solution.py:688
  151.1 14.8 %collective-permute-start.6 = (bf16[12,64,128]{2,1,0:T(8,128)(2,1)}, bf16[12,64,128]{2,1,0:T(8,128)(2,1)S(1)}, u32[]{:S(2)}, u32[]{:S(2)}) collective-permute-start(bf16[12,64,128]{2,1,0:T(8,128)(2,1)} %get-tuple-element.53.low_bot), channel_id=1, source_target_pairs={{0,1},{1,2},{2,3},{3,4},{4,5},{5,6},{6,7},{7,8},{8,9},{9,10},{10,1... | collective-permute-start | bytes 589832 | tf_op jit(solution)/shard_map/ppermute | solution.py:683
  151.4 14.5 %collective-permute-start.7 = (bf16[12,64,128]{2,1,0:T(8,128)(2,1)}, bf16[12,64,128]{2,1,0:T(8,128)(2,1)S(1)}, u32[]{:S(2)}, u32[]{:S(2)}) collective-permute-start(bf16[12,64,128]{2,1,0:T(8,128)(2,1)} %get-tuple-element.52.low_top), channel_id=1, source_target_pairs={{1,0},{2,1},{3,2},{4,3},{5,4},{6,5},{7,6},{8,7},{9,8},{10,9},{11,1... | collective-permute-start | bytes 589832 | tf_op jit(solution)/shard_map/ppermute | solution.py:684
  165.9 0.7 copy-start.19
  165.9 0.7 copy-start.20
  166.2 0.7 copy-start.5
  189.3 15.8 %copy-start.15 = (f32[64]{0:T(128)S(1)}, f32[64]{0:T(128)}, u32[]{:S(2)}) copy-start(f32[64]{0:T(128)} %param.29) | copy-start | bytes 772
  189.3 15.8 %all-to-all-start.5 = ((bf16[32,24,256]{2,1,0:T(8,128)(2,1)}), bf16[32,24,256]{2,1,0:T(8,128)(2,1)S(1)}, u32[]{:S(2)}, u32[]{:S(2)}) async-start(bf16[32,24,256]{2,1,0:T(8,128)(2,1)} %get-tuple-element.56), calls=%async_computation.5 | async-start | bytes 786432 | tf_op jit(solution)/shard_map/all_to_all | solution.py:842
  205.1 0.7 copy-start
  214.8 10.8 %all-to-all-start.6 = ((bf16[32,8,256]{2,1,0:T(8,128)(2,1)}), bf16[32,8,256]{2,1,0:T(8,128)(2,1)S(1)}, u32[]{:S(2)}, u32[]{:S(2)}) async-start(bf16[32,8,256]{2,1,0:T(8,128)(2,1)} %get-tuple-element.57), calls=%async_computation.6 | async-start | bytes 262144 | tf_op jit(solution)/shard_map/all_to_all | solution.py:873
  225.6 0.7 copy-start.4
